TPU v7x, 512 devices: a whole 4x4x16 slice. The times are simulated.
512 devices in a mesh: row: 16 (over z_hi, x), col: 32 (over z_lo, y, core).
Axes of the slice: x: 4, y: 4, z: 16 (z_hi: 4, z_lo: 4; z = z_hi * 4 + z_lo), core: 2. Of those that a mesh axis runs over, the one named last changes fastest.
Arguments:
- images: bfloat16 [11264, 1152], P(('row', 'col')), may hold values from -0.1875 to 0.1875
- texts: bfloat16 [11264, 1152], P(('col', 'row')), may hold values from -0.1875 to 0.1875
- logarithmic_scale: float32 [], replicated, may hold values from 2 to 3
- similarity_bias: float32 [], replicated, may hold values from -4 to -1
Outputs:
- grad_images: float32 [11264, 1152], P(('row', 'col'))
- grad_texts: float32 [11264, 1152], P(('col', 'row'))
All inputs are finite; a program needn't handle non-finite values.
Results may differ from a plain program's by a relative error of at most 0.03.
Values may be sent and summed in bfloat16 or wider, within the bound.
No kernel may reach another device: no remote copies, remote signals or barrier semaphores. Data moves between devices by JAX's collectives and lax.ppermute only.
A program may use at most 64 MiB of HBM per device.

v0:
```python
import jax
import jax.numpy as jnp
from jax import lax
from jax.sharding import PartitionSpec as P


def normalize(values):
    wide = values.astype(jnp.float32)
    length = jnp.sqrt(jnp.sum(wide * wide, axis=1, keepdims=True) + 1e-06)
    return (wide / length, length)


def norm_back(normed, length, upstream):
    along = jnp.sum(normed * upstream, axis=1, keepdims=True)
    return (upstream - normed * along) / length


def pairwise_factors(
    selected_entries, row_offset, column_ranges, column_offset, logit_multiplier, similarity_bias
):
    similarity_logits = lax.dot_general(
        selected_entries,
        column_ranges,
        (((1,), (1,)), ((), ())),
        preferred_element_type=jnp.float32,
    )
    row_ids = row_offset + lax.broadcasted_iota(jnp.int32, similarity_logits.shape, 0)
    col_ids = column_offset + lax.broadcasted_iota(jnp.int32, similarity_logits.shape, 1)
    pair_targets = jnp.where(row_ids == col_ids, jnp.float32(1.0), jnp.float32(-1.0))
    signed_logit = pair_targets * (logit_multiplier * similarity_logits + similarity_bias)
    return (-pair_targets * jax.nn.sigmoid(-signed_logit)).astype(jnp.bfloat16)


def on_device(images, texts, logarithmic_scale, similarity_bias):
    img_unit, img_len = normalize(images)
    txt_unit, txt_len = normalize(texts)
    picture_block = lax.all_gather(img_unit.astype(jnp.bfloat16), "col", axis=0, tiled=True)
    caption_block = lax.all_gather(txt_unit.astype(jnp.bfloat16), "row", axis=0, tiled=True)
    logit_multiplier = jnp.exp(logarithmic_scale)
    row_offset = lax.axis_index("row") * picture_block.shape[0]
    column_offset = lax.axis_index("col") * caption_block.shape[0]
    sigmoid_factors = pairwise_factors(
        picture_block, row_offset, caption_block, column_offset, logit_multiplier, similarity_bias
    )
    caption_contribution = logit_multiplier * lax.dot_general(
        sigmoid_factors, picture_block, (((0,), (0,)), ((), ())), preferred_element_type=jnp.float32
    )
    picture_contribution = logit_multiplier * jnp.dot(
        sigmoid_factors, caption_block, preferred_element_type=jnp.float32
    )
    grad_img_unit = lax.psum_scatter(
        picture_contribution.astype(jnp.bfloat16), "col", scatter_dimension=0, tiled=True
    ).astype(jnp.float32)
    grad_txt_unit = lax.psum_scatter(
        caption_contribution.astype(jnp.bfloat16), "row", scatter_dimension=0, tiled=True
    ).astype(jnp.float32)
    return (
        norm_back(img_unit, img_len, grad_img_unit),
        norm_back(txt_unit, txt_len, grad_txt_unit),
    )


def solution(mesh):
    return jax.shard_map(
        on_device,
        mesh=mesh,
        in_specs=(P(("row", "col"), None), P(("col", "row"), None), P(), P()),
        out_specs=(P(("row", "col"), None), P(("col", "row"), None)),
        check_vma=False,
    )
```

profile of v0, /device:TPU:1, one launch (start us, length us, event | category | flops | bytes accessed | tf_op | source)
XLA Modules:
  0.0 326.8 jit_solution(7426167745584707555)
XLA Ops:
  7.2 0.0 all-gather.4.cloned.1.call-start
  7.2 0.9 fusion.10
  8.2 1.5 convert_bitcast_fusion.1
  9.7 0.0 all-gather.4.cloned.1.call-update
  11.1 1.3 dynamic-slice.10
  12.3 1.3 dynamic-slice.6
  14.8 0.9 fusion.11
  15.8 0.9 convert_bitcast_fusion
  16.7 68.2 %all-gather.1 = bf16[16,22,1152]{2,1,0:T(8,128)(2,1)S(1)} all-gather(bf16[1,22,1152]{2,1,0:T(8,128)(2,1)S(1)} %convert_bitcast_fusion), channel_id=1, replica_groups=mesh['row'=16,'col'=32] {'row'}, dimensions={0}, use_global_device_ids=true | all-gather | bytes 861696 | tf_op jit(solution)/shard_map/all_gather | solution.py:38
  84.9 0.2 reshape.21
  85.2 1.8 all-gather.4.cloned.1.call-done
  87.0 2.4 reshape.19
  89.4 2.1 fusion.9
  91.5 1.9 fusion.3
  93.4 73.7 %fusion.1 = bf16[32,1152]{1,0:T(8,128)(2,1)S(1)} fusion(bf16[352,1152]{1,0:T(8,128)(2,1)S(1)} %fusion.3), kind=kCustom, calls=%all-reduce-scatter.1 | all-reduce-scatter fusion | flops 589825 | bytes 886784
  167.2 5.2 %collective-permute-start.13 = (bf16[32,1152]{1,0:T(8,128)(2,1)S(1)}, bf16[32,1152]{1,0:T(8,128)(2,1)S(1)}, u32[]{:S(2)}, u32[]{:S(2)}) collective-permute-start(bf16[32,1152]{1,0:T(8,128)(2,1)S(1)} %fusion.1), channel_id=1, source_target_pairs={{0,128},{32,160},{64,192},{96,224},{128,256},{160,288},{192,320},{... | collective-permute-start | bytes 221192
  172.4 1.3 collective-permute-start.12
  173.7 4.7 %collective-permute-start.11 = (bf16[32,1152]{1,0:T(8,128)(2,1)S(1)}, bf16[32,1152]{1,0:T(8,128)(2,1)S(1)}, u32[]{:S(2)}, u32[]{:S(2)}) collective-permute-start(bf16[32,1152]{1,0:T(8,128)(2,1)S(1)} %fusion.1), channel_id=1, source_target_pairs={{0,64},{32,96},{64,128},{96,160},{128,192},{160,224},{192,256},{22... | collective-permute-start | bytes 221192
  178.4 1.3 collective-permute-start.10
  179.7 2.1 fusion.2
  181.8 0.0 copy-start
  181.8 6.5 %collective-permute-start.14 = (bf16[22,1152]{1,0:T(8,128)(2,1)S(1)}, bf16[22,1152]{1,0:T(8,128)(2,1)S(1)}, u32[]{:S(2)}, u32[]{:S(2)}) collective-permute-start(bf16[22,1152]{1,0:T(8,128)(2,1)S(1)} %slice.1), channel_id=1, source_target_pairs={{0,160},{32,192},{64,224},{96,256},{128,288},{160,320},{192,352},{... | collective-permute-start | bytes 152072
  188.3 94.2 %fusion = bf16[32,1152]{1,0:T(8,128)(2,1)S(1)} fusion(bf16[704,1152]{1,0:T(8,128)(2,1)S(1)} %fusion.2), kind=kCustom, calls=%all-reduce-scatter | all-reduce-scatter fusion | flops 1179649 | bytes 1697792
  282.5 0.0 copy-start.1
  282.5 0.0 collective-permute-done.14
  282.5 1.3 collective-permute-start.8
  283.8 0.0 collective-permute-done.13
  283.8 1.3 collective-permute-start.7
  285.2 1.3 collective-permute-start.6
  286.5 5.4 %collective-permute-start.5 = (bf16[32,1152]{1,0:T(8,128)(2,1)S(1)}, bf16[32,1152]{1,0:T(8,128)(2,1)S(1)}, u32[]{:S(2)}, u32[]{:S(2)}) collective-permute-start(bf16[32,1152]{1,0:T(8,128)(2,1)S(1)} %fusion), channel_id=1, source_target_pairs={{0,6},{1,7},{2,8},{3,9},{4,10},{5,11},{6,12},{7,13},{8,14},{9,15},... | collective-permute-start | bytes 221192
  291.8 0.0 collective-permute-done.10
  291.9 1.3 collective-permute-start.9
  293.2 1.2 concatenate.1
  294.4 0.2 fusion.14
  294.6 0.0 collective-permute-done.9
  294.6 5.3 %collective-permute-start.4 = (bf16[32,1152]{1,0:T(8,128)(2,1)S(1)}, bf16[32,1152]{1,0:T(8,128)(2,1)S(1)}, u32[]{:S(2)}, u32[]{:S(2)}) collective-permute-start(bf16[32,1152]{1,0:T(8,128)(2,1)S(1)} %fusion), channel_id=1, source_target_pairs={{0,5},{1,6},{2,7},{3,8},{4,9},{5,10},{6,11},{7,12},{8,13},{9,14},{... | collective-permute-start | bytes 221192
  299.9 4.8 %collective-permute-start.3 = (bf16[32,1152]{1,0:T(8,128)(2,1)S(1)}, bf16[32,1152]{1,0:T(8,128)(2,1)S(1)}, u32[]{:S(2)}, u32[]{:S(2)}) collective-permute-start(bf16[32,1152]{1,0:T(8,128)(2,1)S(1)} %fusion), channel_id=1, source_target_pairs={{0,4},{1,5},{2,6},{3,7},{4,8},{5,9},{6,10},{7,11},{8,12},{9,13},{1... | collective-permute-start | bytes 221192
  304.7 0.0 collective-permute-done.7
  304.7 1.3 collective-permute-start.2
  306.0 0.0 collective-permute-done.6
  306.0 4.0 %collective-permute-start.1 = (bf16[32,1152]{1,0:T(8,128)(2,1)S(1)}, bf16[32,1152]{1,0:T(8,128)(2,1)S(1)}, u32[]{:S(2)}, u32[]{:S(2)}) collective-permute-start(bf16[32,1152]{1,0:T(8,128)(2,1)S(1)} %fusion), channel_id=1, source_target_pairs={{0,2},{1,3},{2,4},{3,5},{4,6},{5,7},{6,8},{7,9},{8,10},{9,11},{10,... | collective-permute-start | bytes 221192
  310.0 0.0 collective-permute-done.5
  310.0 5.2 %collective-permute-start = (bf16[32,1152]{1,0:T(8,128)(2,1)S(1)}, bf16[32,1152]{1,0:T(8,128)(2,1)S(1)}, u32[]{:S(2)}, u32[]{:S(2)}) collective-permute-start(bf16[32,1152]{1,0:T(8,128)(2,1)S(1)} %fusion), channel_id=1, source_target_pairs={{0,1},{1,2},{2,3},{3,4},{4,5},{5,6},{6,7},{7,8},{8,9},{9,10},{10,1... | collective-permute-start | bytes 221192
  315.3 0.7 fusion.15
  316.0 0.6 collective-permute-done
  316.6 2.3 concatenate
  319.0 0.2 fusion.12
  319.2 0.7 fusion.13
  (15 shorter events, 0.1 us)
Async XLA Ops:
  7.2 79.8 %all-gather.4.cloned.1.call-start = ((), (), s32[]{:S(2)}) async-start(), calls=%async_computation | async-start | bytes 1824768 | tf_op jit(solution)/shard_map/all_gather | solution.py:37
  167.2 116.7 %collective-permute-start.13 = (bf16[32,1152]{1,0:T(8,128)(2,1)S(1)}, bf16[32,1152]{1,0:T(8,128)(2,1)S(1)}, u32[]{:S(2)}, u32[]{:S(2)}) collective-permute-start(bf16[32,1152]{1,0:T(8,128)(2,1)S(1)} %fusion.1), channel_id=1, source_target_pairs={{0,128},{32,160},{64,192},{96,224},{128,256},{160,288},{192,320},{... | collective-permute-start | bytes 221192
  172.4 112.7 %collective-permute-start.12 = (bf16[32,1152]{1,0:T(8,128)(2,1)S(1)}, bf16[32,1152]{1,0:T(8,128)(2,1)S(1)}, u32[]{:S(2)}, u32[]{:S(2)}) collective-permute-start(bf16[32,1152]{1,0:T(8,128)(2,1)S(1)} %fusion.1), channel_id=1, source_target_pairs={{0,96},{32,128},{64,160},{96,192},{128,224},{160,256},{192,288},{2... | collective-permute-start | bytes 221192
  173.7 112.7 %collective-permute-start.11 = (bf16[32,1152]{1,0:T(8,128)(2,1)S(1)}, bf16[32,1152]{1,0:T(8,128)(2,1)S(1)}, u32[]{:S(2)}, u32[]{:S(2)}) collective-permute-start(bf16[32,1152]{1,0:T(8,128)(2,1)S(1)} %fusion.1), channel_id=1, source_target_pairs={{0,64},{32,96},{64,128},{96,160},{128,192},{160,224},{192,256},{22... | collective-permute-start | bytes 221192
  178.4 113.4 %collective-permute-start.10 = (bf16[32,1152]{1,0:T(8,128)(2,1)S(1)}, bf16[32,1152]{1,0:T(8,128)(2,1)S(1)}, u32[]{:S(2)}, u32[]{:S(2)}) collective-permute-start(bf16[32,1152]{1,0:T(8,128)(2,1)S(1)} %fusion.1), channel_id=1, source_target_pairs={{0,32},{32,64},{64,96},{96,128},{128,160},{160,192},{192,224},{224... | collective-permute-start | bytes 221192
  181.8 112.5 %copy-start = (bf16[22,1152]{1,0:T(8,128)(2,1)S(1)}, bf16[22,1152]{1,0:T(8,128)(2,1)}, u32[]{:S(2)}) copy-start(bf16[22,1152]{1,0:T(8,128)(2,1)} %param.5) | copy-start | bytes 152068
  181.8 100.7 %collective-permute-start.14 = (bf16[22,1152]{1,0:T(8,128)(2,1)S(1)}, bf16[22,1152]{1,0:T(8,128)(2,1)S(1)}, u32[]{:S(2)}, u32[]{:S(2)}) collective-permute-start(bf16[22,1152]{1,0:T(8,128)(2,1)S(1)} %slice.1), channel_id=1, source_target_pairs={{0,160},{32,192},{64,224},{96,256},{128,288},{160,320},{192,352},{... | collective-permute-start | bytes 152072
  282.5 36.5 %copy-start.1 = (bf16[22,1152]{1,0:T(8,128)(2,1)S(1)}, bf16[22,1152]{1,0:T(8,128)(2,1)}, u32[]{:S(2)}) copy-start(bf16[22,1152]{1,0:T(8,128)(2,1)} %param.4) | copy-start | bytes 152068
  282.5 17.4 %collective-permute-start.8 = (bf16[32,1152]{1,0:T(8,128)(2,1)S(1)}, bf16[32,1152]{1,0:T(8,128)(2,1)S(1)}, u32[]{:S(2)}, u32[]{:S(2)}) collective-permute-start(bf16[32,1152]{1,0:T(8,128)(2,1)S(1)} %fusion), channel_id=1, source_target_pairs={{0,9},{1,10},{2,11},{3,12},{4,13},{5,14},{6,15},{7,16},{8,17},{9,1... | collective-permute-start | bytes 221192
  283.8 20.9 %collective-permute-start.7 = (bf16[32,1152]{1,0:T(8,128)(2,1)S(1)}, bf16[32,1152]{1,0:T(8,128)(2,1)S(1)}, u32[]{:S(2)}, u32[]{:S(2)}) collective-permute-start(bf16[32,1152]{1,0:T(8,128)(2,1)S(1)} %fusion), channel_id=1, source_target_pairs={{0,8},{1,9},{2,10},{3,11},{4,12},{5,13},{6,14},{7,15},{8,16},{9,17... | collective-permute-start | bytes 221192
  285.2 20.9 %collective-permute-start.6 = (bf16[32,1152]{1,0:T(8,128)(2,1)S(1)}, bf16[32,1152]{1,0:T(8,128)(2,1)S(1)}, u32[]{:S(2)}, u32[]{:S(2)}) collective-permute-start(bf16[32,1152]{1,0:T(8,128)(2,1)S(1)} %fusion), channel_id=1, source_target_pairs={{0,7},{1,8},{2,9},{3,10},{4,11},{5,12},{6,13},{7,14},{8,15},{9,16}... | collective-permute-start | bytes 221192
  286.5 23.6 %collective-permute-start.5 = (bf16[32,1152]{1,0:T(8,128)(2,1)S(1)}, bf16[32,1152]{1,0:T(8,128)(2,1)S(1)}, u32[]{:S(2)}, u32[]{:S(2)}) collective-permute-start(bf16[32,1152]{1,0:T(8,128)(2,1)S(1)} %fusion), channel_id=1, source_target_pairs={{0,6},{1,7},{2,8},{3,9},{4,10},{5,11},{6,12},{7,13},{8,14},{9,15},... | collective-permute-start | bytes 221192
  291.9 2.7 collective-permute-start.9
  294.6 21.4 %collective-permute-start.4 = (bf16[32,1152]{1,0:T(8,128)(2,1)S(1)}, bf16[32,1152]{1,0:T(8,128)(2,1)S(1)}, u32[]{:S(2)}, u32[]{:S(2)}) collective-permute-start(bf16[32,1152]{1,0:T(8,128)(2,1)S(1)} %fusion), channel_id=1, source_target_pairs={{0,5},{1,6},{2,7},{3,8},{4,9},{5,10},{6,11},{7,12},{8,13},{9,14},{... | collective-permute-start | bytes 221192
  299.9 16.1 %collective-permute-start.3 = (bf16[32,1152]{1,0:T(8,128)(2,1)S(1)}, bf16[32,1152]{1,0:T(8,128)(2,1)S(1)}, u32[]{:S(2)}, u32[]{:S(2)}) collective-permute-start(bf16[32,1152]{1,0:T(8,128)(2,1)S(1)} %fusion), channel_id=1, source_target_pairs={{0,4},{1,5},{2,6},{3,7},{4,8},{5,9},{6,10},{7,11},{8,12},{9,13},{1... | collective-permute-start | bytes 221192
  304.7 11.3 %collective-permute-start.2 = (bf16[32,1152]{1,0:T(8,128)(2,1)S(1)}, bf16[32,1152]{1,0:T(8,128)(2,1)S(1)}, u32[]{:S(2)}, u32[]{:S(2)}) collective-permute-start(bf16[32,1152]{1,0:T(8,128)(2,1)S(1)} %fusion), channel_id=1, source_target_pairs={{0,3},{1,4},{2,5},{3,6},{4,7},{5,8},{6,9},{7,10},{8,11},{9,12},{10... | collective-permute-start | bytes 221192
  306.0 10.0 %collective-permute-start.1 = (bf16[32,1152]{1,0:T(8,128)(2,1)S(1)}, bf16[32,1152]{1,0:T(8,128)(2,1)S(1)}, u32[]{:S(2)}, u32[]{:S(2)}) collective-permute-start(bf16[32,1152]{1,0:T(8,128)(2,1)S(1)} %fusion), channel_id=1, source_target_pairs={{0,2},{1,3},{2,4},{3,5},{4,6},{5,7},{6,8},{7,9},{8,10},{9,11},{10,... | collective-permute-start | bytes 221192
  310.0 6.6 %collective-permute-start = (bf16[32,1152]{1,0:T(8,128)(2,1)S(1)}, bf16[32,1152]{1,0:T(8,128)(2,1)S(1)}, u32[]{:S(2)}, u32[]{:S(2)}) collective-permute-start(bf16[32,1152]{1,0:T(8,128)(2,1)S(1)} %fusion), channel_id=1, source_target_pairs={{0,1},{1,2},{2,3},{3,4},{4,5},{5,6},{6,7},{7,8},{8,9},{9,10},{10,1... | collective-permute-start | bytes 221192
Sparse Core Ops, SparseCore 0:
  10.7 76.1 all-gather.3
where the time goes:
time: 328 us; the launch traced here: 327 us
  blocking collectives  236 us (72%)
  starting transfers between devices  50.2 us (15%)
  between operations  16.9 us (5%)
  local copies, waits for them, and re-layouts  8.74 us (3%)
  other arithmetic  6.21 us (2%)
  matrix products  6.13 us (2%)
    unnamed x2, blocking collectives  168 us
    all_gather x1, blocking collectives, on_device(): lax.all_gather(txt_unit.astype(jnp.bfloat16), 'row', axis=0, tiled=True)  68.2 us
    unnamed x15, starting transfers between devices  50.1 us
    unnamed x12, local copies, waits for them, and re-layouts  8.74 us
  transfers between devices with their start and end apart: 16, of which 2 were waited for; matrix products, arithmetic and copies ran while one was open for 32% of the time, Pallas kernels for 0%

commit v1 on v0

v1 whole, which is shorter than its diff:
```python
import functools

import jax
import jax.numpy as jnp
from jax import lax
from jax.experimental import pallas as pl
from jax.experimental.pallas import tpu as pltpu
from jax.sharding import Mesh
from jax.sharding import PartitionSpec as P

D = 1152
ROWS = 22
PAD = 24
AXES = ("zh", "x", "zl", "y", "core")
SIZES = (4, 4, 4, 4, 2)
IMG_STAGES = (("zl", "pair2"), ("y", "pair3"), ("core", "pair"))
TXT_STAGES = (("zh", "pair3"), ("x", "pair3"))
IMG_BACK = None
TXT_BACK = None
VMEM = 48 * 1024 * 1024


def swap(value, axis, mask):
    size = SIZES[AXES.index(axis)]
    return lax.ppermute(value, axis, [(i, i ^ mask) for i in range(size)])


def order(way):
    return {"pair": (0, 1), "pair2": (0, 1, 2, 3), "pair3": (0, 1, 3, 2), "direct": (0, 1, 3, 2), "a2a": None}[way]


def spread(held, axis, way):
    if way == "pair":
        return jnp.concatenate([held, swap(held, axis, 1)])
    if way in ("pair2", "pair3"):
        held = jnp.concatenate([held, swap(held, axis, 1)])
        return jnp.concatenate([held, swap(held, axis, 2 if way == "pair2" else 3)])
    if way == "direct":
        return jnp.concatenate([held] + [swap(held, axis, m) for m in (1, 3, 2)])
    size = SIZES[AXES.index(axis)]
    out = lax.all_to_all(jnp.broadcast_to(held[None], (size,) + held.shape), axis, 0, 0, tiled=True)
    return out.reshape((-1, held.shape[1]))


def add(parts):
    return sum(p.astype(jnp.float32) for p in parts).astype(jnp.bfloat16)


def collect(held, axis, way):
    size = SIZES[AXES.index(axis)]
    if way in ("pair", "pair2", "pair3"):
        for mask in {"pair": (1,), "pair2": (2, 1), "pair3": (3, 1)}[way]:
            half = held.shape[0] // 2
            held = add([held[:half], swap(held[half:], axis, mask)])
        return held
    parts = held.reshape((size, -1, held.shape[1]))
    if way == "direct":
        return add([parts[0]] + [swap(parts[k], axis, m) for k, m in ((1, 1), (2, 3), (3, 2))])
    parts = lax.all_to_all(parts, axis, 0, 0, tiled=True)
    return add([parts[k] for k in range(size)])


def slots(stages, names):
    coords = {n: lax.axis_index(n) for n in names}
    found = [jnp.int32(0)]
    weight = {}
    total = 1
    for n in reversed(names):
        weight[n] = total
        total *= SIZES[AXES.index(n)]
    for axis, way in stages:
        seq = order(way)
        size = SIZES[AXES.index(axis)]
        here = [jnp.int32(k) if seq is None else coords[axis] ^ seq[k] for k in range(size)]
        found = [f + weight[axis] * h for h in here for f in found]
    return jnp.stack(found)


def unit_kernel(img_ref, txt_ref, img_out, txt_out):
    for src, dst in ((img_ref, img_out), (txt_ref, txt_out)):
        wide = src[...].astype(jnp.float32)
        length = jnp.sqrt(jnp.sum(wide * wide, axis=1, keepdims=True) + 1e-06)
        unit = wide / length
        dst[...] = jnp.concatenate([unit, jnp.zeros((PAD - ROWS, D), jnp.float32)]).astype(jnp.bfloat16)


def pair_kernel(scal_ref, img_ref, txt_ref, row_ref, col_ref, gimg_ref, gtxt_ref, w_ref):
    scale, bias = scal_ref[0], scal_ref[1]
    n = img_ref.shape[0]
    tile = 256
    for t in range(n // tile):
        rows = pl.ds(t * tile, tile)
        s = lax.dot_general(img_ref[rows, :], txt_ref[...], (((1,), (1,)), ((), ())), preferred_element_type=jnp.float32)
        z = scale * s + bias
        same = row_ref[rows, :] == col_ref[...]
        w = jnp.where(same, -1.0, 1.0) / (1.0 + jnp.exp(jnp.where(same, z, -z)))
        w_ref[rows, :] = w.astype(jnp.bfloat16)
    w_all = w_ref[...]
    for t in range(3):
        cols = pl.ds(t * 384, 384)
        g = lax.dot_general(w_all, img_ref[:, cols], (((0,), (0,)), ((), ())), preferred_element_type=jnp.float32)
        gtxt_ref[:, cols] = (scale * g).astype(jnp.bfloat16)
    for t in range(3):
        cols = pl.ds(t * 384, 384)
        g = jnp.dot(w_all, txt_ref[:, cols], preferred_element_type=jnp.float32)
        gimg_ref[:, cols] = (scale * g).astype(jnp.bfloat16)


def back_kernel(img_ref, txt_ref, gi_ref, gt_ref, img_out, txt_out):
    for src, g_ref, dst in ((img_ref, gi_ref, img_out), (txt_ref, gt_ref, txt_out)):
        wide = src[...].astype(jnp.float32)
        length = jnp.sqrt(jnp.sum(wide * wide, axis=1, keepdims=True) + 1e-06)
        unit = wide / length
        g = g_ref[...].astype(jnp.float32)[:ROWS]
        along = jnp.sum(unit * g, axis=1, keepdims=True)
        dst[...] = (g - unit * along) / length


def vm():
    return pl.BlockSpec(memory_space=pltpu.VMEM)


PARAMS = pltpu.CompilerParams(vmem_limit_bytes=VMEM)


def on_device(images, texts, logarithmic_scale, similarity_bias):
    block = jax.ShapeDtypeStruct((PAD, D), jnp.bfloat16)
    img, txt = pl.pallas_call(unit_kernel, out_shape=(block, block), in_specs=[vm()] * 2, out_specs=(vm(), vm()), compiler_params=PARAMS, name="unit")(images, texts)
    for axis, way in TXT_STAGES:
        txt = spread(txt, axis, way)
    for axis, way in IMG_STAGES:
        img = spread(img, axis, way)
    row = lax.axis_index("zh") * 4 + lax.axis_index("x")
    col = (lax.axis_index("zl") * 4 + lax.axis_index("y")) * 2 + lax.axis_index("core")
    img_ids = row * 32 + slots(IMG_STAGES, ("zl", "y", "core"))
    txt_ids = col * 16 + slots(TXT_STAGES, ("zh", "x"))
    within = jnp.arange(PAD, dtype=jnp.int32)
    row_ids = jnp.where(within < ROWS, img_ids[:, None] * ROWS + within, -1).reshape(-1, 1)
    col_ids = jnp.where(within < ROWS, txt_ids[:, None] * ROWS + within, -2).reshape(1, -1)
    scal = jnp.stack([jnp.exp(logarithmic_scale), similarity_bias])
    ni, nt = img.shape[0], txt.shape[0]
    gimg, gtxt = pl.pallas_call(
        pair_kernel,
        out_shape=(jax.ShapeDtypeStruct((ni, D), jnp.bfloat16), jax.ShapeDtypeStruct((nt, D), jnp.bfloat16)),
        in_specs=[pl.BlockSpec(memory_space=pltpu.SMEM)] + [vm()] * 4,
        out_specs=(vm(), vm()),
        scratch_shapes=[pltpu.VMEM((ni, nt), jnp.bfloat16)],
        compiler_params=PARAMS,
        name="pairs",
    )(scal, img, txt, row_ids, col_ids)
    for axis, way in reversed(TXT_BACK or TXT_STAGES):
        gtxt = collect(gtxt, axis, way)
    for axis, way in reversed(IMG_BACK or IMG_STAGES):
        gimg = collect(gimg, axis, way)
    wide = jax.ShapeDtypeStruct((ROWS, D), jnp.float32)
    return pl.pallas_call(back_kernel, out_shape=(wide, wide), in_specs=[vm()] * 4, out_specs=(vm(), vm()), compiler_params=PARAMS, name="back")(images, texts, gimg, gtxt)


def solution(mesh):
    fine = Mesh(mesh.devices.reshape(SIZES), AXES)
    return jax.shard_map(
        on_device,
        mesh=fine,
        in_specs=(P(AXES, None), P(("zl", "y", "core", "zh", "x"), None), P(), P()),
        out_specs=(P(AXES, None), P(("zl", "y", "core", "zh", "x"), None)),
        check_vma=False,
    )
```

time: 328 us -> 133 us (0.41)
  the two profiles are of different devices: /device:TPU:1 before, /device:TPU:24 now
where the time goes in v1:
time: 133 us; the launch traced here: 132 us
  starting transfers between devices  71.2 us (54%)
  waiting for transfers between devices  48.3 us (36%)
  Pallas kernels  4.86 us (4%)
  local copies, waits for them, and re-layouts  3.98 us (3%)
  between operations  2.46 us (2%)
    ppermute x18, starting transfers between devices, swap(): return lax.ppermute(value, axis, [(i, i ^ mask) for i in range(size)])  71.2 us
    ppermute x18, waiting for transfers between devices, swap(): return lax.ppermute(value, axis, [(i, i ^ mask) for i in range(size)])  48.3 us
    pallas_call x1, Pallas kernels, on_device(): pl.pallas_call(pair_kernel, out_shape=(jax.ShapeDtypeStruct((ni, D), jnp....  3.84 us
    unnamed x17, local copies, waits for them, and re-layouts  3.04 us
  transfers between devices with their start and end apart: 18, of which 9 were waited for; matrix products, arithmetic and copies ran while one was open for 2% of the time, Pallas kernels for 0%

profile of v1, /device:TPU:24, one launch (start us, length us, event | category | flops | bytes accessed | tf_op | source)
XLA Modules:
  0.0 131.8 jit_solution(5762484619679667166)
XLA Ops:
  0.6 0.8 copy-done
  1.4 0.8 copy-done.2
  2.3 0.1 unit.1
  2.4 3.8 %collective-permute-start = (bf16[24,1152]{1,0:T(8,128)(2,1)S(1)}, bf16[24,1152]{1,0:T(8,128)(2,1)S(1)}, u32[]{:S(2)}, u32[]{:S(2)}) collective-permute-start(bf16[24,1152]{1,0:T(8,128)(2,1)S(1)} %get-tuple-element.6), channel_id=1, source_target_pairs={{0,8},{8,0},{16,24},{24,16},{1,9},{9,1},{17,25},{25,17},{2,10},{10... | collective-permute-start | bytes 165896 | tf_op jit(solution)/shard_map/ppermute | solution.py:25
  6.2 9.1 %collective-permute-start.5 = (bf16[24,1152]{1,0:T(8,128)(2,1)S(1)}, bf16[24,1152]{1,0:T(8,128)(2,1)S(1)}, u32[]{:S(2)}, u32[]{:S(2)}) collective-permute-start(bf16[24,1152]{1,0:T(8,128)(2,1)S(1)} %get-tuple-element.7), channel_id=1, source_target_pairs={{0,128},{128,0},{256,384},{384,256},{1,129},{129,1},{257,385},{385... | collective-permute-start | bytes 165896 | tf_op jit(solution)/shard_map/ppermute | solution.py:25
  15.3 0.6 constant_dynamic-update-slice_fusion.4
  16.0 0.1 stack.194
  16.1 0.1 add_select_fusion
  16.2 0.1 stack.211
  16.3 0.1 add_select_fusion.1
  17.7 0.1 pad_maximum_fusion.6.scal_ref
  17.8 0.2 select_n.32.row_ref
  17.9 0.1 select_n.31.col_ref
  18.1 5.2 %collective-permute-start.1 = (bf16[48,1152]{1,0:T(8,128)(2,1)S(1)}, bf16[48,1152]{1,0:T(8,128)(2,1)S(1)}, u32[]{:S(2)}, u32[]{:S(2)}) collective-permute-start(bf16[48,1152]{1,0:T(8,128)(2,1)S(1)} %pad_maximum_fusion.4), channel_id=1, source_target_pairs={{0,16},{8,24},{16,0},{24,8},{1,17},{9,25},{17,1},{25,9},{2,18},{10... | collective-permute-start | bytes 331784 | tf_op jit(solution)/shard_map/ppermute | solution.py:25
  23.3 6.4 %collective-permute-start.6 = (bf16[48,1152]{1,0:T(8,128)(2,1)S(1)}, bf16[48,1152]{1,0:T(8,128)(2,1)S(1)}, u32[]{:S(2)}, u32[]{:S(2)}) collective-permute-start(bf16[48,1152]{1,0:T(8,128)(2,1)S(1)} %pad_maximum_fusion.5), channel_id=1, source_target_pairs={{0,384},{128,256},{256,128},{384,0},{1,385},{129,257},{257,129},{3... | collective-permute-start | bytes 331784 | tf_op jit(solution)/shard_map/ppermute | solution.py:25
  29.7 0.6 constant_dynamic-update-slice_fusion.3
  30.4 2.8 %collective-permute-start.2 = (bf16[96,1152]{1,0:T(8,128)(2,1)S(1)}, bf16[96,1152]{1,0:T(8,128)(2,1)S(1)}, u32[]{:S(2)}, u32[]{:S(2)}) collective-permute-start(bf16[96,1152]{1,0:T(8,128)(2,1)S(1)} %pad_maximum_fusion.2), channel_id=1, source_target_pairs={{0,2},{2,0},{4,6},{6,4},{1,3},{3,1},{5,7},{7,5},{8,10},{10,8},{12,... | collective-permute-start | bytes 663560 | tf_op jit(solution)/shard_map/ppermute | solution.py:25
  33.2 5.1 %collective-permute-done.6 = bf16[48,1152]{1,0:T(8,128)(2,1)S(1)} collective-permute-done((bf16[48,1152]{1,0:T(8,128)(2,1)S(1)}, bf16[48,1152]{1,0:T(8,128)(2,1)S(1)}, u32[]{:S(2)}, u32[]{:S(2)}) %collective-permute-start.6) | collective-permute-done | bytes 110624 | tf_op jit(solution)/shard_map/ppermute | solution.py:25
  38.3 3.4 %collective-permute-start.7 = (bf16[96,1152]{1,0:T(8,128)(2,1)S(1)}, bf16[96,1152]{1,0:T(8,128)(2,1)S(1)}, u32[]{:S(2)}, u32[]{:S(2)}) collective-permute-start(bf16[96,1152]{1,0:T(8,128)(2,1)S(1)} %pad_maximum_fusion.3), channel_id=1, source_target_pairs={{0,32},{32,0},{64,96},{96,64},{1,33},{33,1},{65,97},{97,65},{2,34}... | collective-permute-start | bytes 663560 | tf_op jit(solution)/shard_map/ppermute | solution.py:25
  41.7 2.1 %collective-permute-start.3 = (bf16[192,1152]{1,0:T(8,128)(2,1)S(1)}, bf16[192,1152]{1,0:T(8,128)(2,1)S(1)}, u32[]{:S(2)}, u32[]{:S(2)}) collective-permute-start(bf16[192,1152]{1,0:T(8,128)(2,1)S(1)} %pad_maximum_fusion), channel_id=1, source_target_pairs={{0,6},{2,4},{4,2},{6,0},{1,7},{3,5},{5,3},{7,1},{8,14},{10,12},{12... | collective-permute-start | bytes 1327112 | tf_op jit(solution)/shard_map/ppermute | solution.py:25
  44.0 12.0 %collective-permute-done.3 = bf16[192,1152]{1,0:T(8,128)(2,1)S(1)} collective-permute-done((bf16[192,1152]{1,0:T(8,128)(2,1)S(1)}, bf16[192,1152]{1,0:T(8,128)(2,1)S(1)}, u32[]{:S(2)}, u32[]{:S(2)}) %collective-permute-start.3) | collective-permute-done | bytes 442400 | tf_op jit(solution)/shard_map/ppermute | solution.py:25
  56.0 0.1 constant_dynamic-update-slice_fusion
  56.1 1.9 %collective-permute-start.4 = (bf16[384,1152]{1,0:T(8,128)(2,1)S(1)}, bf16[384,1152]{1,0:T(8,128)(2,1)S(1)}, u32[]{:S(2)}, u32[]{:S(2)}) collective-permute-start(bf16[384,1152]{1,0:T(8,128)(2,1)S(1)} %get-tuple-element.10), channel_id=1, source_target_pairs={{0,1},{1,0},{2,3},{3,2},{4,5},{5,4},{6,7},{7,6},{8,9},{9,8},{10,11... | collective-permute-start | bytes 2654216 | tf_op jit(solution)/shard_map/ppermute | solution.py:25
  58.1 4.0 %collective-permute-start.8 = (bf16[192,1152]{1,0:T(8,128)(2,1)S(1)}, bf16[192,1152]{1,0:T(8,128)(2,1)S(1)}, u32[]{:S(2)}, u32[]{:S(2)}) collective-permute-start(bf16[192,1152]{1,0:T(8,128)(2,1)S(1)} %pad_maximum_fusion.1), channel_id=1, source_target_pairs={{0,96},{32,64},{64,32},{96,0},{1,97},{33,65},{65,33},{97,1},{2,98}... | collective-permute-start | bytes 1327112 | tf_op jit(solution)/shard_map/ppermute | solution.py:25
  62.2 11.6 %collective-permute-done.8 = bf16[192,1152]{1,0:T(8,128)(2,1)S(1)} collective-permute-done((bf16[192,1152]{1,0:T(8,128)(2,1)S(1)}, bf16[192,1152]{1,0:T(8,128)(2,1)S(1)}, u32[]{:S(2)}, u32[]{:S(2)}) %collective-permute-start.8) | collective-permute-done | bytes 442400 | tf_op jit(solution)/shard_map/ppermute | solution.py:25
  73.8 0.1 constant_dynamic-update-slice_fusion.5.img_ref
  74.0 3.8 %pairs.1 = (bf16[768,1152]{1,0:T(8,128)(2,1)S(1)}, bf16[384,1152]{1,0:T(8,128)(2,1)S(1)}) custom-call(f32[2]{0:T(128)S(1)} %pad_maximum_fusion.6.scal_ref, bf16[768,1152]{1,0:T(8,128)(2,1)S(1)} %constant_dynamic-update-slice_fusion.5.img_ref, bf16[384,1152]{1,0:T(8,128)(2,1)S(1)} %constant_dynamic-update-slice_fusion.11.txt_ref, ...), custom_call_target="tpu_custom_call" | custom-call | tf_op jit(solution)/shard_map/pairs/pallas_call | solution.py:142
  77.8 0.1 slice.55
  77.9 1.9 %collective-permute-start.9 = (bf16[384,1152]{1,0:T(8,128)(2,1)S(1)}, bf16[384,1152]{1,0:T(8,128)(2,1)S(1)}, u32[]{:S(2)}, u32[]{:S(2)}) collective-permute-start(bf16[384,1152]{1,0:T(8,128)(2,1)S(1)} %slice.55), channel_id=1, source_target_pairs={{0,1},{1,0},{2,3},{3,2},{4,5},{5,4},{6,7},{7,6},{8,9},{9,8},{10,11... | collective-permute-start | bytes 2654216 | tf_op jit(solution)/shard_map/ppermute | solution.py:25
  79.8 4.0 %collective-permute-start.14 = (bf16[192,1152]{1,0:T(8,128)(2,1)S(1)}, bf16[192,1152]{1,0:T(8,128)(2,1)S(1)}, u32[]{:S(2)}, u32[]{:S(2)}) collective-permute-start(bf16[192,1152]{1,0:T(8,128)(2,1)S(1)} %slice.65), channel_id=1, source_target_pairs={{0,96},{32,64},{64,32},{96,0},{1,97},{33,65},{65,33},{97,1},{2,98}... | collective-permute-start | bytes 1327112 | tf_op jit(solution)/shard_map/ppermute | solution.py:25
  83.9 0.2 add_convert_fusion
  84.1 2.2 %collective-permute-start.10 = (bf16[192,1152]{1,0:T(8,128)(2,1)S(1)}, bf16[192,1152]{1,0:T(8,128)(2,1)S(1)}, u32[]{:S(2)}, u32[]{:S(2)}) collective-permute-start(bf16[192,1152]{1,0:T(8,128)(2,1)S(1)} %slice.73), channel_id=1, source_target_pairs={{0,6},{2,4},{4,2},{6,0},{1,7},{3,5},{5,3},{7,1},{8,14},{10,12},{12... | collective-permute-start | bytes 1327112 | tf_op jit(solution)/shard_map/ppermute | solution.py:25
  86.3 9.2 %collective-permute-done.14 = bf16[192,1152]{1,0:T(8,128)(2,1)S(1)} collective-permute-done((bf16[192,1152]{1,0:T(8,128)(2,1)S(1)}, bf16[192,1152]{1,0:T(8,128)(2,1)S(1)}, u32[]{:S(2)}, u32[]{:S(2)}) %collective-permute-start.14) | collective-permute-done | bytes 442400 | tf_op jit(solution)/shard_map/ppermute | solution.py:25
  95.5 0.1 add_convert_fusion.1
  95.7 1.9 %collective-permute-start.15 = (bf16[96,1152]{1,0:T(8,128)(2,1)S(1)}, bf16[96,1152]{1,0:T(8,128)(2,1)S(1)}, u32[]{:S(2)}, u32[]{:S(2)}) collective-permute-start(bf16[96,1152]{1,0:T(8,128)(2,1)S(1)} %slice.81), channel_id=1, source_target_pairs={{0,32},{32,0},{64,96},{96,64},{1,33},{33,1},{65,97},{97,65},{2,34}... | collective-permute-start | bytes 663560 | tf_op jit(solution)/shard_map/ppermute | solution.py:25
  97.6 1.9 %collective-permute-done.10 = bf16[192,1152]{1,0:T(8,128)(2,1)S(1)} collective-permute-done((bf16[192,1152]{1,0:T(8,128)(2,1)S(1)}, bf16[192,1152]{1,0:T(8,128)(2,1)S(1)}, u32[]{:S(2)}, u32[]{:S(2)}) %collective-permute-start.10) | collective-permute-done | bytes 442400 | tf_op jit(solution)/shard_map/ppermute | solution.py:25
  99.5 0.1 add_convert_fusion.2
  99.7 1.9 %collective-permute-start.11 = (bf16[96,1152]{1,0:T(8,128)(2,1)S(1)}, bf16[96,1152]{1,0:T(8,128)(2,1)S(1)}, u32[]{:S(2)}, u32[]{:S(2)}) collective-permute-start(bf16[96,1152]{1,0:T(8,128)(2,1)S(1)} %slice.75), channel_id=1, source_target_pairs={{0,2},{2,0},{4,6},{6,4},{1,3},{3,1},{5,7},{7,5},{8,10},{10,8},{12,... | collective-permute-start | bytes 663560 | tf_op jit(solution)/shard_map/ppermute | solution.py:25
  101.6 3.0 %collective-permute-done.15 = bf16[96,1152]{1,0:T(8,128)(2,1)S(1)} collective-permute-done((bf16[96,1152]{1,0:T(8,128)(2,1)S(1)}, bf16[96,1152]{1,0:T(8,128)(2,1)S(1)}, u32[]{:S(2)}, u32[]{:S(2)}) %collective-permute-start.15) | collective-permute-done | bytes 221216 | tf_op jit(solution)/shard_map/ppermute | solution.py:25
  104.7 8.4 %collective-permute-start.16 = (bf16[48,1152]{1,0:T(8,128)(2,1)S(1)}, bf16[48,1152]{1,0:T(8,128)(2,1)S(1)}, u32[]{:S(2)}, u32[]{:S(2)}) collective-permute-start(bf16[48,1152]{1,0:T(8,128)(2,1)S(1)} %slice.83), channel_id=1, source_target_pairs={{0,384},{128,256},{256,128},{384,0},{1,385},{129,257},{257,129},{3... | collective-permute-start | bytes 331784 | tf_op jit(solution)/shard_map/ppermute | solution.py:25
  113.1 0.1 add_convert_fusion.4
  113.2 1.9 %collective-permute-start.12 = (bf16[48,1152]{1,0:T(8,128)(2,1)S(1)}, bf16[48,1152]{1,0:T(8,128)(2,1)S(1)}, u32[]{:S(2)}, u32[]{:S(2)}) collective-permute-start(bf16[48,1152]{1,0:T(8,128)(2,1)S(1)} %slice.77), channel_id=1, source_target_pairs={{0,16},{8,24},{16,0},{24,8},{1,17},{9,25},{17,1},{25,9},{2,18},{10... | collective-permute-start | bytes 331784 | tf_op jit(solution)/shard_map/ppermute | solution.py:25
  115.1 1.3 %collective-permute-done.16 = bf16[48,1152]{1,0:T(8,128)(2,1)S(1)} collective-permute-done((bf16[48,1152]{1,0:T(8,128)(2,1)S(1)}, bf16[48,1152]{1,0:T(8,128)(2,1)S(1)}, u32[]{:S(2)}, u32[]{:S(2)}) %collective-permute-start.16) | collective-permute-done | bytes 110624 | tf_op jit(solution)/shard_map/ppermute | solution.py:25
  116.5 8.3 %collective-permute-start.17 = (bf16[24,1152]{1,0:T(8,128)(2,1)S(1)}, bf16[24,1152]{1,0:T(8,128)(2,1)S(1)}, u32[]{:S(2)}, u32[]{:S(2)}) collective-permute-start(bf16[24,1152]{1,0:T(8,128)(2,1)S(1)} %slice.85), channel_id=1, source_target_pairs={{0,128},{128,0},{256,384},{384,256},{1,129},{129,1},{257,385},{385... | collective-permute-start | bytes 165896 | tf_op jit(solution)/shard_map/ppermute | solution.py:25
  124.9 1.9 %collective-permute-start.13 = (bf16[24,1152]{1,0:T(8,128)(2,1)S(1)}, bf16[24,1152]{1,0:T(8,128)(2,1)S(1)}, u32[]{:S(2)}, u32[]{:S(2)}) collective-permute-start(bf16[24,1152]{1,0:T(8,128)(2,1)S(1)} %slice.79), channel_id=1, source_target_pairs={{0,8},{8,0},{16,24},{24,16},{1,9},{9,1},{17,25},{25,17},{2,10},{10... | collective-permute-start | bytes 165896 | tf_op jit(solution)/shard_map/ppermute | solution.py:25
  126.8 0.1 collective-permute-done.17
  126.9 4.0 %collective-permute-done.13 = bf16[24,1152]{1,0:T(8,128)(2,1)S(1)} collective-permute-done((bf16[24,1152]{1,0:T(8,128)(2,1)S(1)}, bf16[24,1152]{1,0:T(8,128)(2,1)S(1)}, u32[]{:S(2)}, u32[]{:S(2)}) %collective-permute-start.13) | collective-permute-done | bytes 55328 | tf_op jit(solution)/shard_map/ppermute | solution.py:25
  130.9 0.9 back.1
  (45 shorter events, 0.7 us)
Async XLA Ops:
  0.6 0.8 copy-start
  1.4 0.8 copy-start.2
  2.4 15.6 %collective-permute-start = (bf16[24,1152]{1,0:T(8,128)(2,1)S(1)}, bf16[24,1152]{1,0:T(8,128)(2,1)S(1)}, u32[]{:S(2)}, u32[]{:S(2)}) collective-permute-start(bf16[24,1152]{1,0:T(8,128)(2,1)S(1)} %get-tuple-element.6), channel_id=1, source_target_pairs={{0,8},{8,0},{16,24},{24,16},{1,9},{9,1},{17,25},{25,17},{2,10},{10... | collective-permute-start | bytes 165896 | tf_op jit(solution)/shard_map/ppermute | solution.py:25
  6.2 17.0 %collective-permute-start.5 = (bf16[24,1152]{1,0:T(8,128)(2,1)S(1)}, bf16[24,1152]{1,0:T(8,128)(2,1)S(1)}, u32[]{:S(2)}, u32[]{:S(2)}) collective-permute-start(bf16[24,1152]{1,0:T(8,128)(2,1)S(1)} %get-tuple-element.7), channel_id=1, source_target_pairs={{0,128},{128,0},{256,384},{384,256},{1,129},{129,1},{257,385},{385... | collective-permute-start | bytes 165896 | tf_op jit(solution)/shard_map/ppermute | solution.py:25
  18.1 12.3 %collective-permute-start.1 = (bf16[48,1152]{1,0:T(8,128)(2,1)S(1)}, bf16[48,1152]{1,0:T(8,128)(2,1)S(1)}, u32[]{:S(2)}, u32[]{:S(2)}) collective-permute-start(bf16[48,1152]{1,0:T(8,128)(2,1)S(1)} %pad_maximum_fusion.4), channel_id=1, source_target_pairs={{0,16},{8,24},{16,0},{24,8},{1,17},{9,25},{17,1},{25,9},{2,18},{10... | collective-permute-start | bytes 331784 | tf_op jit(solution)/shard_map/ppermute | solution.py:25
  23.3 15.0 %collective-permute-start.6 = (bf16[48,1152]{1,0:T(8,128)(2,1)S(1)}, bf16[48,1152]{1,0:T(8,128)(2,1)S(1)}, u32[]{:S(2)}, u32[]{:S(2)}) collective-permute-start(bf16[48,1152]{1,0:T(8,128)(2,1)S(1)} %pad_maximum_fusion.5), channel_id=1, source_target_pairs={{0,384},{128,256},{256,128},{384,0},{1,385},{129,257},{257,129},{3... | collective-permute-start | bytes 331784 | tf_op jit(solution)/shard_map/ppermute | solution.py:25
  30.3 13.5 %copy-start.4 = (bf16[384,1152]{1,0:T(8,128)(2,1)S(1)}, bf16[384,1152]{1,0:T(8,128)(2,1)}, u32[]{:S(2)}) copy-start(bf16[384,1152]{1,0:T(8,128)(2,1)} %get-tuple-element.16) | copy-start | bytes 2654212
  30.4 11.3 %collective-permute-start.2 = (bf16[96,1152]{1,0:T(8,128)(2,1)S(1)}, bf16[96,1152]{1,0:T(8,128)(2,1)S(1)}, u32[]{:S(2)}, u32[]{:S(2)}) collective-permute-start(bf16[96,1152]{1,0:T(8,128)(2,1)S(1)} %pad_maximum_fusion.2), channel_id=1, source_target_pairs={{0,2},{2,0},{4,6},{6,4},{1,3},{3,1},{5,7},{7,5},{8,10},{10,8},{12,... | collective-permute-start | bytes 663560 | tf_op jit(solution)/shard_map/ppermute | solution.py:25
  38.3 19.8 %collective-permute-start.7 = (bf16[96,1152]{1,0:T(8,128)(2,1)S(1)}, bf16[96,1152]{1,0:T(8,128)(2,1)S(1)}, u32[]{:S(2)}, u32[]{:S(2)}) collective-permute-start(bf16[96,1152]{1,0:T(8,128)(2,1)S(1)} %pad_maximum_fusion.3), channel_id=1, source_target_pairs={{0,32},{32,0},{64,96},{96,64},{1,33},{33,1},{65,97},{97,65},{2,34}... | collective-permute-start | bytes 663560 | tf_op jit(solution)/shard_map/ppermute | solution.py:25
  41.7 14.3 %collective-permute-start.3 = (bf16[192,1152]{1,0:T(8,128)(2,1)S(1)}, bf16[192,1152]{1,0:T(8,128)(2,1)S(1)}, u32[]{:S(2)}, u32[]{:S(2)}) collective-permute-start(bf16[192,1152]{1,0:T(8,128)(2,1)S(1)} %pad_maximum_fusion), channel_id=1, source_target_pairs={{0,6},{2,4},{4,2},{6,0},{1,7},{3,5},{5,3},{7,1},{8,14},{10,12},{12... | collective-permute-start | bytes 1327112 | tf_op jit(solution)/shard_map/ppermute | solution.py:25
  56.1 17.7 %collective-permute-start.4 = (bf16[384,1152]{1,0:T(8,128)(2,1)S(1)}, bf16[384,1152]{1,0:T(8,128)(2,1)S(1)}, u32[]{:S(2)}, u32[]{:S(2)}) collective-permute-start(bf16[384,1152]{1,0:T(8,128)(2,1)S(1)} %get-tuple-element.10), channel_id=1, source_target_pairs={{0,1},{1,0},{2,3},{3,2},{4,5},{5,4},{6,7},{7,6},{8,9},{9,8},{10,11... | collective-permute-start | bytes 2654216 | tf_op jit(solution)/shard_map/ppermute | solution.py:25
  58.1 15.7 %collective-permute-start.8 = (bf16[192,1152]{1,0:T(8,128)(2,1)S(1)}, bf16[192,1152]{1,0:T(8,128)(2,1)S(1)}, u32[]{:S(2)}, u32[]{:S(2)}) collective-permute-start(bf16[192,1152]{1,0:T(8,128)(2,1)S(1)} %pad_maximum_fusion.1), channel_id=1, source_target_pairs={{0,96},{32,64},{64,32},{96,0},{1,97},{33,65},{65,33},{97,1},{2,98}... | collective-permute-start | bytes 1327112 | tf_op jit(solution)/shard_map/ppermute | solution.py:25
  77.9 6.0 %collective-permute-start.9 = (bf16[384,1152]{1,0:T(8,128)(2,1)S(1)}, bf16[384,1152]{1,0:T(8,128)(2,1)S(1)}, u32[]{:S(2)}, u32[]{:S(2)}) collective-permute-start(bf16[384,1152]{1,0:T(8,128)(2,1)S(1)} %slice.55), channel_id=1, source_target_pairs={{0,1},{1,0},{2,3},{3,2},{4,5},{5,4},{6,7},{7,6},{8,9},{9,8},{10,11... | collective-permute-start | bytes 2654216 | tf_op jit(solution)/shard_map/ppermute | solution.py:25
  79.8 15.7 %collective-permute-start.14 = (bf16[192,1152]{1,0:T(8,128)(2,1)S(1)}, bf16[192,1152]{1,0:T(8,128)(2,1)S(1)}, u32[]{:S(2)}, u32[]{:S(2)}) collective-permute-start(bf16[192,1152]{1,0:T(8,128)(2,1)S(1)} %slice.65), channel_id=1, source_target_pairs={{0,96},{32,64},{64,32},{96,0},{1,97},{33,65},{65,33},{97,1},{2,98}... | collective-permute-start | bytes 1327112 | tf_op jit(solution)/shard_map/ppermute | solution.py:25
  84.1 15.4 %collective-permute-start.10 = (bf16[192,1152]{1,0:T(8,128)(2,1)S(1)}, bf16[192,1152]{1,0:T(8,128)(2,1)S(1)}, u32[]{:S(2)}, u32[]{:S(2)}) collective-permute-start(bf16[192,1152]{1,0:T(8,128)(2,1)S(1)} %slice.73), channel_id=1, source_target_pairs={{0,6},{2,4},{4,2},{6,0},{1,7},{3,5},{5,3},{7,1},{8,14},{10,12},{12... | collective-permute-start | bytes 1327112 | tf_op jit(solution)/shard_map/ppermute | solution.py:25
  95.7 8.9 %collective-permute-start.15 = (bf16[96,1152]{1,0:T(8,128)(2,1)S(1)}, bf16[96,1152]{1,0:T(8,128)(2,1)S(1)}, u32[]{:S(2)}, u32[]{:S(2)}) collective-permute-start(bf16[96,1152]{1,0:T(8,128)(2,1)S(1)} %slice.81), channel_id=1, source_target_pairs={{0,32},{32,0},{64,96},{96,64},{1,33},{33,1},{65,97},{97,65},{2,34}... | collective-permute-start | bytes 663560 | tf_op jit(solution)/shard_map/ppermute | solution.py:25
  99.6 31.3 %copy-start.1 = (bf16[22,1152]{1,0:T(8,128)(2,1)S(1)}, bf16[22,1152]{1,0:T(8,128)(2,1)}, u32[]{:S(2)}) copy-start(bf16[22,1152]{1,0:T(8,128)(2,1)} %img_ref.3) | copy-start | bytes 152068
  99.7 31.3 %copy-start.3 = (bf16[22,1152]{1,0:T(8,128)(2,1)S(1)}, bf16[22,1152]{1,0:T(8,128)(2,1)}, u32[]{:S(2)}) copy-start(bf16[22,1152]{1,0:T(8,128)(2,1)} %txt_ref.3) | copy-start | bytes 152068
  99.7 13.4 %collective-permute-start.11 = (bf16[96,1152]{1,0:T(8,128)(2,1)S(1)}, bf16[96,1152]{1,0:T(8,128)(2,1)S(1)}, u32[]{:S(2)}, u32[]{:S(2)}) collective-permute-start(bf16[96,1152]{1,0:T(8,128)(2,1)S(1)} %slice.75), channel_id=1, source_target_pairs={{0,2},{2,0},{4,6},{6,4},{1,3},{3,1},{5,7},{7,5},{8,10},{10,8},{12,... | collective-permute-start | bytes 663560 | tf_op jit(solution)/shard_map/ppermute | solution.py:25
  104.7 11.8 %collective-permute-start.16 = (bf16[48,1152]{1,0:T(8,128)(2,1)S(1)}, bf16[48,1152]{1,0:T(8,128)(2,1)S(1)}, u32[]{:S(2)}, u32[]{:S(2)}) collective-permute-start(bf16[48,1152]{1,0:T(8,128)(2,1)S(1)} %slice.83), channel_id=1, source_target_pairs={{0,384},{128,256},{256,128},{384,0},{1,385},{129,257},{257,129},{3... | collective-permute-start | bytes 331784 | tf_op jit(solution)/shard_map/ppermute | solution.py:25
  113.2 11.6 %collective-permute-start.12 = (bf16[48,1152]{1,0:T(8,128)(2,1)S(1)}, bf16[48,1152]{1,0:T(8,128)(2,1)S(1)}, u32[]{:S(2)}, u32[]{:S(2)}) collective-permute-start(bf16[48,1152]{1,0:T(8,128)(2,1)S(1)} %slice.77), channel_id=1, source_target_pairs={{0,16},{8,24},{16,0},{24,8},{1,17},{9,25},{17,1},{25,9},{2,18},{10... | collective-permute-start | bytes 331784 | tf_op jit(solution)/shard_map/ppermute | solution.py:25
  116.5 10.4 %collective-permute-start.17 = (bf16[24,1152]{1,0:T(8,128)(2,1)S(1)}, bf16[24,1152]{1,0:T(8,128)(2,1)S(1)}, u32[]{:S(2)}, u32[]{:S(2)}) collective-permute-start(bf16[24,1152]{1,0:T(8,128)(2,1)S(1)} %slice.85), channel_id=1, source_target_pairs={{0,128},{128,0},{256,384},{384,256},{1,129},{129,1},{257,385},{385... | collective-permute-start | bytes 165896 | tf_op jit(solution)/shard_map/ppermute | solution.py:25
  124.9 6.0 %collective-permute-start.13 = (bf16[24,1152]{1,0:T(8,128)(2,1)S(1)}, bf16[24,1152]{1,0:T(8,128)(2,1)S(1)}, u32[]{:S(2)}, u32[]{:S(2)}) collective-permute-start(bf16[24,1152]{1,0:T(8,128)(2,1)S(1)} %slice.79), channel_id=1, source_target_pairs={{0,8},{8,0},{16,24},{24,16},{1,9},{9,1},{17,25},{25,17},{2,10},{10... | collective-permute-start | bytes 165896 | tf_op jit(solution)/shard_map/ppermute | solution.py:25

commit v2 on v1

--- a/solution.py
+++ b/solution.py
@@ -13,33 +13,32 @@
 PAD = 24
 AXES = ("zh", "x", "zl", "y", "core")
 SIZES = (4, 4, 4, 4, 2)
-IMG_STAGES = (("zl", "pair2"), ("y", "pair3"), ("core", "pair"))
-TXT_STAGES = (("zh", "pair3"), ("x", "pair3"))
-IMG_BACK = None
-TXT_BACK = None
+OUT = (
+    ("t", "zh", (1, 3)),
+    ("i", "zl", "a"),
+    ("t", "zh", (3, 1)),
+    ("i", "y", "a"),
+    ("t", "x", (1, 3)),
+    ("t", "x", (3, 1)),
+    ("i", "core", (1, 1)),
+)
+BACK = tuple(reversed(OUT))
 VMEM = 48 * 1024 * 1024
 
 
-def swap(value, axis, mask):
+def swap(value, axis, masks):
     size = SIZES[AXES.index(axis)]
-    return lax.ppermute(value, axis, [(i, i ^ mask) for i in range(size)])
-
-
-def order(way):
-    return {"pair": (0, 1), "pair2": (0, 1, 2, 3), "pair3": (0, 1, 3, 2), "direct": (0, 1, 3, 2), "a2a": None}[way]
+    if axis == "core" or masks[0] == masks[1]:
+        return lax.ppermute(value, axis, [(i, i ^ masks[0]) for i in range(size)])
+    return lax.ppermute(value, (axis, "core"), [(2 * i + c, 2 * (i ^ masks[c]) + c) for i in range(size) for c in range(2)])
 
 
 def spread(held, axis, way):
-    if way == "pair":
-        return jnp.concatenate([held, swap(held, axis, 1)])
-    if way in ("pair2", "pair3"):
-        held = jnp.concatenate([held, swap(held, axis, 1)])
-        return jnp.concatenate([held, swap(held, axis, 2 if way == "pair2" else 3)])
-    if way == "direct":
-        return jnp.concatenate([held] + [swap(held, axis, m) for m in (1, 3, 2)])
-    size = SIZES[AXES.index(axis)]
-    out = lax.all_to_all(jnp.broadcast_to(held[None], (size,) + held.shape), axis, 0, 0, tiled=True)
-    return out.reshape((-1, held.shape[1]))
+    if way == "a":
+        size = SIZES[AXES.index(axis)]
+        out = lax.all_to_all(jnp.broadcast_to(held[None], (size,) + held.shape), axis, 0, 0, tiled=True)
+        return out.reshape((-1, held.shape[1]))
+    return jnp.concatenate([held, swap(held, axis, way)])
 
 
 def add(parts):
@@ -47,33 +46,47 @@
 
 
 def collect(held, axis, way):
-    size = SIZES[AXES.index(axis)]
-    if way in ("pair", "pair2", "pair3"):
-        for mask in {"pair": (1,), "pair2": (2, 1), "pair3": (3, 1)}[way]:
-            half = held.shape[0] // 2
-            held = add([held[:half], swap(held[half:], axis, mask)])
-        return held
-    parts = held.reshape((size, -1, held.shape[1]))
-    if way == "direct":
-        return add([parts[0]] + [swap(parts[k], axis, m) for k, m in ((1, 1), (2, 3), (3, 2))])
-    parts = lax.all_to_all(parts, axis, 0, 0, tiled=True)
-    return add([parts[k] for k in range(size)])
+    if way == "a":
+        size = SIZES[AXES.index(axis)]
+        parts = lax.all_to_all(held.reshape((size, -1, held.shape[1])), axis, 0, 0, tiled=True)
+        return add([parts[k] for k in range(size)])
+    half = held.shape[0] // 2
+    return add([held[:half], swap(held[half:], axis, way)])
 
 
-def slots(stages, names):
-    coords = {n: lax.axis_index(n) for n in names}
-    found = [jnp.int32(0)]
-    weight = {}
-    total = 1
-    for n in reversed(names):
-        weight[n] = total
-        total *= SIZES[AXES.index(n)]
-    for axis, way in stages:
-        seq = order(way)
-        size = SIZES[AXES.index(axis)]
-        here = [jnp.int32(k) if seq is None else coords[axis] ^ seq[k] for k in range(size)]
-        found = [f + weight[axis] * h for h in here for f in found]
-    return jnp.stack(found)
+def run(steps, do, held):
+    for step in steps:
+        if step == "b":
+            held["i"], held["t"] = lax.optimization_barrier((held["i"], held["t"]))
+        else:
+            which, axis, way = step
+            held[which] = do(held[which], axis, way)
+
+
+def slots(which, names):
+    core = lax.axis_index("core")
+    here = {n: lax.axis_index(n) for n in names}
+    both = []
+    for c in (core, 1 - core):
+        both.append([{n: c if n == "core" else here[n] for n in names}])
+    for step in OUT:
+        if step == "b" or step[0] != which:
+            continue
+        _, axis, way = step
+        if axis == "core":
+            both = [both[0] + both[1], both[1] + both[0]]
+        elif way == "a":
+            both = [[{**f, axis: jnp.int32(k)} for k in range(SIZES[AXES.index(axis)]) for f in b] for b in both]
+        else:
+            masks = [jnp.where(c == 0, way[0], way[1]) for c in (core, 1 - core)]
+            both = [b + [{**f, axis: f[axis] ^ m} for f in b] for b, m in zip(both, masks)]
+    blocks = []
+    for f in both[0]:
+        block = jnp.int32(0)
+        for n in names:
+            block = block * SIZES[AXES.index(n)] + f[n]
+        blocks.append(block)
+    return jnp.stack(blocks)
 
 
 def unit_kernel(img_ref, txt_ref, img_out, txt_out):
@@ -126,14 +139,13 @@
 def on_device(images, texts, logarithmic_scale, similarity_bias):
     block = jax.ShapeDtypeStruct((PAD, D), jnp.bfloat16)
     img, txt = pl.pallas_call(unit_kernel, out_shape=(block, block), in_specs=[vm()] * 2, out_specs=(vm(), vm()), compiler_params=PARAMS, name="unit")(images, texts)
-    for axis, way in TXT_STAGES:
-        txt = spread(txt, axis, way)
-    for axis, way in IMG_STAGES:
-        img = spread(img, axis, way)
+    held = {"i": img, "t": txt}
+    run(OUT, spread, held)
+    img, txt = held["i"], held["t"]
     row = lax.axis_index("zh") * 4 + lax.axis_index("x")
     col = (lax.axis_index("zl") * 4 + lax.axis_index("y")) * 2 + lax.axis_index("core")
-    img_ids = row * 32 + slots(IMG_STAGES, ("zl", "y", "core"))
-    txt_ids = col * 16 + slots(TXT_STAGES, ("zh", "x"))
+    img_ids = row * 32 + slots("i", ("zl", "y", "core"))
+    txt_ids = col * 16 + slots("t", ("zh", "x"))
     within = jnp.arange(PAD, dtype=jnp.int32)
     row_ids = jnp.where(within < ROWS, img_ids[:, None] * ROWS + within, -1).reshape(-1, 1)
     col_ids = jnp.where(within < ROWS, txt_ids[:, None] * ROWS + within, -2).reshape(1, -1)
@@ -148,10 +160,9 @@
         compiler_params=PARAMS,
         name="pairs",
     )(scal, img, txt, row_ids, col_ids)
-    for axis, way in reversed(TXT_BACK or TXT_STAGES):
-        gtxt = collect(gtxt, axis, way)
-    for axis, way in reversed(IMG_BACK or IMG_STAGES):
-        gimg = collect(gimg, axis, way)
+    held = {"i": gimg, "t": gtxt}
+    run(BACK, collect, held)
+    gimg, gtxt = held["i"], held["t"]
     wide = jax.ShapeDtypeStruct((ROWS, D), jnp.float32)
     return pl.pallas_call(back_kernel, out_shape=(wide, wide), in_specs=[vm()] * 4, out_specs=(vm(), vm()), compiler_params=PARAMS, name="back")(images, texts, gimg, gtxt)
 

time: 133 us -> 116 us (0.87)
  the two profiles are of different devices: /device:TPU:24 before, /device:TPU:36 now
where the time goes in v2:
time: 116 us; the launch traced here: 115 us
  starting transfers between devices  59 us (51%)
  waiting for transfers between devices  42.4 us (37%)
  Pallas kernels  4.89 us (4%)
  local copies, waits for them, and re-layouts  4.01 us (3%)
  other arithmetic  2.65 us (2%)
  between operations  2.27 us (2%)
    ppermute x8, starting transfers between devices, swap(): lax.ppermute(value, (axis, 'core'), [(2 * i + c, 2 * (i ^ masks[c]) + c)...  34.9 us
    ppermute x8, waiting for transfers between devices, swap(): lax.ppermute(value, (axis, 'core'), [(2 * i + c, 2 * (i ^ masks[c]) + c)...  31.6 us
    all_to_all x2, starting transfers between devices, spread(): lax.all_to_all(jnp.broadcast_to(held[None], (size,) + held.shape), axis,...  10.5 us
    all_to_all x2, starting transfers between devices, collect(): lax.all_to_all(held.reshape((size, -1, held.shape[1])), axis, 0, 0, tiled...  9.71 us
    all_to_all x2, waiting for transfers between devices, spread(): lax.all_to_all(jnp.broadcast_to(held[None], (size,) + held.shape), axis,...  5.45 us
    all_to_all x2, waiting for transfers between devices, collect(): lax.all_to_all(held.reshape((size, -1, held.shape[1])), axis, 0, 0, tiled...  5.3 us
    pallas_call x1, Pallas kernels, on_device(): pl.pallas_call(pair_kernel, out_shape=(jax.ShapeDtypeStruct((ni, D), jnp....  3.88 us
    ppermute x2, starting transfers between devices, swap(): return lax.ppermute(value, axis, [(i, i ^ masks[0]) for i in range(size)])  3.84 us
  transfers between devices with their start and end apart: 14, of which 7 were waited for; matrix products, arithmetic and copies ran while one was open for 4% of the time, Pallas kernels for 0%

profile of v2, /device:TPU:36, one launch (start us, length us, event | category | flops | bytes accessed | tf_op | source)
XLA Modules:
  0.0 115.2 jit_solution(3513888772788232359)
XLA Ops:
  0.6 0.0 copy-start
  0.6 0.8 copy-done
  1.4 0.8 copy-done.2
  2.3 0.1 unit.1
  2.4 9.1 %collective-permute-start.1 = (bf16[24,1152]{1,0:T(8,128)(2,1)S(1)}, bf16[24,1152]{1,0:T(8,128)(2,1)S(1)}, u32[]{:S(2)}, u32[]{:S(2)}) collective-permute-start(bf16[24,1152]{1,0:T(8,128)(2,1)S(1)} %get-tuple-element.7), channel_id=1, source_target_pairs={{0,128},{1,385},{128,0},{129,257},{256,384},{257,129},{384,256},{3... | collective-permute-start | bytes 165896 | tf_op jit(solution)/shard_map/ppermute | solution.py:33
  11.5 0.7 broadcast_in_dim.33
  12.2 6.0 %all-to-all-start = ((bf16[4,24,1152]{2,1,0:T(8,128)(2,1)}), bf16[4,24,1152]{2,1,0:T(8,128)(2,1)S(1)}, u32[]{:S(2)}, u32[]{:S(2)}) async-start(bf16[4,24,1152]{2,1,0:T(8,128)(2,1)} %broadcast_in_dim.33), calls=%async_computation | async-start | bytes 442368 | tf_op jit(solution)/shard_map/all_to_all | solution.py:39
  18.2 0.1 stack.194
  18.3 0.1 add_select_fusion
  18.4 0.1 stack.211
  18.5 0.1 add_select_fusion.1
  19.9 0.1 select_n.42.col_ref
  20.0 0.2 select_n.43.row_ref
  20.2 5.4 %all-to-all-done = bf16[4,24,1152]{2,1,0:T(8,128)(2,1)S(1)} async-done(((bf16[4,24,1152]{2,1,0:T(8,128)(2,1)}), bf16[4,24,1152]{2,1,0:T(8,128)(2,1)S(1)}, u32[]{:S(2)}, u32[]{:S(2)}) %all-to-all-start) | async-done | bytes 221216 | tf_op jit(solution)/shard_map/all_to_all | solution.py:39
  25.6 1.0 broadcast_in_dim.35
  26.6 4.5 %all-to-all-start.1 = ((bf16[4,96,1152]{2,1,0:T(8,128)(2,1)}), bf16[4,96,1152]{2,1,0:T(8,128)(2,1)S(1)}, u32[]{:S(2)}, u32[]{:S(2)}) async-start(bf16[4,96,1152]{2,1,0:T(8,128)(2,1)} %broadcast_in_dim.35), calls=%async_computation.1 | async-start | bytes 1769472 | tf_op jit(solution)/shard_map/all_to_all | solution.py:39
  31.1 0.0 collective-permute-done.1
  31.1 5.0 %collective-permute-start.2 = (bf16[48,1152]{1,0:T(8,128)(2,1)S(1)}, bf16[48,1152]{1,0:T(8,128)(2,1)S(1)}, u32[]{:S(2)}, u32[]{:S(2)}) collective-permute-start(bf16[48,1152]{1,0:T(8,128)(2,1)S(1)} %pad_maximum_fusion.3), channel_id=1, source_target_pairs={{0,384},{1,129},{128,256},{129,1},{256,128},{257,385},{384,0},{385... | collective-permute-start | bytes 331784 | tf_op jit(solution)/shard_map/ppermute | solution.py:33
  36.1 0.1 pad_maximum_fusion.4.scal_ref
  36.2 7.6 %collective-permute-done.2 = bf16[48,1152]{1,0:T(8,128)(2,1)S(1)} collective-permute-done((bf16[48,1152]{1,0:T(8,128)(2,1)S(1)}, bf16[48,1152]{1,0:T(8,128)(2,1)S(1)}, u32[]{:S(2)}, u32[]{:S(2)}) %collective-permute-start.2) | collective-permute-done | bytes 110624 | tf_op jit(solution)/shard_map/ppermute | solution.py:33
  43.8 3.1 %collective-permute-start.3 = (bf16[96,1152]{1,0:T(8,128)(2,1)S(1)}, bf16[96,1152]{1,0:T(8,128)(2,1)S(1)}, u32[]{:S(2)}, u32[]{:S(2)}) collective-permute-start(bf16[96,1152]{1,0:T(8,128)(2,1)S(1)} %pad_maximum_fusion.2), channel_id=1, source_target_pairs={{0,32},{1,97},{32,0},{33,65},{64,96},{65,33},{96,64},{97,1},{2,34}... | collective-permute-start | bytes 663560 | tf_op jit(solution)/shard_map/ppermute | solution.py:33
  47.0 0.0 all-to-all-done.1
  47.0 1.9 %collective-permute-start = (bf16[384,1152]{1,0:T(8,128)(2,1)S(1)}, bf16[384,1152]{1,0:T(8,128)(2,1)S(1)}, u32[]{:S(2)}, u32[]{:S(2)}) collective-permute-start(bf16[384,1152]{1,0:T(8,128)(2,1)S(1)} %bitcast.57), channel_id=1, source_target_pairs={{0,1},{1,0},{2,3},{3,2},{4,5},{5,4},{6,7},{7,6},{8,9},{9,8},{10,11... | collective-permute-start | bytes 2654216 | tf_op jit(solution)/shard_map/ppermute | solution.py:32
  48.9 2.8 %collective-permute-done.3 = bf16[96,1152]{1,0:T(8,128)(2,1)S(1)} collective-permute-done((bf16[96,1152]{1,0:T(8,128)(2,1)S(1)}, bf16[96,1152]{1,0:T(8,128)(2,1)S(1)}, u32[]{:S(2)}, u32[]{:S(2)}) %collective-permute-start.3) | collective-permute-done | bytes 221216 | tf_op jit(solution)/shard_map/ppermute | solution.py:33
  51.7 2.4 %collective-permute-start.4 = (bf16[192,1152]{1,0:T(8,128)(2,1)S(1)}, bf16[192,1152]{1,0:T(8,128)(2,1)S(1)}, u32[]{:S(2)}, u32[]{:S(2)}) collective-permute-start(bf16[192,1152]{1,0:T(8,128)(2,1)S(1)} %pad_maximum_fusion.1), channel_id=1, source_target_pairs={{0,96},{1,33},{32,64},{33,1},{64,32},{65,97},{96,0},{97,65},{2,98}... | collective-permute-start | bytes 1327112 | tf_op jit(solution)/shard_map/ppermute | solution.py:33
  54.2 7.7 %collective-permute-done.4 = bf16[192,1152]{1,0:T(8,128)(2,1)S(1)} collective-permute-done((bf16[192,1152]{1,0:T(8,128)(2,1)S(1)}, bf16[192,1152]{1,0:T(8,128)(2,1)S(1)}, u32[]{:S(2)}, u32[]{:S(2)}) %collective-permute-start.4) | collective-permute-done | bytes 442400 | tf_op jit(solution)/shard_map/ppermute | solution.py:33
  61.9 0.0 collective-permute-done
  61.9 0.1 pad_maximum_fusion.img_ref
  62.1 3.9 %pairs.1 = (bf16[768,1152]{1,0:T(8,128)(2,1)S(1)}, bf16[384,1152]{1,0:T(8,128)(2,1)S(1)}) custom-call(f32[2]{0:T(128)S(1)} %pad_maximum_fusion.4.scal_ref, bf16[768,1152]{1,0:T(8,128)(2,1)S(1)} %pad_maximum_fusion.img_ref, bf16[384,1152]{1,0:T(8,128)(2,1)S(1)} %constant_dynamic-update-slice_fusion.txt_ref, s32[768,1]{1,0:T(8,128)S(1)} %select_n.43.row_ref, ...), custom_call_target="tpu_custom_call" | custom-call | tf_op jit(solution)/shard_map/pairs/pallas_call | solution.py:154
  66.0 2.4 %collective-permute-start.6 = (bf16[192,1152]{1,0:T(8,128)(2,1)S(1)}, bf16[192,1152]{1,0:T(8,128)(2,1)S(1)}, u32[]{:S(2)}, u32[]{:S(2)}) collective-permute-start(bf16[192,1152]{1,0:T(8,128)(2,1)S(1)} %slice.65), channel_id=1, source_target_pairs={{0,96},{1,33},{32,64},{33,1},{64,32},{65,97},{96,0},{97,65},{2,98}... | collective-permute-start | bytes 1327112 | tf_op jit(solution)/shard_map/ppermute | solution.py:33
  68.5 0.1 slice.55
  68.5 1.9 %collective-permute-start.5 = (bf16[384,1152]{1,0:T(8,128)(2,1)S(1)}, bf16[384,1152]{1,0:T(8,128)(2,1)S(1)}, u32[]{:S(2)}, u32[]{:S(2)}) collective-permute-start(bf16[384,1152]{1,0:T(8,128)(2,1)S(1)} %slice.55), channel_id=1, source_target_pairs={{0,1},{1,0},{2,3},{3,2},{4,5},{5,4},{6,7},{7,6},{8,9},{9,8},{10,11... | collective-permute-start | bytes 2654216 | tf_op jit(solution)/shard_map/ppermute | solution.py:32
  70.5 5.7 %collective-permute-done.6 = bf16[192,1152]{1,0:T(8,128)(2,1)S(1)} collective-permute-done((bf16[192,1152]{1,0:T(8,128)(2,1)S(1)}, bf16[192,1152]{1,0:T(8,128)(2,1)S(1)}, u32[]{:S(2)}, u32[]{:S(2)}) %collective-permute-start.6) | collective-permute-done | bytes 442400 | tf_op jit(solution)/shard_map/ppermute | solution.py:33
  76.2 0.1 add_convert_fusion.1
  76.4 6.1 %collective-permute-start.7 = (bf16[96,1152]{1,0:T(8,128)(2,1)S(1)}, bf16[96,1152]{1,0:T(8,128)(2,1)S(1)}, u32[]{:S(2)}, u32[]{:S(2)}) collective-permute-start(bf16[96,1152]{1,0:T(8,128)(2,1)S(1)} %slice.81), channel_id=1, source_target_pairs={{0,32},{1,97},{32,0},{33,65},{64,96},{65,33},{96,64},{97,1},{2,34}... | collective-permute-start | bytes 663560 | tf_op jit(solution)/shard_map/ppermute | solution.py:33
  82.5 0.0 collective-permute-done.5
  82.5 1.1 add_convert_fusion
  83.6 4.5 %all-to-all-start.2 = ((bf16[4,96,1152]{2,1,0:T(8,128)(2,1)}), bf16[4,96,1152]{2,1,0:T(8,128)(2,1)S(1)}, u32[]{:S(2)}, u32[]{:S(2)}) async-start(bf16[4,96,1152]{2,1,0:T(8,128)(2,1)} %bitcast.52), calls=%async_computation.2 | async-start | bytes 1769472 | tf_op jit(solution)/shard_map/all_to_all | solution.py:51
  88.2 0.0 collective-permute-done.7
  88.2 0.1 add_convert_fusion.2
  88.3 4.6 %collective-permute-start.8 = (bf16[48,1152]{1,0:T(8,128)(2,1)S(1)}, bf16[48,1152]{1,0:T(8,128)(2,1)S(1)}, u32[]{:S(2)}, u32[]{:S(2)}) collective-permute-start(bf16[48,1152]{1,0:T(8,128)(2,1)S(1)} %slice.83), channel_id=1, source_target_pairs={{0,384},{1,129},{128,256},{129,1},{256,128},{257,385},{384,0},{385... | collective-permute-start | bytes 331784 | tf_op jit(solution)/shard_map/ppermute | solution.py:33
  92.9 5.3 %all-to-all-done.2 = bf16[4,96,1152]{2,1,0:T(8,128)(2,1)S(1)} async-done(((bf16[4,96,1152]{2,1,0:T(8,128)(2,1)}), bf16[4,96,1152]{2,1,0:T(8,128)(2,1)S(1)}, u32[]{:S(2)}, u32[]{:S(2)}) %all-to-all-start.2) | async-done | bytes 884768 | tf_op jit(solution)/shard_map/all_to_all | solution.py:51
  98.2 0.8 add_convert_fusion.3
  99.0 5.2 %all-to-all-start.3 = ((bf16[4,24,1152]{2,1,0:T(8,128)(2,1)}), bf16[4,24,1152]{2,1,0:T(8,128)(2,1)S(1)}, u32[]{:S(2)}, u32[]{:S(2)}) async-start(bf16[4,24,1152]{2,1,0:T(8,128)(2,1)} %bitcast.53), calls=%async_computation.3 | async-start | bytes 442368 | tf_op jit(solution)/shard_map/all_to_all | solution.py:51
  104.2 2.1 %collective-permute-start.9 = (bf16[24,1152]{1,0:T(8,128)(2,1)S(1)}, bf16[24,1152]{1,0:T(8,128)(2,1)S(1)}, u32[]{:S(2)}, u32[]{:S(2)}) collective-permute-start(bf16[24,1152]{1,0:T(8,128)(2,1)S(1)} %slice.85), channel_id=1, source_target_pairs={{0,128},{1,385},{128,0},{129,257},{256,384},{257,129},{384,256},{3... | collective-permute-start | bytes 165896 | tf_op jit(solution)/shard_map/ppermute | solution.py:33
  106.3 7.8 %collective-permute-done.9 = bf16[24,1152]{1,0:T(8,128)(2,1)S(1)} collective-permute-done((bf16[24,1152]{1,0:T(8,128)(2,1)S(1)}, bf16[24,1152]{1,0:T(8,128)(2,1)S(1)}, u32[]{:S(2)}, u32[]{:S(2)}) %collective-permute-start.9) | collective-permute-done | bytes 55328 | tf_op jit(solution)/shard_map/ppermute | solution.py:33
  114.2 0.0 all-to-all-done.3
  114.3 0.9 back.1
  (24 shorter events, 0.4 us)
Async XLA Ops:
  0.6 0.8 copy-start
  1.4 0.8 copy-start.2
  2.4 28.7 %collective-permute-start.1 = (bf16[24,1152]{1,0:T(8,128)(2,1)S(1)}, bf16[24,1152]{1,0:T(8,128)(2,1)S(1)}, u32[]{:S(2)}, u32[]{:S(2)}) collective-permute-start(bf16[24,1152]{1,0:T(8,128)(2,1)S(1)} %get-tuple-element.7), channel_id=1, source_target_pairs={{0,128},{1,385},{128,0},{129,257},{256,384},{257,129},{384,256},{3... | collective-permute-start | bytes 165896 | tf_op jit(solution)/shard_map/ppermute | solution.py:33
  12.2 13.4 %all-to-all-start = ((bf16[4,24,1152]{2,1,0:T(8,128)(2,1)}), bf16[4,24,1152]{2,1,0:T(8,128)(2,1)S(1)}, u32[]{:S(2)}, u32[]{:S(2)}) async-start(bf16[4,24,1152]{2,1,0:T(8,128)(2,1)} %broadcast_in_dim.33), calls=%async_computation | async-start | bytes 442368 | tf_op jit(solution)/shard_map/all_to_all | solution.py:39
  26.6 20.3 %all-to-all-start.1 = ((bf16[4,96,1152]{2,1,0:T(8,128)(2,1)}), bf16[4,96,1152]{2,1,0:T(8,128)(2,1)S(1)}, u32[]{:S(2)}, u32[]{:S(2)}) async-start(bf16[4,96,1152]{2,1,0:T(8,128)(2,1)} %broadcast_in_dim.35), calls=%async_computation.1 | async-start | bytes 1769472 | tf_op jit(solution)/shard_map/all_to_all | solution.py:39
  31.1 12.7 %collective-permute-start.2 = (bf16[48,1152]{1,0:T(8,128)(2,1)S(1)}, bf16[48,1152]{1,0:T(8,128)(2,1)S(1)}, u32[]{:S(2)}, u32[]{:S(2)}) collective-permute-start(bf16[48,1152]{1,0:T(8,128)(2,1)S(1)} %pad_maximum_fusion.3), channel_id=1, source_target_pairs={{0,384},{1,129},{128,256},{129,1},{256,128},{257,385},{384,0},{385... | collective-permute-start | bytes 331784 | tf_op jit(solution)/shard_map/ppermute | solution.py:33
  43.8 7.8 %collective-permute-start.3 = (bf16[96,1152]{1,0:T(8,128)(2,1)S(1)}, bf16[96,1152]{1,0:T(8,128)(2,1)S(1)}, u32[]{:S(2)}, u32[]{:S(2)}) collective-permute-start(bf16[96,1152]{1,0:T(8,128)(2,1)S(1)} %pad_maximum_fusion.2), channel_id=1, source_target_pairs={{0,32},{1,97},{32,0},{33,65},{64,96},{65,33},{96,64},{97,1},{2,34}... | collective-permute-start | bytes 663560 | tf_op jit(solution)/shard_map/ppermute | solution.py:33
  47.0 15.0 %collective-permute-start = (bf16[384,1152]{1,0:T(8,128)(2,1)S(1)}, bf16[384,1152]{1,0:T(8,128)(2,1)S(1)}, u32[]{:S(2)}, u32[]{:S(2)}) collective-permute-start(bf16[384,1152]{1,0:T(8,128)(2,1)S(1)} %bitcast.57), channel_id=1, source_target_pairs={{0,1},{1,0},{2,3},{3,2},{4,5},{5,4},{6,7},{7,6},{8,9},{9,8},{10,11... | collective-permute-start | bytes 2654216 | tf_op jit(solution)/shard_map/ppermute | solution.py:32
  51.7 10.2 %collective-permute-start.4 = (bf16[192,1152]{1,0:T(8,128)(2,1)S(1)}, bf16[192,1152]{1,0:T(8,128)(2,1)S(1)}, u32[]{:S(2)}, u32[]{:S(2)}) collective-permute-start(bf16[192,1152]{1,0:T(8,128)(2,1)S(1)} %pad_maximum_fusion.1), channel_id=1, source_target_pairs={{0,96},{1,33},{32,64},{33,1},{64,32},{65,97},{96,0},{97,65},{2,98}... | collective-permute-start | bytes 1327112 | tf_op jit(solution)/shard_map/ppermute | solution.py:33
  66.0 10.2 %collective-permute-start.6 = (bf16[192,1152]{1,0:T(8,128)(2,1)S(1)}, bf16[192,1152]{1,0:T(8,128)(2,1)S(1)}, u32[]{:S(2)}, u32[]{:S(2)}) collective-permute-start(bf16[192,1152]{1,0:T(8,128)(2,1)S(1)} %slice.65), channel_id=1, source_target_pairs={{0,96},{1,33},{32,64},{33,1},{64,32},{65,97},{96,0},{97,65},{2,98}... | collective-permute-start | bytes 1327112 | tf_op jit(solution)/shard_map/ppermute | solution.py:33
  68.5 13.9 %collective-permute-start.5 = (bf16[384,1152]{1,0:T(8,128)(2,1)S(1)}, bf16[384,1152]{1,0:T(8,128)(2,1)S(1)}, u32[]{:S(2)}, u32[]{:S(2)}) collective-permute-start(bf16[384,1152]{1,0:T(8,128)(2,1)S(1)} %slice.55), channel_id=1, source_target_pairs={{0,1},{1,0},{2,3},{3,2},{4,5},{5,4},{6,7},{7,6},{8,9},{9,8},{10,11... | collective-permute-start | bytes 2654216 | tf_op jit(solution)/shard_map/ppermute | solution.py:32
  76.4 11.8 %collective-permute-start.7 = (bf16[96,1152]{1,0:T(8,128)(2,1)S(1)}, bf16[96,1152]{1,0:T(8,128)(2,1)S(1)}, u32[]{:S(2)}, u32[]{:S(2)}) collective-permute-start(bf16[96,1152]{1,0:T(8,128)(2,1)S(1)} %slice.81), channel_id=1, source_target_pairs={{0,32},{1,97},{32,0},{33,65},{64,96},{65,33},{96,64},{97,1},{2,34}... | collective-permute-start | bytes 663560 | tf_op jit(solution)/shard_map/ppermute | solution.py:33
  83.6 14.5 %all-to-all-start.2 = ((bf16[4,96,1152]{2,1,0:T(8,128)(2,1)}), bf16[4,96,1152]{2,1,0:T(8,128)(2,1)S(1)}, u32[]{:S(2)}, u32[]{:S(2)}) async-start(bf16[4,96,1152]{2,1,0:T(8,128)(2,1)} %bitcast.52), calls=%async_computation.2 | async-start | bytes 1769472 | tf_op jit(solution)/shard_map/all_to_all | solution.py:51
  88.2 26.1 %copy-start.1 = (bf16[22,1152]{1,0:T(8,128)(2,1)S(1)}, bf16[22,1152]{1,0:T(8,128)(2,1)}, u32[]{:S(2)}) copy-start(bf16[22,1152]{1,0:T(8,128)(2,1)} %img_ref.3) | copy-start | bytes 152068
  88.2 26.1 %copy-start.3 = (bf16[22,1152]{1,0:T(8,128)(2,1)S(1)}, bf16[22,1152]{1,0:T(8,128)(2,1)}, u32[]{:S(2)}) copy-start(bf16[22,1152]{1,0:T(8,128)(2,1)} %txt_ref.3) | copy-start | bytes 152068
  88.3 15.9 %collective-permute-start.8 = (bf16[48,1152]{1,0:T(8,128)(2,1)S(1)}, bf16[48,1152]{1,0:T(8,128)(2,1)S(1)}, u32[]{:S(2)}, u32[]{:S(2)}) collective-permute-start(bf16[48,1152]{1,0:T(8,128)(2,1)S(1)} %slice.83), channel_id=1, source_target_pairs={{0,384},{1,129},{128,256},{129,1},{256,128},{257,385},{384,0},{385... | collective-permute-start | bytes 331784 | tf_op jit(solution)/shard_map/ppermute | solution.py:33
  99.0 15.2 %all-to-all-start.3 = ((bf16[4,24,1152]{2,1,0:T(8,128)(2,1)}), bf16[4,24,1152]{2,1,0:T(8,128)(2,1)S(1)}, u32[]{:S(2)}, u32[]{:S(2)}) async-start(bf16[4,24,1152]{2,1,0:T(8,128)(2,1)} %bitcast.53), calls=%async_computation.3 | async-start | bytes 442368 | tf_op jit(solution)/shard_map/all_to_all | solution.py:51
  104.2 10.0 %collective-permute-start.9 = (bf16[24,1152]{1,0:T(8,128)(2,1)S(1)}, bf16[24,1152]{1,0:T(8,128)(2,1)S(1)}, u32[]{:S(2)}, u32[]{:S(2)}) collective-permute-start(bf16[24,1152]{1,0:T(8,128)(2,1)S(1)} %slice.85), channel_id=1, source_target_pairs={{0,128},{1,385},{128,0},{129,257},{256,384},{257,129},{384,256},{3... | collective-permute-start | bytes 165896 | tf_op jit(solution)/shard_map/ppermute | solution.py:33

commit v3 on v0

v3 whole, which is shorter than its diff:
```python
import functools

import jax
import jax.numpy as jnp
from jax import lax
from jax.experimental import pallas as pl
from jax.experimental.pallas import tpu as pltpu
from jax.sharding import Mesh
from jax.sharding import PartitionSpec as P

D = 1152
ROWS = 22
PAD = 24
AXES = ("zh", "x", "zl", "y", "core")
SIZES = (4, 4, 4, 4, 2)
VMEM = 48 * 1024 * 1024
def at_z(move):
    return lambda p: {**p, "z": move(p["z"])}


def at_y(mask):
    return lambda p: {**p, "y": p["y"] ^ mask}


def at_x(mask):
    return lambda p: {**p, "x": p["x"] ^ mask}


FAR = (at_z(lambda z: z ^ 4), at_z(lambda z: z ^ 12))
NEAR = (at_z(lambda z: z ^ 1), at_z(lambda z: z ^ 2))
BOTH = (at_z(lambda z: z ^ 5), at_z(lambda z: z ^ 14))
LAST = tuple((at_y(m), at_x(m)) for m in (1, 3, 2))
ROUNDS = ((FAR, NEAR, BOTH), LAST)
BACK = ((FAR,), (NEAR,))


def flat(zh, x, zl, y, core):
    return (((zh * 4 + x) * 4 + zl) * 4 + y) * 2 + core


def fetch(value, sources, back=False):
    pairs = []
    for z in range(16):
        for x in range(4):
            for y in range(4):
                for c in range(2):
                    at = {"x": x, "y": y, "z": z}
                    pairs.append(tuple(flat(p["z"] >> 2, p["x"], p["z"] & 3, p["y"], c) for p in (sources[c](at), at)))
    return lax.ppermute(value, AXES, [(b, a) for a, b in pairs] if back else pairs)


def core_swap(value):
    return lax.ppermute(value, "core", [(0, 1), (1, 0)])


def add(parts):
    return sum(p.astype(jnp.float32) for p in parts).astype(jnp.bfloat16)


def origins(at, core):
    found = [at]
    for sources in reversed(ROUNDS):
        found = [q for p in found for q in [p] + [s[core](p) for s in sources]]
    return [{**p, "core": c} for p in found for c in (core, 1 - core)]


def unit_of(ref):
    wide = ref[...].astype(jnp.float32)
    length = jnp.sqrt(jnp.sum(wide * wide, axis=1, keepdims=True) + 1e-06)
    return wide / length, length


def unit_kernel(core_ref, img_ref, txt_ref, keep_ref, send_ref):
    pad = jnp.zeros((PAD - ROWS, D), jnp.float32)
    img, txt = (jnp.concatenate([unit_of(ref)[0], pad]).astype(jnp.bfloat16) for ref in (img_ref, txt_ref))

    @pl.when(core_ref[0] == 0)
    def _():
        keep_ref[...] = img
        send_ref[...] = txt

    @pl.when(core_ref[0] == 1)
    def _():
        keep_ref[...] = txt
        send_ref[...] = img


def row_ids(ids_ref, first, count):
    within = lax.broadcasted_iota(jnp.int32, (PAD, 1), 0)
    return jnp.concatenate([jnp.where(within < ROWS, ids_ref[first + k] * ROWS + within, -1) for k in range(count)])


def column_ids(ids_ref, first, count):
    at = lax.broadcasted_iota(jnp.int32, (1, count * PAD), 1)
    found = jnp.full(at.shape, -2, jnp.int32)
    for k in range(count):
        within = at - k * PAD
        found = jnp.where((within >= 0) & (within < ROWS), ids_ref[first + k] * ROWS + within, found)
    return found


def pair_kernel(scal_ref, mine_ids, their_ids, me_ref, ml_ref, re_ref, rl_ref, *outs):
    scale, bias = scal_ref[0], scal_ref[1]
    half = me_ref.shape[0] // 2
    slots = me_ref.shape[0] // PAD
    theirs = [(ref, column_ids(their_ids, k * slots, slots)) for k, ref in enumerate((re_ref, rl_ref))]
    for k, mine_ref in enumerate((me_ref, ml_ref)):
        rows = row_ids(mine_ids, k * slots, slots)
        weights = []
        for their_ref, columns in theirs:
            s = lax.dot_general(mine_ref[...], their_ref[...], (((1,), (1,)), ((), ())), preferred_element_type=jnp.float32)
            z = scale * s + bias
            same = rows == columns
            d = 1.0 + jnp.exp(jnp.where(same, z, -z))
            r = pl.reciprocal(d, approx=True)
            r = r * (2.0 - d * r)
            weights.append(jnp.where(same, -r, r).astype(jnp.bfloat16))
        for t in range(3):
            cols = pl.ds(t * 384, 384)
            g = sum(jnp.dot(w, ref[:, cols], preferred_element_type=jnp.float32) for w, (ref, _) in zip(weights, theirs))
            g = (scale * g).astype(jnp.bfloat16)
            outs[2 * k][:, cols] = g[:half]
            outs[2 * k + 1][:, cols] = g[half:]


def back_kernel(core_ref, img_ref, txt_ref, *refs):
    *mine, recv_ref, img_out, txt_out = refs

    def work(own_src, own_out, other_src, other_out):
        own = sum(ref[...].astype(jnp.float32) for ref in mine)
        for src, g, dst in ((own_src, own, own_out), (other_src, recv_ref[...].astype(jnp.float32), other_out)):
            unit, length = unit_of(src)
            g = g[:ROWS]
            along = jnp.sum(unit * g, axis=1, keepdims=True)
            dst[...] = (g - unit * along) / length

    pl.when(core_ref[0] == 0)(lambda: work(img_ref, img_out, txt_ref, txt_out))
    pl.when(core_ref[0] == 1)(lambda: work(txt_ref, txt_out, img_ref, img_out))


PARAMS = pltpu.CompilerParams(vmem_limit_bytes=VMEM)


def call(kernel, name, out_shape, scalars, args, flops=0):
    return pl.pallas_call(
        kernel,
        out_shape=out_shape,
        in_specs=[pl.BlockSpec(memory_space=pltpu.SMEM)] * len(scalars) + [pl.BlockSpec(memory_space=pltpu.VMEM)] * len(args),
        out_specs=tuple(pl.BlockSpec(memory_space=pltpu.VMEM) for _ in out_shape),
        compiler_params=PARAMS,
        cost_estimate=pl.CostEstimate(flops=flops, bytes_accessed=1 << 20, transcendentals=0),
        name=name,
    )(*scalars, *args)


def on_device(images, texts, logarithmic_scale, similarity_bias):
    core = lax.axis_index("core")
    at = {"x": lax.axis_index("x"), "y": lax.axis_index("y"), "z": lax.axis_index("zh") * 4 + lax.axis_index("zl")}
    cores = core.reshape((1,))
    block = jax.ShapeDtypeStruct((PAD, D), jnp.bfloat16)
    keep, send = call(unit_kernel, "unit", (block, block), [cores], [images, texts])
    held = jnp.concatenate([keep, core_swap(send)])
    for sources in ROUNDS[:-1]:
        held = jnp.concatenate([held] + [fetch(held, s) for s in sources])
    first, second, third = [fetch(held, s) for s in ROUNDS[-1]]
    me = jnp.concatenate([held, first])
    ml = jnp.concatenate([second, third])
    re, rl = core_swap(me), core_swap(ml)

    img_ids = jnp.stack([((p["z"] >> 2) * 4 + p["x"]) * 32 + ((p["z"] & 3) * 4 + p["y"]) * 2 + p["core"] for p in origins(at, 0)])
    txt_ids = jnp.stack([(((p["z"] & 3) * 4 + p["y"]) * 2 + p["core"]) * 16 + (p["z"] >> 2) * 4 + p["x"] for p in origins(at, 1)])
    mine_ids, their_ids = jnp.where(core == 0, img_ids, txt_ids), jnp.where(core == 0, txt_ids, img_ids)
    scal = jnp.stack([jnp.exp(logarithmic_scale), similarity_bias])
    n = me.shape[0]
    piece = jax.ShapeDtypeStruct((n // 2, D), jnp.bfloat16)
    keep, *sends = call(pair_kernel, "pairs", (piece,) * 4, [scal, mine_ids, their_ids], [me, ml, re, rl], 16 * n * n * D)
    parts = [keep] + [fetch(p, s, True) for p, s in zip(sends, ROUNDS[-1])]
    for sources in reversed(BACK):
        n = parts[0].shape[0] // (len(sources) + 1)
        sends = [add([p[k * n : (k + 1) * n] for p in parts]) for k in range(1, len(sources) + 1)]
        parts = [p[:n] for p in parts] + [fetch(p, s, True) for p, s in zip(sends, sources)]
    recv = core_swap(add([p[PAD:] for p in parts]))
    wide = jax.ShapeDtypeStruct((ROWS, D), jnp.float32)
    return call(back_kernel, "back", (wide, wide), [cores], [images, texts] + [p[:PAD] for p in parts] + [recv])


def solution(mesh):
    fine = Mesh(mesh.devices.reshape(SIZES), AXES)
    return jax.shard_map(
        on_device,
        mesh=fine,
        in_specs=(P(AXES, None), P(("zl", "y", "core", "zh", "x"), None), P(), P()),
        out_specs=(P(AXES, None), P(("zl", "y", "core", "zh", "x"), None)),
        check_vma=False,
    )
```

time: 328 us -> 107 us (0.33)
  blocking collectives: 236 us -> 0 us
  waiting for transfers between devices: 2.48 us -> 33.4 us
  between operations: 16.9 us -> 2.35 us
  starting transfers between devices: 50.2 us -> 61.8 us
  local copies, waits for them, and re-layouts: 8.74 us -> 2.18 us
  Pallas kernels: 0 us -> 6.46 us
  matrix products: 6.13 us -> 0 us
  other arithmetic: 6.21 us -> 0.31 us
    unnamed x2 -> x0, blocking collectives: 168 us -> none
    all_gather x1 -> x0, blocking collectives: 68.2 us -> none  [on_device(): lax.all_gather(txt_unit.astype(jnp.bfloat16), 'row', axis=0, tiled=True)]
    ppermute x0 -> x15, starting transfers between devices: none -> 61.8 us  [the longest x11 39.2 us: fetch(): lax.ppermute(value, AXES, [(b, a) for a, b in pairs] if back else pairs)]
    unnamed x15 -> x0, starting transfers between devices: 50.1 us -> none
    ppermute x0 -> x15, waiting for transfers between devices: none -> 33.4 us  [the longest x11 31.4 us: fetch(): lax.ppermute(value, AXES, [(b, a) for a, b in pairs] if back else pairs)]
    unnamed x12 -> x13, local copies, waits for them, and re-layouts: 8.74 us -> 1.8 us
    pallas_call x0 -> x3, Pallas kernels: none -> 6.46 us  [call(): pl.pallas_call(kernel, out_shape=out_shape, in_specs=[pl.BlockSpec(memory...]
    dot_general x3 -> x0, matrix products: 6.13 us -> none  [the longest x1 2.09 us: pairwise_factors(): lax.dot_general(selected_entries, column_ranges, (((1,), (1,)), ((), ()))...]
  transfers between devices with their start and end apart: 16 -> 15, of which waited for: 2 -> 9; matrix products, arithmetic and copies ran while one was open for 32% -> 0% of each run, Pallas kernels for 0% -> 0%
where the time goes in v3:
time: 107 us; the launch traced here: 106 us
  starting transfers between devices  61.8 us (58%)
  waiting for transfers between devices  33.4 us (31%)
  Pallas kernels  6.46 us (6%)
  between operations  2.35 us (2%)
  local copies, waits for them, and re-layouts  2.18 us (2%)
    ppermute x11, starting transfers between devices, fetch(): lax.ppermute(value, AXES, [(b, a) for a, b in pairs] if back else pairs)  39.2 us
    ppermute x11, waiting for transfers between devices, fetch(): lax.ppermute(value, AXES, [(b, a) for a, b in pairs] if back else pairs)  31.4 us
    ppermute x4, starting transfers between devices, core_swap(): return lax.ppermute(value, 'core', [(0, 1), (1, 0)])  22.6 us
    pallas_call x3, Pallas kernels, call(): pl.pallas_call(kernel, out_shape=out_shape, in_specs=[pl.BlockSpec(memory...  6.46 us
  transfers between devices with their start and end apart: 15, of which 9 were waited for; matrix products, arithmetic and copies ran while one was open for 0% of the time, Pallas kernels for 0%

profile of v3, /device:TPU:1, one launch (start us, length us, event | category | flops | bytes accessed | tf_op | source)
XLA Modules:
  0.0 106.4 jit_solution(10251948845354382527)
XLA Ops:
  0.6 0.0 copy-start
  0.6 0.8 copy-done
  1.5 0.0 copy-start.2
  1.5 0.8 copy-done.2
  2.3 0.1 unit.1
  2.4 8.8 %collective-permute-start = (bf16[24,1152]{1,0:T(8,128)(2,1)S(1)}, bf16[24,1152]{1,0:T(8,128)(2,1)S(1)}, u32[]{:S(2)}, u32[]{:S(2)}) collective-permute-start(bf16[24,1152]{1,0:T(8,128)(2,1)S(1)} %get-tuple-element.9), channel_id=1, source_target_pairs={{0,1},{1,0},{2,3},{3,2},{4,5},{5,4},{6,7},{7,6},{8,9},{9,8},{10,11... | collective-permute-start | bytes 165896 | tf_op jit(solution)/shard_map/ppermute | solution.py:53
  11.2 0.8 collective-permute-done
  12.1 7.1 %collective-permute-start.1 = (bf16[48,1152]{1,0:T(8,128)(2,1)S(1)}, bf16[48,1152]{1,0:T(8,128)(2,1)S(1)}, u32[]{:S(2)}, u32[]{:S(2)}) collective-permute-start(bf16[48,1152]{1,0:T(8,128)(2,1)S(1)} %get-tuple-element.22), channel_id=1, source_target_pairs={{128,0},{385,1},{130,2},{387,3},{132,4},{389,5},{134,6},{391,7},{1... | collective-permute-start | bytes 331784 | tf_op jit(solution)/shard_map/ppermute | solution.py:49
  19.2 1.9 %collective-permute-start.3 = (bf16[48,1152]{1,0:T(8,128)(2,1)S(1)}, bf16[48,1152]{1,0:T(8,128)(2,1)S(1)}, u32[]{:S(2)}, u32[]{:S(2)}) collective-permute-start(bf16[48,1152]{1,0:T(8,128)(2,1)S(1)} %get-tuple-element.22), channel_id=1, source_target_pairs={{136,0},{401,1},{138,2},{403,3},{140,4},{405,5},{142,6},{407,7},{1... | collective-permute-start | bytes 331784 | tf_op jit(solution)/shard_map/ppermute | solution.py:49
  21.1 4.2 %collective-permute-start.2 = (bf16[48,1152]{1,0:T(8,128)(2,1)S(1)}, bf16[48,1152]{1,0:T(8,128)(2,1)S(1)}, u32[]{:S(2)}, u32[]{:S(2)}) collective-permute-start(bf16[48,1152]{1,0:T(8,128)(2,1)S(1)} %get-tuple-element.22), channel_id=1, source_target_pairs={{8,0},{17,1},{10,2},{19,3},{12,4},{21,5},{14,6},{23,7},{40,32},{49... | collective-permute-start | bytes 331784 | tf_op jit(solution)/shard_map/ppermute | solution.py:49
  25.3 0.0 collective-permute-done.1
  25.3 6.7 %collective-permute-done.2 = bf16[48,1152]{1,0:T(8,128)(2,1)S(1)} collective-permute-done((bf16[48,1152]{1,0:T(8,128)(2,1)S(1)}, bf16[48,1152]{1,0:T(8,128)(2,1)S(1)}, u32[]{:S(2)}, u32[]{:S(2)}) %collective-permute-start.2) | collective-permute-done | bytes 110624 | tf_op jit(solution)/shard_map/ppermute | solution.py:49
  32.0 0.0 collective-permute-done.3
  32.1 1.9 %collective-permute-start.4 = (bf16[192,1152]{1,0:T(8,128)(2,1)S(1)}, bf16[192,1152]{1,0:T(8,128)(2,1)S(1)}, u32[]{:S(2)}, u32[]{:S(2)}) collective-permute-start(bf16[192,1152]{1,0:T(8,128)(2,1)S(1)} %get-tuple-element.14), channel_id=1, source_target_pairs={{2,0},{33,1},{0,2},{35,3},{6,4},{37,5},{4,6},{39,7},{34,32},{1,33}... | collective-permute-start | bytes 1327112 | tf_op jit(solution)/shard_map/ppermute | solution.py:49
  34.0 3.4 %collective-permute-start.5 = (bf16[192,1152]{1,0:T(8,128)(2,1)S(1)}, bf16[192,1152]{1,0:T(8,128)(2,1)S(1)}, u32[]{:S(2)}, u32[]{:S(2)}) collective-permute-start(bf16[192,1152]{1,0:T(8,128)(2,1)S(1)} %get-tuple-element.14), channel_id=1, source_target_pairs={{6,0},{97,1},{4,2},{99,3},{2,4},{101,5},{0,6},{103,7},{38,32},{65,... | collective-permute-start | bytes 1327112 | tf_op jit(solution)/shard_map/ppermute | solution.py:49
  37.4 3.7 %collective-permute-start.6 = (bf16[192,1152]{1,0:T(8,128)(2,1)S(1)}, bf16[192,1152]{1,0:T(8,128)(2,1)S(1)}, u32[]{:S(2)}, u32[]{:S(2)}) collective-permute-start(bf16[192,1152]{1,0:T(8,128)(2,1)S(1)} %get-tuple-element.14), channel_id=1, source_target_pairs={{4,0},{65,1},{6,2},{67,3},{0,4},{69,5},{2,6},{71,7},{36,32},{97,33... | collective-permute-start | bytes 1327112 | tf_op jit(solution)/shard_map/ppermute | solution.py:49
  41.1 0.3 collective-permute-done.4
  41.5 3.6 %collective-permute-start.7 = (bf16[384,1152]{1,0:T(8,128)(2,1)S(1)}, bf16[384,1152]{1,0:T(8,128)(2,1)S(1)}, u32[]{:S(2)}, u32[]{:S(2)}) collective-permute-start(bf16[384,1152]{1,0:T(8,128)(2,1)S(1)} %constant_dynamic-update-slice_fusion.7.me_ref), channel_id=1, source_target_pairs={{0,1},{1,0},{2,3},{3,2},{4,5},{5,4},{6,7},{7,6},{8,9},{9,8},{10,11... | collective-permute-start | bytes 2654216 | tf_op jit(solution)/shard_map/ppermute | solution.py:53
  45.1 4.2 %collective-permute-done.5 = bf16[192,1152]{1,0:T(8,128)(2,1)S(1)} collective-permute-done((bf16[192,1152]{1,0:T(8,128)(2,1)S(1)}, bf16[192,1152]{1,0:T(8,128)(2,1)S(1)}, u32[]{:S(2)}, u32[]{:S(2)}) %collective-permute-start.5) | collective-permute-done | bytes 442400 | tf_op jit(solution)/shard_map/ppermute | solution.py:49
  49.3 0.0 collective-permute-done.6
  49.4 4.3 %collective-permute-start.8 = (bf16[384,1152]{1,0:T(8,128)(2,1)S(1)}, bf16[384,1152]{1,0:T(8,128)(2,1)S(1)}, u32[]{:S(2)}, u32[]{:S(2)}) collective-permute-start(bf16[384,1152]{1,0:T(8,128)(2,1)S(1)} %constant_dynamic-update-slice_fusion.13.ml_ref), channel_id=1, source_target_pairs={{0,1},{1,0},{2,3},{3,2},{4,5},{5,4},{6,7},{7,6},{8,9},{9,8},{10,11... | collective-permute-start | bytes 2654216 | tf_op jit(solution)/shard_map/ppermute | solution.py:53
  55.1 0.1 stack.242
  55.2 0.1 stack.275
  55.4 0.1 pad_maximum_fusion.scal_ref
  55.4 0.0 collective-permute-done.7.re_ref
  55.4 0.3 collective-permute-done.8.rl_ref
  55.7 5.4 %pairs.1 = (bf16[192,1152]{1,0:T(8,128)(2,1)S(1)}, bf16[192,1152]{1,0:T(8,128)(2,1)S(1)}, bf16[192,1152]{1,0:T(8,128)(2,1)S(1)}, bf16[192,1152]{1,0:T(8,128)(2,1)S(1)}) custom-call(f32[2]{0:T(128)S(1)} %pad_maximum_fusion.scal_ref, s32[32]{0:T(128)S(1)} %get-tuple-element.27.mine_ids, s32[32]{0:T(128)S(1)} %get-tuple-element.26.their_ids, ...), custom_call_target="tpu_custom_call" | custom-call | flops 2717908992 | bytes 1048576 | tf_op jit(solution)/shard_map/pairs/pallas_call | solution.py:145
  61.2 3.1 %collective-permute-start.9 = (bf16[192,1152]{1,0:T(8,128)(2,1)S(1)}, bf16[192,1152]{1,0:T(8,128)(2,1)S(1)}, u32[]{:S(2)}, u32[]{:S(2)}) collective-permute-start(bf16[192,1152]{1,0:T(8,128)(2,1)S(1)} %get-tuple-element.11), channel_id=1, source_target_pairs={{0,2},{1,33},{2,0},{3,35},{4,6},{5,37},{6,4},{7,39},{32,34},{33,1}... | collective-permute-start | bytes 1327112 | tf_op jit(solution)/shard_map/ppermute | solution.py:49
  64.3 3.7 %collective-permute-start.10 = (bf16[192,1152]{1,0:T(8,128)(2,1)S(1)}, bf16[192,1152]{1,0:T(8,128)(2,1)S(1)}, u32[]{:S(2)}, u32[]{:S(2)}) collective-permute-start(bf16[192,1152]{1,0:T(8,128)(2,1)S(1)} %get-tuple-element.12), channel_id=1, source_target_pairs={{0,6},{1,97},{2,4},{3,99},{4,2},{5,101},{6,0},{7,103},{32,38},{33,... | collective-permute-start | bytes 1327112 | tf_op jit(solution)/shard_map/ppermute | solution.py:49
  68.0 2.6 %collective-permute-start.11 = (bf16[192,1152]{1,0:T(8,128)(2,1)S(1)}, bf16[192,1152]{1,0:T(8,128)(2,1)S(1)}, u32[]{:S(2)}, u32[]{:S(2)}) collective-permute-start(bf16[192,1152]{1,0:T(8,128)(2,1)S(1)} %get-tuple-element.13), channel_id=1, source_target_pairs={{0,4},{1,65},{2,6},{3,67},{4,0},{5,69},{6,2},{7,71},{32,36},{33,97... | collective-permute-start | bytes 1327112 | tf_op jit(solution)/shard_map/ppermute | solution.py:49
  70.6 0.0 collective-permute-done.9
  70.6 8.9 %collective-permute-done.10 = bf16[192,1152]{1,0:T(8,128)(2,1)S(1)} collective-permute-done((bf16[192,1152]{1,0:T(8,128)(2,1)S(1)}, bf16[192,1152]{1,0:T(8,128)(2,1)S(1)}, u32[]{:S(2)}, u32[]{:S(2)}) %collective-permute-start.10) | collective-permute-done | bytes 442400 | tf_op jit(solution)/shard_map/ppermute | solution.py:49
  79.5 0.0 collective-permute-done.11
  79.5 0.1 add_convert_fusion
  79.6 2.4 %collective-permute-start.12 = (bf16[96,1152]{1,0:T(8,128)(2,1)S(1)}, bf16[96,1152]{1,0:T(8,128)(2,1)S(1)}, u32[]{:S(2)}, u32[]{:S(2)}) collective-permute-start(bf16[96,1152]{1,0:T(8,128)(2,1)S(1)} %add_convert_fusion), channel_id=1, source_target_pairs={{0,8},{1,17},{2,10},{3,19},{4,12},{5,21},{6,14},{7,23},{32,40},{33... | collective-permute-start | bytes 663560 | tf_op jit(solution)/shard_map/ppermute | solution.py:49
  82.1 7.1 %collective-permute-done.12 = bf16[96,1152]{1,0:T(8,128)(2,1)S(1)} collective-permute-done((bf16[96,1152]{1,0:T(8,128)(2,1)S(1)}, bf16[96,1152]{1,0:T(8,128)(2,1)S(1)}, u32[]{:S(2)}, u32[]{:S(2)}) %collective-permute-start.12) | collective-permute-done | bytes 221216 | tf_op jit(solution)/shard_map/ppermute | solution.py:49
  89.2 0.1 add_convert_fusion.1
  89.3 5.3 %collective-permute-start.13 = (bf16[48,1152]{1,0:T(8,128)(2,1)S(1)}, bf16[48,1152]{1,0:T(8,128)(2,1)S(1)}, u32[]{:S(2)}, u32[]{:S(2)}) collective-permute-start(bf16[48,1152]{1,0:T(8,128)(2,1)S(1)} %add_convert_fusion.1), channel_id=1, source_target_pairs={{0,128},{1,385},{2,130},{3,387},{4,132},{5,389},{6,134},{7,391},{3... | collective-permute-start | bytes 331784 | tf_op jit(solution)/shard_map/ppermute | solution.py:49
  94.5 4.2 %collective-permute-done.13 = bf16[48,1152]{1,0:T(8,128)(2,1)S(1)} collective-permute-done((bf16[48,1152]{1,0:T(8,128)(2,1)S(1)}, bf16[48,1152]{1,0:T(8,128)(2,1)S(1)}, u32[]{:S(2)}, u32[]{:S(2)}) %collective-permute-start.13) | collective-permute-done | bytes 110624 | tf_op jit(solution)/shard_map/ppermute | solution.py:49
  98.8 5.8 %collective-permute-start.14 = (bf16[24,1152]{1,0:T(8,128)(2,1)S(1)}, bf16[24,1152]{1,0:T(8,128)(2,1)S(1)}, u32[]{:S(2)}, u32[]{:S(2)}) collective-permute-start(bf16[24,1152]{1,0:T(8,128)(2,1)S(1)} %add_convert_fusion.2), channel_id=1, source_target_pairs={{0,1},{1,0},{2,3},{3,2},{4,5},{5,4},{6,7},{7,6},{8,9},{9,8},{10,11... | collective-permute-start | bytes 165896 | tf_op jit(solution)/shard_map/ppermute | solution.py:53
  104.7 0.0 copy-start.1
  104.7 0.0 copy-start.3
  104.7 0.8 collective-permute-done.14.refs_6_
  105.5 0.0 copy-done.1
  105.5 0.0 copy-done.3
  105.5 0.9 back.1
  (16 shorter events, 0.3 us)
Async XLA Ops:
  0.6 0.8 copy-start
  1.5 0.8 copy-start.2
  2.4 9.7 %collective-permute-start = (bf16[24,1152]{1,0:T(8,128)(2,1)S(1)}, bf16[24,1152]{1,0:T(8,128)(2,1)S(1)}, u32[]{:S(2)}, u32[]{:S(2)}) collective-permute-start(bf16[24,1152]{1,0:T(8,128)(2,1)S(1)} %get-tuple-element.9), channel_id=1, source_target_pairs={{0,1},{1,0},{2,3},{3,2},{4,5},{5,4},{6,7},{7,6},{8,9},{9,8},{10,11... | collective-permute-start | bytes 165896 | tf_op jit(solution)/shard_map/ppermute | solution.py:53
  12.1 13.2 %collective-permute-start.1 = (bf16[48,1152]{1,0:T(8,128)(2,1)S(1)}, bf16[48,1152]{1,0:T(8,128)(2,1)S(1)}, u32[]{:S(2)}, u32[]{:S(2)}) collective-permute-start(bf16[48,1152]{1,0:T(8,128)(2,1)S(1)} %get-tuple-element.22), channel_id=1, source_target_pairs={{128,0},{385,1},{130,2},{387,3},{132,4},{389,5},{134,6},{391,7},{1... | collective-permute-start | bytes 331784 | tf_op jit(solution)/shard_map/ppermute | solution.py:49
  19.2 12.8 %collective-permute-start.3 = (bf16[48,1152]{1,0:T(8,128)(2,1)S(1)}, bf16[48,1152]{1,0:T(8,128)(2,1)S(1)}, u32[]{:S(2)}, u32[]{:S(2)}) collective-permute-start(bf16[48,1152]{1,0:T(8,128)(2,1)S(1)} %get-tuple-element.22), channel_id=1, source_target_pairs={{136,0},{401,1},{138,2},{403,3},{140,4},{405,5},{142,6},{407,7},{1... | collective-permute-start | bytes 331784 | tf_op jit(solution)/shard_map/ppermute | solution.py:49
  21.1 10.9 %collective-permute-start.2 = (bf16[48,1152]{1,0:T(8,128)(2,1)S(1)}, bf16[48,1152]{1,0:T(8,128)(2,1)S(1)}, u32[]{:S(2)}, u32[]{:S(2)}) collective-permute-start(bf16[48,1152]{1,0:T(8,128)(2,1)S(1)} %get-tuple-element.22), channel_id=1, source_target_pairs={{8,0},{17,1},{10,2},{19,3},{12,4},{21,5},{14,6},{23,7},{40,32},{49... | collective-permute-start | bytes 331784 | tf_op jit(solution)/shard_map/ppermute | solution.py:49
  32.1 9.3 %collective-permute-start.4 = (bf16[192,1152]{1,0:T(8,128)(2,1)S(1)}, bf16[192,1152]{1,0:T(8,128)(2,1)S(1)}, u32[]{:S(2)}, u32[]{:S(2)}) collective-permute-start(bf16[192,1152]{1,0:T(8,128)(2,1)S(1)} %get-tuple-element.14), channel_id=1, source_target_pairs={{2,0},{33,1},{0,2},{35,3},{6,4},{37,5},{4,6},{39,7},{34,32},{1,33}... | collective-permute-start | bytes 1327112 | tf_op jit(solution)/shard_map/ppermute | solution.py:49
  34.0 15.3 %collective-permute-start.5 = (bf16[192,1152]{1,0:T(8,128)(2,1)S(1)}, bf16[192,1152]{1,0:T(8,128)(2,1)S(1)}, u32[]{:S(2)}, u32[]{:S(2)}) collective-permute-start(bf16[192,1152]{1,0:T(8,128)(2,1)S(1)} %get-tuple-element.14), channel_id=1, source_target_pairs={{6,0},{97,1},{4,2},{99,3},{2,4},{101,5},{0,6},{103,7},{38,32},{65,... | collective-permute-start | bytes 1327112 | tf_op jit(solution)/shard_map/ppermute | solution.py:49
  37.4 12.0 %collective-permute-start.6 = (bf16[192,1152]{1,0:T(8,128)(2,1)S(1)}, bf16[192,1152]{1,0:T(8,128)(2,1)S(1)}, u32[]{:S(2)}, u32[]{:S(2)}) collective-permute-start(bf16[192,1152]{1,0:T(8,128)(2,1)S(1)} %get-tuple-element.14), channel_id=1, source_target_pairs={{4,0},{65,1},{6,2},{67,3},{0,4},{69,5},{2,6},{71,7},{36,32},{97,33... | collective-permute-start | bytes 1327112 | tf_op jit(solution)/shard_map/ppermute | solution.py:49
  41.5 14.0 %collective-permute-start.7 = (bf16[384,1152]{1,0:T(8,128)(2,1)S(1)}, bf16[384,1152]{1,0:T(8,128)(2,1)S(1)}, u32[]{:S(2)}, u32[]{:S(2)}) collective-permute-start(bf16[384,1152]{1,0:T(8,128)(2,1)S(1)} %constant_dynamic-update-slice_fusion.7.me_ref), channel_id=1, source_target_pairs={{0,1},{1,0},{2,3},{3,2},{4,5},{5,4},{6,7},{7,6},{8,9},{9,8},{10,11... | collective-permute-start | bytes 2654216 | tf_op jit(solution)/shard_map/ppermute | solution.py:53
  49.4 6.4 %collective-permute-start.8 = (bf16[384,1152]{1,0:T(8,128)(2,1)S(1)}, bf16[384,1152]{1,0:T(8,128)(2,1)S(1)}, u32[]{:S(2)}, u32[]{:S(2)}) collective-permute-start(bf16[384,1152]{1,0:T(8,128)(2,1)S(1)} %constant_dynamic-update-slice_fusion.13.ml_ref), channel_id=1, source_target_pairs={{0,1},{1,0},{2,3},{3,2},{4,5},{5,4},{6,7},{7,6},{8,9},{9,8},{10,11... | collective-permute-start | bytes 2654216 | tf_op jit(solution)/shard_map/ppermute | solution.py:53
  61.2 9.4 %collective-permute-start.9 = (bf16[192,1152]{1,0:T(8,128)(2,1)S(1)}, bf16[192,1152]{1,0:T(8,128)(2,1)S(1)}, u32[]{:S(2)}, u32[]{:S(2)}) collective-permute-start(bf16[192,1152]{1,0:T(8,128)(2,1)S(1)} %get-tuple-element.11), channel_id=1, source_target_pairs={{0,2},{1,33},{2,0},{3,35},{4,6},{5,37},{6,4},{7,39},{32,34},{33,1}... | collective-permute-start | bytes 1327112 | tf_op jit(solution)/shard_map/ppermute | solution.py:49
  64.3 15.2 %collective-permute-start.10 = (bf16[192,1152]{1,0:T(8,128)(2,1)S(1)}, bf16[192,1152]{1,0:T(8,128)(2,1)S(1)}, u32[]{:S(2)}, u32[]{:S(2)}) collective-permute-start(bf16[192,1152]{1,0:T(8,128)(2,1)S(1)} %get-tuple-element.12), channel_id=1, source_target_pairs={{0,6},{1,97},{2,4},{3,99},{4,2},{5,101},{6,0},{7,103},{32,38},{33,... | collective-permute-start | bytes 1327112 | tf_op jit(solution)/shard_map/ppermute | solution.py:49
  68.0 11.5 %collective-permute-start.11 = (bf16[192,1152]{1,0:T(8,128)(2,1)S(1)}, bf16[192,1152]{1,0:T(8,128)(2,1)S(1)}, u32[]{:S(2)}, u32[]{:S(2)}) collective-permute-start(bf16[192,1152]{1,0:T(8,128)(2,1)S(1)} %get-tuple-element.13), channel_id=1, source_target_pairs={{0,4},{1,65},{2,6},{3,67},{4,0},{5,69},{6,2},{7,71},{32,36},{33,97... | collective-permute-start | bytes 1327112 | tf_op jit(solution)/shard_map/ppermute | solution.py:49
  79.6 9.6 %collective-permute-start.12 = (bf16[96,1152]{1,0:T(8,128)(2,1)S(1)}, bf16[96,1152]{1,0:T(8,128)(2,1)S(1)}, u32[]{:S(2)}, u32[]{:S(2)}) collective-permute-start(bf16[96,1152]{1,0:T(8,128)(2,1)S(1)} %add_convert_fusion), channel_id=1, source_target_pairs={{0,8},{1,17},{2,10},{3,19},{4,12},{5,21},{6,14},{7,23},{32,40},{33... | collective-permute-start | bytes 663560 | tf_op jit(solution)/shard_map/ppermute | solution.py:49
  89.3 9.5 %collective-permute-start.13 = (bf16[48,1152]{1,0:T(8,128)(2,1)S(1)}, bf16[48,1152]{1,0:T(8,128)(2,1)S(1)}, u32[]{:S(2)}, u32[]{:S(2)}) collective-permute-start(bf16[48,1152]{1,0:T(8,128)(2,1)S(1)} %add_convert_fusion.1), channel_id=1, source_target_pairs={{0,128},{1,385},{2,130},{3,387},{4,132},{5,389},{6,134},{7,391},{3... | collective-permute-start | bytes 331784 | tf_op jit(solution)/shard_map/ppermute | solution.py:49
  98.8 6.7 %collective-permute-start.14 = (bf16[24,1152]{1,0:T(8,128)(2,1)S(1)}, bf16[24,1152]{1,0:T(8,128)(2,1)S(1)}, u32[]{:S(2)}, u32[]{:S(2)}) collective-permute-start(bf16[24,1152]{1,0:T(8,128)(2,1)S(1)} %add_convert_fusion.2), channel_id=1, source_target_pairs={{0,1},{1,0},{2,3},{3,2},{4,5},{5,4},{6,7},{7,6},{8,9},{9,8},{10,11... | collective-permute-start | bytes 165896 | tf_op jit(solution)/shard_map/ppermute | solution.py:53
  104.7 0.8 copy-start.1
  104.7 0.8 copy-start.3

commit v4 on v3

v4 whole, which is shorter than its diff:
```python
import functools

import jax
import jax.numpy as jnp
import numpy as np
from jax import lax
from jax.experimental import pallas as pl
from jax.experimental.pallas import tpu as pltpu
from jax.sharding import Mesh
from jax.sharding import PartitionSpec as P

D = 1152
ROWS = 22
PAD = 24
AXES = ("zh", "x", "zl", "y", "core")
SIZES = (4, 4, 4, 4, 2)
VMEM = 16 * 1024 * 1024
def at_z(move):
    return lambda p: {**p, "z": move(p["z"])}


def at_y(mask):
    return lambda p: {**p, "y": p["y"] ^ mask}


def at_x(mask):
    return lambda p: {**p, "x": p["x"] ^ mask}


FAR = (at_z(lambda z: z ^ 4), at_z(lambda z: z ^ 12))
NEAR = (at_z(lambda z: z ^ 1), at_z(lambda z: z ^ 2))
BOTH = (at_z(lambda z: z ^ 5), at_z(lambda z: z ^ 14))
LAST = tuple((at_y(m), at_x(m)) for m in (1, 3, 2))
ROUNDS = ((FAR, NEAR, BOTH), LAST)
BACK = ((FAR,), (NEAR,))


def flat(zh, x, zl, y, core):
    return (((zh * 4 + x) * 4 + zl) * 4 + y) * 2 + core


def fetch(value, sources, back=False):
    pairs = []
    for z in range(16):
        for x in range(4):
            for y in range(4):
                for c in range(2):
                    at = {"x": x, "y": y, "z": z}
                    pairs.append(tuple(flat(p["z"] >> 2, p["x"], p["z"] & 3, p["y"], c) for p in (sources[c](at), at)))
    return lax.ppermute(value, AXES, [(b, a) for a, b in pairs] if back else pairs)


def core_swap(value):
    return lax.ppermute(value, "core", [(0, 1), (1, 0)])


def add(parts):
    return sum(p.astype(jnp.float32) for p in parts).astype(jnp.bfloat16)


def blocks_of(place_ref, mine):
    x, y, z, core = (place_ref[k] for k in range(4))
    images = core == 0 if mine else core == 1

    def first(mask):
        zi, zt = z ^ mask[0], z ^ mask[1]
        return jnp.where(images, (zi >> 2) * 128 + (zi & 3) * 8, (zt & 3) * 128 + (zt >> 2) * 4)

    firsts = [first(mask) for mask in ((0, 0), (4, 12), (1, 2), (5, 14))]
    lasts = [jnp.where(images, x * 32 + (y ^ m) * 2, y * 32 + (x ^ m)) for m in (0, 1, 3, 2)]
    sides = [jnp.where(images, k, (1 - k) * 16) for k in range(2)]
    return lasts, firsts, sides


def cat_kernel(core_ref, both_ref, keep_ref, send_ref):
    img, txt = (unit_of(both_ref[k])[0].astype(jnp.bfloat16) for k in range(2))

    @pl.when(core_ref[0] == 0)
    def _():
        keep_ref[...] = img
        send_ref[...] = txt

    @pl.when(core_ref[0] == 1)
    def _():
        keep_ref[...] = txt
        send_ref[...] = img


def row_ids(blocks, start, stop):
    within = lax.broadcasted_iota(jnp.int32, (PAD, 1), 0)
    lasts, firsts, sides = blocks
    ids = [a + b + c for a in lasts[start:stop] for b in firsts for c in sides]
    return jnp.concatenate([jnp.where(within < ROWS, k * ROWS + within, -1) for k in ids])


def column_ids(blocks, start, stop):
    lasts, firsts, sides = blocks
    ids = [a + b + c for a in lasts[start:stop] for b in firsts for c in sides]
    at = lax.broadcasted_iota(jnp.int32, (1, len(ids) * PAD), 1)
    found = jnp.full(at.shape, -2, jnp.int32)
    for k, block in enumerate(ids):
        within = at - k * PAD
        found = jnp.where((within >= 0) & (within < ROWS), block * ROWS + within, found)
    return found


def unit_of(wide):
    wide = wide.astype(jnp.float32)
    length = jnp.sqrt(jnp.sum(wide * wide, axis=1, keepdims=True) + 1e-06)
    return wide / length, length


def unit_kernel(core_ref, both_ref, keep_ref, send_ref):
    img, txt = (unit_of(both_ref[k])[0].astype(jnp.bfloat16) for k in range(2))

    @pl.when(core_ref[0] == 0)
    def _():
        keep_ref[...] = img
        send_ref[...] = txt

    @pl.when(core_ref[0] == 1)
    def _():
        keep_ref[...] = txt
        send_ref[...] = img


def row_ids(blocks, start, stop):
    within = lax.broadcasted_iota(jnp.int32, (PAD, 1), 0)
    lasts, firsts, sides = blocks
    ids = [a + b + c for a in lasts[start:stop] for b in firsts for c in sides]
    return jnp.concatenate([jnp.where(within < ROWS, k * ROWS + within, -1) for k in ids])


def column_ids(blocks, start, stop):
    lasts, firsts, sides = blocks
    ids = [a + b + c for a in lasts[start:stop] for b in firsts for c in sides]
    at = lax.broadcasted_iota(jnp.int32, (1, len(ids) * PAD), 1)
    found = jnp.full(at.shape, -2, jnp.int32)
    for k, block in enumerate(ids):
        within = at - k * PAD
        found = jnp.where((within >= 0) & (within < ROWS), block * ROWS + within, found)
    return found


def unit_of(wide):
    wide = wide.astype(jnp.float32)
    length = jnp.sqrt(jnp.sum(wide * wide, axis=1, keepdims=True) + 1e-06)
    return wide / length, length


def weights_of(scal_ref, rows, columns, mine_ref, their_ref):
    s = lax.dot_general(mine_ref[...], their_ref[...], (((1,), (1,)), ((), ())), preferred_element_type=jnp.float32)
    label = jnp.where(rows == columns, 1.0, -1.0)
    d = 1.0 + jnp.exp(label * (scal_ref[0] * s + scal_ref[1]))
    r = pl.reciprocal(d, approx=True)
    r = r * (2.0 - d * r)
    return (-label * r).astype(jnp.bfloat16)


def pair_kernel(scal_ref, place_ref, me_ref, ml_ref, re_ref, rl_ref, *refs):
    *outs, their_ref = refs
    n = me_ref.shape[0]
    their_ref[:n, :] = re_ref[...]
    their_ref[n:, :] = rl_ref[...]
    mine_blocks, their_blocks = blocks_of(place_ref, True), blocks_of(place_ref, False)
    columns = column_ids(their_blocks, 0, 4)
    halves = [
        (k, weights_of(scal_ref, row_ids(mine_blocks, 2 * k, 2 * k + 2), columns, mine_ref, their_ref))
        for k, mine_ref in ((1, ml_ref), (0, me_ref))
    ]
    for k, w in halves:
        for t in range(3):
            cols = pl.ds(t * 384, 384)
            g = (scal_ref[0] * jnp.dot(w, their_ref[:, cols], preferred_element_type=jnp.float32)).astype(jnp.bfloat16)
            outs[2 * k][:, cols] = g[: n // 2]
            outs[2 * k + 1][:, cols] = g[n // 2 :]


def back_kernel(core_ref, img_ref, txt_ref, *refs):
    *mine, recv_ref, img_out, txt_out = refs

    def work(own_src, own_out, other_src, other_out):
        own = sum(ref[...].astype(jnp.float32) for ref in mine)
        for src, g, dst in ((own_src, own, own_out), (other_src, recv_ref[...].astype(jnp.float32), other_out)):
            unit, length = unit_of(src[...])
            g = g[:ROWS]
            along = jnp.sum(unit * g, axis=1, keepdims=True)
            dst[...] = (g - unit * along) / length

    pl.when(core_ref[0] == 0)(lambda: work(img_ref, img_out, txt_ref, txt_out))
    pl.when(core_ref[0] == 1)(lambda: work(txt_ref, txt_out, img_ref, img_out))


def call(kernel, name, out_shape, scalars, args, flops=0, scratch=()):
    vmem = pl.BlockSpec(memory_space=pltpu.VMEM)
    return pl.pallas_call(
        kernel,
        out_shape=out_shape,
        scratch_shapes=list(scratch),
        in_specs=[pl.BlockSpec(memory_space=pltpu.SMEM)] * len(scalars) + [vmem] * len(args),
        out_specs=(vmem,) * len(out_shape),
        compiler_params=pltpu.CompilerParams(vmem_limit_bytes=VMEM),
        cost_estimate=pl.CostEstimate(flops=flops, bytes_accessed=1 << 20, transcendentals=0),
        name=name,
    )(*scalars, *args)


def on_device(images, texts, logarithmic_scale, similarity_bias):
    core = lax.axis_index("core")
    place = jnp.stack([lax.axis_index("x"), lax.axis_index("y"), lax.axis_index("zh") * 4 + lax.axis_index("zl"), core])
    scal = jnp.stack([jnp.exp(logarithmic_scale), similarity_bias])
    cores = core.reshape((1,))
    block = jax.ShapeDtypeStruct((PAD, D), jnp.bfloat16)
    both = jnp.stack([jnp.pad(v, ((0, PAD - ROWS), (0, 0))) for v in (images, texts)])
    keep, send = call(unit_kernel, "unit", (block, block), [cores], [both])
    held = jnp.concatenate([keep, core_swap(send)])
    for sources in ROUNDS[:-1]:
        held = jnp.concatenate([held] + [fetch(held, s) for s in sources])
    one, three, two = [fetch(held, s) for s in ROUNDS[-1]]
    me = jnp.concatenate([held, one])
    re = core_swap(me)
    scalars = [scal, place]
    n = me.shape[0]
    piece = jax.ShapeDtypeStruct((n // 2, D), jnp.bfloat16)
    flops = 4 * n * n * D

    ml = jnp.concatenate([three, two])
    rl = core_swap(ml)
    keep, p1, p3, p2 = call(
        pair_kernel, "pairs", (piece,) * 4, scalars, [me, ml, re, rl], 4 * flops, [pltpu.VMEM((2 * n, D), jnp.bfloat16)]
    )
    parts = [keep] + [fetch(p, s, True) for p, s in zip((p1, p3, p2), LAST)]
    for sources in reversed(BACK):
        n = parts[0].shape[0] // (len(sources) + 1)
        sends = [add([p[k * n : (k + 1) * n] for p in parts]) for k in range(1, len(sources) + 1)]
        parts = [p[:n] for p in parts] + [fetch(p, s, True) for p, s in zip(sends, sources)]
    recv = core_swap(add([p[PAD:] for p in parts]))
    wide = jax.ShapeDtypeStruct((ROWS, D), jnp.float32)
    return call(back_kernel, "back", (wide, wide), [cores], [images, texts] + [p[:PAD] for p in parts] + [recv])


def solution(mesh):
    fine = Mesh(mesh.devices.reshape(SIZES), AXES)
    return jax.shard_map(
        on_device,
        mesh=fine,
        in_specs=(P(AXES, None), P(("zl", "y", "core", "zh", "x"), None), P(), P()),
        out_specs=(P(AXES, None), P(("zl", "y", "core", "zh", "x"), None)),
        check_vma=False,
    )
```

time: 107 us -> 105 us (0.981)
    unnamed x13 -> x9, local copies, waits for them, and re-layouts: 1.8 us -> 0.18 us
where the time goes in v4:
time: 105 us
  starting transfers between devices  61.8 us (59%)
  waiting for transfers between devices  33.6 us (32%)
  Pallas kernels  5.56 us (5%)
  between operations  2.27 us (2%)
  local copies, waits for them, and re-layouts  1.18 us (1%)
    ppermute x11, starting transfers between devices, fetch(): lax.ppermute(value, AXES, [(b, a) for a, b in pairs] if back else pairs)  39.2 us
    ppermute x11, waiting for transfers between devices, fetch(): lax.ppermute(value, AXES, [(b, a) for a, b in pairs] if back else pairs)  31.5 us
    ppermute x4, starting transfers between devices, core_swap(): return lax.ppermute(value, 'core', [(0, 1), (1, 0)])  22.5 us
    pallas_call x3, Pallas kernels, call(): pl.pallas_call(kernel, out_shape=out_shape, scratch_shapes=list(scratch),...  5.56 us
    ppermute x4, waiting for transfers between devices, core_swap(): return lax.ppermute(value, 'core', [(0, 1), (1, 0)])  2.13 us
  transfers between devices with their start and end apart: 15, of which 9 were waited for; matrix products, arithmetic and copies ran while one was open for 0% of the time, Pallas kernels for 0%

profile of v4, /device:TPU:1, one launch (start us, length us, event | category | flops | bytes accessed | tf_op | source)
XLA Modules:
  0.0 104.8 jit_solution(16135453047241709079)
XLA Ops:
  0.6 0.9 pad_bitcast_fusion
  1.5 0.1 unit.1
  1.7 8.8 %collective-permute-start = (bf16[24,1152]{1,0:T(8,128)(2,1)S(1)}, bf16[24,1152]{1,0:T(8,128)(2,1)S(1)}, u32[]{:S(2)}, u32[]{:S(2)}) collective-permute-start(bf16[24,1152]{1,0:T(8,128)(2,1)S(1)} %get-tuple-element.9), channel_id=1, source_target_pairs={{0,1},{1,0},{2,3},{3,2},{4,5},{5,4},{6,7},{7,6},{8,9},{9,8},{10,11... | collective-permute-start | bytes 165896 | tf_op jit(solution)/shard_map/ppermute | solution.py:54
  10.5 0.8 collective-permute-done
  11.3 7.1 %collective-permute-start.1 = (bf16[48,1152]{1,0:T(8,128)(2,1)S(1)}, bf16[48,1152]{1,0:T(8,128)(2,1)S(1)}, u32[]{:S(2)}, u32[]{:S(2)}) collective-permute-start(bf16[48,1152]{1,0:T(8,128)(2,1)S(1)} %get-tuple-element.22), channel_id=1, source_target_pairs={{128,0},{385,1},{130,2},{387,3},{132,4},{389,5},{134,6},{391,7},{1... | collective-permute-start | bytes 331784 | tf_op jit(solution)/shard_map/ppermute | solution.py:50
  18.4 1.9 %collective-permute-start.3 = (bf16[48,1152]{1,0:T(8,128)(2,1)S(1)}, bf16[48,1152]{1,0:T(8,128)(2,1)S(1)}, u32[]{:S(2)}, u32[]{:S(2)}) collective-permute-start(bf16[48,1152]{1,0:T(8,128)(2,1)S(1)} %get-tuple-element.22), channel_id=1, source_target_pairs={{136,0},{401,1},{138,2},{403,3},{140,4},{405,5},{142,6},{407,7},{1... | collective-permute-start | bytes 331784 | tf_op jit(solution)/shard_map/ppermute | solution.py:50
  20.4 4.2 %collective-permute-start.2 = (bf16[48,1152]{1,0:T(8,128)(2,1)S(1)}, bf16[48,1152]{1,0:T(8,128)(2,1)S(1)}, u32[]{:S(2)}, u32[]{:S(2)}) collective-permute-start(bf16[48,1152]{1,0:T(8,128)(2,1)S(1)} %get-tuple-element.22), channel_id=1, source_target_pairs={{8,0},{17,1},{10,2},{19,3},{12,4},{21,5},{14,6},{23,7},{40,32},{49... | collective-permute-start | bytes 331784 | tf_op jit(solution)/shard_map/ppermute | solution.py:50
  24.5 0.0 collective-permute-done.1
  24.6 6.7 %collective-permute-done.2 = bf16[48,1152]{1,0:T(8,128)(2,1)S(1)} collective-permute-done((bf16[48,1152]{1,0:T(8,128)(2,1)S(1)}, bf16[48,1152]{1,0:T(8,128)(2,1)S(1)}, u32[]{:S(2)}, u32[]{:S(2)}) %collective-permute-start.2) | collective-permute-done | bytes 110624 | tf_op jit(solution)/shard_map/ppermute | solution.py:50
  31.3 0.0 collective-permute-done.3
  31.3 1.9 %collective-permute-start.4 = (bf16[192,1152]{1,0:T(8,128)(2,1)S(1)}, bf16[192,1152]{1,0:T(8,128)(2,1)S(1)}, u32[]{:S(2)}, u32[]{:S(2)}) collective-permute-start(bf16[192,1152]{1,0:T(8,128)(2,1)S(1)} %get-tuple-element.14), channel_id=1, source_target_pairs={{2,0},{33,1},{0,2},{35,3},{6,4},{37,5},{4,6},{39,7},{34,32},{1,33}... | collective-permute-start | bytes 1327112 | tf_op jit(solution)/shard_map/ppermute | solution.py:50
  33.2 3.4 %collective-permute-start.5 = (bf16[192,1152]{1,0:T(8,128)(2,1)S(1)}, bf16[192,1152]{1,0:T(8,128)(2,1)S(1)}, u32[]{:S(2)}, u32[]{:S(2)}) collective-permute-start(bf16[192,1152]{1,0:T(8,128)(2,1)S(1)} %get-tuple-element.14), channel_id=1, source_target_pairs={{6,0},{97,1},{4,2},{99,3},{2,4},{101,5},{0,6},{103,7},{38,32},{65,... | collective-permute-start | bytes 1327112 | tf_op jit(solution)/shard_map/ppermute | solution.py:50
  36.6 3.7 %collective-permute-start.6 = (bf16[192,1152]{1,0:T(8,128)(2,1)S(1)}, bf16[192,1152]{1,0:T(8,128)(2,1)S(1)}, u32[]{:S(2)}, u32[]{:S(2)}) collective-permute-start(bf16[192,1152]{1,0:T(8,128)(2,1)S(1)} %get-tuple-element.14), channel_id=1, source_target_pairs={{4,0},{65,1},{6,2},{67,3},{0,4},{69,5},{2,6},{71,7},{36,32},{97,33... | collective-permute-start | bytes 1327112 | tf_op jit(solution)/shard_map/ppermute | solution.py:50
  40.3 0.3 collective-permute-done.4
  40.7 3.6 %collective-permute-start.7 = (bf16[384,1152]{1,0:T(8,128)(2,1)S(1)}, bf16[384,1152]{1,0:T(8,128)(2,1)S(1)}, u32[]{:S(2)}, u32[]{:S(2)}) collective-permute-start(bf16[384,1152]{1,0:T(8,128)(2,1)S(1)} %constant_dynamic-update-slice_fusion.7.me_ref), channel_id=1, source_target_pairs={{0,1},{1,0},{2,3},{3,2},{4,5},{5,4},{6,7},{7,6},{8,9},{9,8},{10,11... | collective-permute-start | bytes 2654216 | tf_op jit(solution)/shard_map/ppermute | solution.py:54
  44.3 4.2 %collective-permute-done.5 = bf16[192,1152]{1,0:T(8,128)(2,1)S(1)} collective-permute-done((bf16[192,1152]{1,0:T(8,128)(2,1)S(1)}, bf16[192,1152]{1,0:T(8,128)(2,1)S(1)}, u32[]{:S(2)}, u32[]{:S(2)}) %collective-permute-start.5) | collective-permute-done | bytes 442400 | tf_op jit(solution)/shard_map/ppermute | solution.py:50
  48.6 0.0 collective-permute-done.6
  48.6 4.3 %collective-permute-start.8 = (bf16[384,1152]{1,0:T(8,128)(2,1)S(1)}, bf16[384,1152]{1,0:T(8,128)(2,1)S(1)}, u32[]{:S(2)}, u32[]{:S(2)}) collective-permute-start(bf16[384,1152]{1,0:T(8,128)(2,1)S(1)} %constant_dynamic-update-slice_fusion.13.ml_ref), channel_id=1, source_target_pairs={{0,1},{1,0},{2,3},{3,2},{4,5},{5,4},{6,7},{7,6},{8,9},{9,8},{10,11... | collective-permute-start | bytes 2654216 | tf_op jit(solution)/shard_map/ppermute | solution.py:54
  54.3 0.1 pad_maximum_fusion.1.scal_ref
  54.4 0.1 pad_add_fusion.place_ref
  54.5 0.0 collective-permute-done.7.re_ref
  54.5 0.5 collective-permute-done.8.rl_ref
  55.0 4.5 %pairs.1 = (bf16[192,1152]{1,0:T(8,128)(2,1)S(1)}, bf16[192,1152]{1,0:T(8,128)(2,1)S(1)}, bf16[192,1152]{1,0:T(8,128)(2,1)S(1)}, bf16[192,1152]{1,0:T(8,128)(2,1)S(1)}) custom-call(f32[2]{0:T(128)S(1)} %pad_maximum_fusion.1.scal_ref, s32[4]{0:T(128)S(1)} %pad_add_fusion.place_ref, bf16[384,1152]{1,0:T(8,128)(2,1)S(1)} %constant_dynamic-update-slice_fusion.7.me_ref, ...), custom_call_target="tpu_custom_call" | custom-call | flops 2717908992 | bytes 1048576 | tf_op jit(solution)/shard_map/pairs/pallas_call | solution.py:196
  59.5 3.1 %collective-permute-start.9 = (bf16[192,1152]{1,0:T(8,128)(2,1)S(1)}, bf16[192,1152]{1,0:T(8,128)(2,1)S(1)}, u32[]{:S(2)}, u32[]{:S(2)}) collective-permute-start(bf16[192,1152]{1,0:T(8,128)(2,1)S(1)} %get-tuple-element.11), channel_id=1, source_target_pairs={{0,2},{1,33},{2,0},{3,35},{4,6},{5,37},{6,4},{7,39},{32,34},{33,1}... | collective-permute-start | bytes 1327112 | tf_op jit(solution)/shard_map/ppermute | solution.py:50
  62.7 3.7 %collective-permute-start.10 = (bf16[192,1152]{1,0:T(8,128)(2,1)S(1)}, bf16[192,1152]{1,0:T(8,128)(2,1)S(1)}, u32[]{:S(2)}, u32[]{:S(2)}) collective-permute-start(bf16[192,1152]{1,0:T(8,128)(2,1)S(1)} %get-tuple-element.12), channel_id=1, source_target_pairs={{0,6},{1,97},{2,4},{3,99},{4,2},{5,101},{6,0},{7,103},{32,38},{33,... | collective-permute-start | bytes 1327112 | tf_op jit(solution)/shard_map/ppermute | solution.py:50
  66.4 2.6 %collective-permute-start.11 = (bf16[192,1152]{1,0:T(8,128)(2,1)S(1)}, bf16[192,1152]{1,0:T(8,128)(2,1)S(1)}, u32[]{:S(2)}, u32[]{:S(2)}) collective-permute-start(bf16[192,1152]{1,0:T(8,128)(2,1)S(1)} %get-tuple-element.13), channel_id=1, source_target_pairs={{0,4},{1,65},{2,6},{3,67},{4,0},{5,69},{6,2},{7,71},{32,36},{33,97... | collective-permute-start | bytes 1327112 | tf_op jit(solution)/shard_map/ppermute | solution.py:50
  68.9 0.0 collective-permute-done.9
  69.0 8.9 %collective-permute-done.10 = bf16[192,1152]{1,0:T(8,128)(2,1)S(1)} collective-permute-done((bf16[192,1152]{1,0:T(8,128)(2,1)S(1)}, bf16[192,1152]{1,0:T(8,128)(2,1)S(1)}, u32[]{:S(2)}, u32[]{:S(2)}) %collective-permute-start.10) | collective-permute-done | bytes 442400 | tf_op jit(solution)/shard_map/ppermute | solution.py:50
  77.8 0.0 collective-permute-done.11
  77.8 0.1 add_convert_fusion
  78.0 2.4 %collective-permute-start.12 = (bf16[96,1152]{1,0:T(8,128)(2,1)S(1)}, bf16[96,1152]{1,0:T(8,128)(2,1)S(1)}, u32[]{:S(2)}, u32[]{:S(2)}) collective-permute-start(bf16[96,1152]{1,0:T(8,128)(2,1)S(1)} %add_convert_fusion), channel_id=1, source_target_pairs={{0,8},{1,17},{2,10},{3,19},{4,12},{5,21},{6,14},{7,23},{32,40},{33... | collective-permute-start | bytes 663560 | tf_op jit(solution)/shard_map/ppermute | solution.py:50
  80.4 7.1 %collective-permute-done.12 = bf16[96,1152]{1,0:T(8,128)(2,1)S(1)} collective-permute-done((bf16[96,1152]{1,0:T(8,128)(2,1)S(1)}, bf16[96,1152]{1,0:T(8,128)(2,1)S(1)}, u32[]{:S(2)}, u32[]{:S(2)}) %collective-permute-start.12) | collective-permute-done | bytes 221216 | tf_op jit(solution)/shard_map/ppermute | solution.py:50
  87.5 0.1 add_convert_fusion.1
  87.6 5.2 %collective-permute-start.13 = (bf16[48,1152]{1,0:T(8,128)(2,1)S(1)}, bf16[48,1152]{1,0:T(8,128)(2,1)S(1)}, u32[]{:S(2)}, u32[]{:S(2)}) collective-permute-start(bf16[48,1152]{1,0:T(8,128)(2,1)S(1)} %add_convert_fusion.1), channel_id=1, source_target_pairs={{0,128},{1,385},{2,130},{3,387},{4,132},{5,389},{6,134},{7,391},{3... | collective-permute-start | bytes 331784 | tf_op jit(solution)/shard_map/ppermute | solution.py:50
  92.9 4.3 %collective-permute-done.13 = bf16[48,1152]{1,0:T(8,128)(2,1)S(1)} collective-permute-done((bf16[48,1152]{1,0:T(8,128)(2,1)S(1)}, bf16[48,1152]{1,0:T(8,128)(2,1)S(1)}, u32[]{:S(2)}, u32[]{:S(2)}) %collective-permute-start.13) | collective-permute-done | bytes 110624 | tf_op jit(solution)/shard_map/ppermute | solution.py:50
  97.2 5.8 %collective-permute-start.14 = (bf16[24,1152]{1,0:T(8,128)(2,1)S(1)}, bf16[24,1152]{1,0:T(8,128)(2,1)S(1)}, u32[]{:S(2)}, u32[]{:S(2)}) collective-permute-start(bf16[24,1152]{1,0:T(8,128)(2,1)S(1)} %add_convert_fusion.2), channel_id=1, source_target_pairs={{0,1},{1,0},{2,3},{3,2},{4,5},{5,4},{6,7},{7,6},{8,9},{9,8},{10,11... | collective-permute-start | bytes 165896 | tf_op jit(solution)/shard_map/ppermute | solution.py:54
  103.0 0.0 copy-start
  103.1 0.0 copy-start.1
  103.1 0.8 collective-permute-done.14.refs_6_
  103.8 0.0 copy-done
  103.9 0.0 copy-done.1
  103.9 0.9 back.1
  (16 shorter events, 0.3 us)
Async XLA Ops:
  1.7 9.7 %collective-permute-start = (bf16[24,1152]{1,0:T(8,128)(2,1)S(1)}, bf16[24,1152]{1,0:T(8,128)(2,1)S(1)}, u32[]{:S(2)}, u32[]{:S(2)}) collective-permute-start(bf16[24,1152]{1,0:T(8,128)(2,1)S(1)} %get-tuple-element.9), channel_id=1, source_target_pairs={{0,1},{1,0},{2,3},{3,2},{4,5},{5,4},{6,7},{7,6},{8,9},{9,8},{10,11... | collective-permute-start | bytes 165896 | tf_op jit(solution)/shard_map/ppermute | solution.py:54
  11.3 13.2 %collective-permute-start.1 = (bf16[48,1152]{1,0:T(8,128)(2,1)S(1)}, bf16[48,1152]{1,0:T(8,128)(2,1)S(1)}, u32[]{:S(2)}, u32[]{:S(2)}) collective-permute-start(bf16[48,1152]{1,0:T(8,128)(2,1)S(1)} %get-tuple-element.22), channel_id=1, source_target_pairs={{128,0},{385,1},{130,2},{387,3},{132,4},{389,5},{134,6},{391,7},{1... | collective-permute-start | bytes 331784 | tf_op jit(solution)/shard_map/ppermute | solution.py:50
  18.4 12.8 %collective-permute-start.3 = (bf16[48,1152]{1,0:T(8,128)(2,1)S(1)}, bf16[48,1152]{1,0:T(8,128)(2,1)S(1)}, u32[]{:S(2)}, u32[]{:S(2)}) collective-permute-start(bf16[48,1152]{1,0:T(8,128)(2,1)S(1)} %get-tuple-element.22), channel_id=1, source_target_pairs={{136,0},{401,1},{138,2},{403,3},{140,4},{405,5},{142,6},{407,7},{1... | collective-permute-start | bytes 331784 | tf_op jit(solution)/shard_map/ppermute | solution.py:50
  20.4 10.9 %collective-permute-start.2 = (bf16[48,1152]{1,0:T(8,128)(2,1)S(1)}, bf16[48,1152]{1,0:T(8,128)(2,1)S(1)}, u32[]{:S(2)}, u32[]{:S(2)}) collective-permute-start(bf16[48,1152]{1,0:T(8,128)(2,1)S(1)} %get-tuple-element.22), channel_id=1, source_target_pairs={{8,0},{17,1},{10,2},{19,3},{12,4},{21,5},{14,6},{23,7},{40,32},{49... | collective-permute-start | bytes 331784 | tf_op jit(solution)/shard_map/ppermute | solution.py:50
  31.3 9.3 %collective-permute-start.4 = (bf16[192,1152]{1,0:T(8,128)(2,1)S(1)}, bf16[192,1152]{1,0:T(8,128)(2,1)S(1)}, u32[]{:S(2)}, u32[]{:S(2)}) collective-permute-start(bf16[192,1152]{1,0:T(8,128)(2,1)S(1)} %get-tuple-element.14), channel_id=1, source_target_pairs={{2,0},{33,1},{0,2},{35,3},{6,4},{37,5},{4,6},{39,7},{34,32},{1,33}... | collective-permute-start | bytes 1327112 | tf_op jit(solution)/shard_map/ppermute | solution.py:50
  33.2 15.3 %collective-permute-start.5 = (bf16[192,1152]{1,0:T(8,128)(2,1)S(1)}, bf16[192,1152]{1,0:T(8,128)(2,1)S(1)}, u32[]{:S(2)}, u32[]{:S(2)}) collective-permute-start(bf16[192,1152]{1,0:T(8,128)(2,1)S(1)} %get-tuple-element.14), channel_id=1, source_target_pairs={{6,0},{97,1},{4,2},{99,3},{2,4},{101,5},{0,6},{103,7},{38,32},{65,... | collective-permute-start | bytes 1327112 | tf_op jit(solution)/shard_map/ppermute | solution.py:50
  36.6 12.0 %collective-permute-start.6 = (bf16[192,1152]{1,0:T(8,128)(2,1)S(1)}, bf16[192,1152]{1,0:T(8,128)(2,1)S(1)}, u32[]{:S(2)}, u32[]{:S(2)}) collective-permute-start(bf16[192,1152]{1,0:T(8,128)(2,1)S(1)} %get-tuple-element.14), channel_id=1, source_target_pairs={{4,0},{65,1},{6,2},{67,3},{0,4},{69,5},{2,6},{71,7},{36,32},{97,33... | collective-permute-start | bytes 1327112 | tf_op jit(solution)/shard_map/ppermute | solution.py:50
  40.7 13.8 %collective-permute-start.7 = (bf16[384,1152]{1,0:T(8,128)(2,1)S(1)}, bf16[384,1152]{1,0:T(8,128)(2,1)S(1)}, u32[]{:S(2)}, u32[]{:S(2)}) collective-permute-start(bf16[384,1152]{1,0:T(8,128)(2,1)S(1)} %constant_dynamic-update-slice_fusion.7.me_ref), channel_id=1, source_target_pairs={{0,1},{1,0},{2,3},{3,2},{4,5},{5,4},{6,7},{7,6},{8,9},{9,8},{10,11... | collective-permute-start | bytes 2654216 | tf_op jit(solution)/shard_map/ppermute | solution.py:54
  48.6 6.4 %collective-permute-start.8 = (bf16[384,1152]{1,0:T(8,128)(2,1)S(1)}, bf16[384,1152]{1,0:T(8,128)(2,1)S(1)}, u32[]{:S(2)}, u32[]{:S(2)}) collective-permute-start(bf16[384,1152]{1,0:T(8,128)(2,1)S(1)} %constant_dynamic-update-slice_fusion.13.ml_ref), channel_id=1, source_target_pairs={{0,1},{1,0},{2,3},{3,2},{4,5},{5,4},{6,7},{7,6},{8,9},{9,8},{10,11... | collective-permute-start | bytes 2654216 | tf_op jit(solution)/shard_map/ppermute | solution.py:54
  59.5 9.4 %collective-permute-start.9 = (bf16[192,1152]{1,0:T(8,128)(2,1)S(1)}, bf16[192,1152]{1,0:T(8,128)(2,1)S(1)}, u32[]{:S(2)}, u32[]{:S(2)}) collective-permute-start(bf16[192,1152]{1,0:T(8,128)(2,1)S(1)} %get-tuple-element.11), channel_id=1, source_target_pairs={{0,2},{1,33},{2,0},{3,35},{4,6},{5,37},{6,4},{7,39},{32,34},{33,1}... | collective-permute-start | bytes 1327112 | tf_op jit(solution)/shard_map/ppermute | solution.py:50
  62.7 15.2 %collective-permute-start.10 = (bf16[192,1152]{1,0:T(8,128)(2,1)S(1)}, bf16[192,1152]{1,0:T(8,128)(2,1)S(1)}, u32[]{:S(2)}, u32[]{:S(2)}) collective-permute-start(bf16[192,1152]{1,0:T(8,128)(2,1)S(1)} %get-tuple-element.12), channel_id=1, source_target_pairs={{0,6},{1,97},{2,4},{3,99},{4,2},{5,101},{6,0},{7,103},{32,38},{33,... | collective-permute-start | bytes 1327112 | tf_op jit(solution)/shard_map/ppermute | solution.py:50
  66.4 11.5 %collective-permute-start.11 = (bf16[192,1152]{1,0:T(8,128)(2,1)S(1)}, bf16[192,1152]{1,0:T(8,128)(2,1)S(1)}, u32[]{:S(2)}, u32[]{:S(2)}) collective-permute-start(bf16[192,1152]{1,0:T(8,128)(2,1)S(1)} %get-tuple-element.13), channel_id=1, source_target_pairs={{0,4},{1,65},{2,6},{3,67},{4,0},{5,69},{6,2},{7,71},{32,36},{33,97... | collective-permute-start | bytes 1327112 | tf_op jit(solution)/shard_map/ppermute | solution.py:50
  78.0 9.6 %collective-permute-start.12 = (bf16[96,1152]{1,0:T(8,128)(2,1)S(1)}, bf16[96,1152]{1,0:T(8,128)(2,1)S(1)}, u32[]{:S(2)}, u32[]{:S(2)}) collective-permute-start(bf16[96,1152]{1,0:T(8,128)(2,1)S(1)} %add_convert_fusion), channel_id=1, source_target_pairs={{0,8},{1,17},{2,10},{3,19},{4,12},{5,21},{6,14},{7,23},{32,40},{33... | collective-permute-start | bytes 663560 | tf_op jit(solution)/shard_map/ppermute | solution.py:50
  87.6 9.5 %collective-permute-start.13 = (bf16[48,1152]{1,0:T(8,128)(2,1)S(1)}, bf16[48,1152]{1,0:T(8,128)(2,1)S(1)}, u32[]{:S(2)}, u32[]{:S(2)}) collective-permute-start(bf16[48,1152]{1,0:T(8,128)(2,1)S(1)} %add_convert_fusion.1), channel_id=1, source_target_pairs={{0,128},{1,385},{2,130},{3,387},{4,132},{5,389},{6,134},{7,391},{3... | collective-permute-start | bytes 331784 | tf_op jit(solution)/shard_map/ppermute | solution.py:50
  97.2 6.7 %collective-permute-start.14 = (bf16[24,1152]{1,0:T(8,128)(2,1)S(1)}, bf16[24,1152]{1,0:T(8,128)(2,1)S(1)}, u32[]{:S(2)}, u32[]{:S(2)}) collective-permute-start(bf16[24,1152]{1,0:T(8,128)(2,1)S(1)} %add_convert_fusion.2), channel_id=1, source_target_pairs={{0,1},{1,0},{2,3},{3,2},{4,5},{5,4},{6,7},{7,6},{8,9},{9,8},{10,11... | collective-permute-start | bytes 165896 | tf_op jit(solution)/shard_map/ppermute | solution.py:54
  103.0 0.8 copy-start
  103.1 0.8 copy-start.1

commit v5 on v4

--- a/solution.py
+++ b/solution.py
@@ -169,8 +169,8 @@
         for k, mine_ref in ((1, ml_ref), (0, me_ref))
     ]
     for k, w in halves:
-        for t in range(3):
-            cols = pl.ds(t * 384, 384)
+        for start, width in ((0, 512), (512, 512), (1024, 128)):
+            cols = pl.ds(start, width)
             g = (scal_ref[0] * jnp.dot(w, their_ref[:, cols], preferred_element_type=jnp.float32)).astype(jnp.bfloat16)
             outs[2 * k][:, cols] = g[: n // 2]
             outs[2 * k + 1][:, cols] = g[n // 2 :]

time: 105 us -> 105 us (level)
  no operation moved by 1% of the time
where the time goes in v5:
time: 105 us; the launch traced here: 104 us
  starting transfers between devices  61.8 us (59%)
  waiting for transfers between devices  33.6 us (32%)
  Pallas kernels  5.17 us (5%)
  between operations  2.27 us (2%)
  local copies, waits for them, and re-layouts  1.18 us (1%)
    ppermute x11, starting transfers between devices, fetch(): lax.ppermute(value, AXES, [(b, a) for a, b in pairs] if back else pairs)  39.2 us
    ppermute x11, waiting for transfers between devices, fetch(): lax.ppermute(value, AXES, [(b, a) for a, b in pairs] if back else pairs)  31.5 us
    ppermute x4, starting transfers between devices, core_swap(): return lax.ppermute(value, 'core', [(0, 1), (1, 0)])  22.6 us
    pallas_call x3, Pallas kernels, call(): pl.pallas_call(kernel, out_shape=out_shape, scratch_shapes=list(scratch),...  5.17 us
    ppermute x4, waiting for transfers between devices, core_swap(): return lax.ppermute(value, 'core', [(0, 1), (1, 0)])  2.13 us
  transfers between devices with their start and end apart: 15, of which 9 were waited for; matrix products, arithmetic and copies ran while one was open for 0% of the time, Pallas kernels for 0%

profile of v5, /device:TPU:1, one launch (start us, length us, event | category | flops | bytes accessed | tf_op | source)
XLA Modules:
  0.0 104.4 jit_solution(14789950999640763885)
XLA Ops:
  0.6 0.9 pad_bitcast_fusion
  1.5 0.1 unit.1
  1.7 8.8 %collective-permute-start = (bf16[24,1152]{1,0:T(8,128)(2,1)S(1)}, bf16[24,1152]{1,0:T(8,128)(2,1)S(1)}, u32[]{:S(2)}, u32[]{:S(2)}) collective-permute-start(bf16[24,1152]{1,0:T(8,128)(2,1)S(1)} %get-tuple-element.9), channel_id=1, source_target_pairs={{0,1},{1,0},{2,3},{3,2},{4,5},{5,4},{6,7},{7,6},{8,9},{9,8},{10,11... | collective-permute-start | bytes 165896 | tf_op jit(solution)/shard_map/ppermute | solution.py:54
  10.5 0.8 collective-permute-done
  11.3 7.1 %collective-permute-start.1 = (bf16[48,1152]{1,0:T(8,128)(2,1)S(1)}, bf16[48,1152]{1,0:T(8,128)(2,1)S(1)}, u32[]{:S(2)}, u32[]{:S(2)}) collective-permute-start(bf16[48,1152]{1,0:T(8,128)(2,1)S(1)} %get-tuple-element.22), channel_id=1, source_target_pairs={{128,0},{385,1},{130,2},{387,3},{132,4},{389,5},{134,6},{391,7},{1... | collective-permute-start | bytes 331784 | tf_op jit(solution)/shard_map/ppermute | solution.py:50
  18.4 1.9 %collective-permute-start.3 = (bf16[48,1152]{1,0:T(8,128)(2,1)S(1)}, bf16[48,1152]{1,0:T(8,128)(2,1)S(1)}, u32[]{:S(2)}, u32[]{:S(2)}) collective-permute-start(bf16[48,1152]{1,0:T(8,128)(2,1)S(1)} %get-tuple-element.22), channel_id=1, source_target_pairs={{136,0},{401,1},{138,2},{403,3},{140,4},{405,5},{142,6},{407,7},{1... | collective-permute-start | bytes 331784 | tf_op jit(solution)/shard_map/ppermute | solution.py:50
  20.4 4.2 %collective-permute-start.2 = (bf16[48,1152]{1,0:T(8,128)(2,1)S(1)}, bf16[48,1152]{1,0:T(8,128)(2,1)S(1)}, u32[]{:S(2)}, u32[]{:S(2)}) collective-permute-start(bf16[48,1152]{1,0:T(8,128)(2,1)S(1)} %get-tuple-element.22), channel_id=1, source_target_pairs={{8,0},{17,1},{10,2},{19,3},{12,4},{21,5},{14,6},{23,7},{40,32},{49... | collective-permute-start | bytes 331784 | tf_op jit(solution)/shard_map/ppermute | solution.py:50
  24.5 0.0 collective-permute-done.1
  24.6 6.7 %collective-permute-done.2 = bf16[48,1152]{1,0:T(8,128)(2,1)S(1)} collective-permute-done((bf16[48,1152]{1,0:T(8,128)(2,1)S(1)}, bf16[48,1152]{1,0:T(8,128)(2,1)S(1)}, u32[]{:S(2)}, u32[]{:S(2)}) %collective-permute-start.2) | collective-permute-done | bytes 110624 | tf_op jit(solution)/shard_map/ppermute | solution.py:50
  31.3 0.0 collective-permute-done.3
  31.3 1.9 %collective-permute-start.4 = (bf16[192,1152]{1,0:T(8,128)(2,1)S(1)}, bf16[192,1152]{1,0:T(8,128)(2,1)S(1)}, u32[]{:S(2)}, u32[]{:S(2)}) collective-permute-start(bf16[192,1152]{1,0:T(8,128)(2,1)S(1)} %get-tuple-element.14), channel_id=1, source_target_pairs={{2,0},{33,1},{0,2},{35,3},{6,4},{37,5},{4,6},{39,7},{34,32},{1,33}... | collective-permute-start | bytes 1327112 | tf_op jit(solution)/shard_map/ppermute | solution.py:50
  33.2 3.4 %collective-permute-start.5 = (bf16[192,1152]{1,0:T(8,128)(2,1)S(1)}, bf16[192,1152]{1,0:T(8,128)(2,1)S(1)}, u32[]{:S(2)}, u32[]{:S(2)}) collective-permute-start(bf16[192,1152]{1,0:T(8,128)(2,1)S(1)} %get-tuple-element.14), channel_id=1, source_target_pairs={{6,0},{97,1},{4,2},{99,3},{2,4},{101,5},{0,6},{103,7},{38,32},{65,... | collective-permute-start | bytes 1327112 | tf_op jit(solution)/shard_map/ppermute | solution.py:50
  36.6 3.7 %collective-permute-start.6 = (bf16[192,1152]{1,0:T(8,128)(2,1)S(1)}, bf16[192,1152]{1,0:T(8,128)(2,1)S(1)}, u32[]{:S(2)}, u32[]{:S(2)}) collective-permute-start(bf16[192,1152]{1,0:T(8,128)(2,1)S(1)} %get-tuple-element.14), channel_id=1, source_target_pairs={{4,0},{65,1},{6,2},{67,3},{0,4},{69,5},{2,6},{71,7},{36,32},{97,33... | collective-permute-start | bytes 1327112 | tf_op jit(solution)/shard_map/ppermute | solution.py:50
  40.3 0.3 collective-permute-done.4
  40.7 3.6 %collective-permute-start.7 = (bf16[384,1152]{1,0:T(8,128)(2,1)S(1)}, bf16[384,1152]{1,0:T(8,128)(2,1)S(1)}, u32[]{:S(2)}, u32[]{:S(2)}) collective-permute-start(bf16[384,1152]{1,0:T(8,128)(2,1)S(1)} %constant_dynamic-update-slice_fusion.7.me_ref), channel_id=1, source_target_pairs={{0,1},{1,0},{2,3},{3,2},{4,5},{5,4},{6,7},{7,6},{8,9},{9,8},{10,11... | collective-permute-start | bytes 2654216 | tf_op jit(solution)/shard_map/ppermute | solution.py:54
  44.3 4.2 %collective-permute-done.5 = bf16[192,1152]{1,0:T(8,128)(2,1)S(1)} collective-permute-done((bf16[192,1152]{1,0:T(8,128)(2,1)S(1)}, bf16[192,1152]{1,0:T(8,128)(2,1)S(1)}, u32[]{:S(2)}, u32[]{:S(2)}) %collective-permute-start.5) | collective-permute-done | bytes 442400 | tf_op jit(solution)/shard_map/ppermute | solution.py:50
  48.6 0.0 collective-permute-done.6
  48.6 4.3 %collective-permute-start.8 = (bf16[384,1152]{1,0:T(8,128)(2,1)S(1)}, bf16[384,1152]{1,0:T(8,128)(2,1)S(1)}, u32[]{:S(2)}, u32[]{:S(2)}) collective-permute-start(bf16[384,1152]{1,0:T(8,128)(2,1)S(1)} %constant_dynamic-update-slice_fusion.13.ml_ref), channel_id=1, source_target_pairs={{0,1},{1,0},{2,3},{3,2},{4,5},{5,4},{6,7},{7,6},{8,9},{9,8},{10,11... | collective-permute-start | bytes 2654216 | tf_op jit(solution)/shard_map/ppermute | solution.py:54
  54.3 0.1 pad_maximum_fusion.1.scal_ref
  54.4 0.1 pad_add_fusion.place_ref
  54.5 0.0 collective-permute-done.7.re_ref
  54.5 0.5 collective-permute-done.8.rl_ref
  55.0 4.1 %pairs.1 = (bf16[192,1152]{1,0:T(8,128)(2,1)S(1)}, bf16[192,1152]{1,0:T(8,128)(2,1)S(1)}, bf16[192,1152]{1,0:T(8,128)(2,1)S(1)}, bf16[192,1152]{1,0:T(8,128)(2,1)S(1)}) custom-call(f32[2]{0:T(128)S(1)} %pad_maximum_fusion.1.scal_ref, s32[4]{0:T(128)S(1)} %pad_add_fusion.place_ref, bf16[384,1152]{1,0:T(8,128)(2,1)S(1)} %constant_dynamic-update-slice_fusion.7.me_ref, ...), custom_call_target="tpu_custom_call" | custom-call | flops 2717908992 | bytes 1048576 | tf_op jit(solution)/shard_map/pairs/pallas_call | solution.py:196
  59.1 3.1 %collective-permute-start.9 = (bf16[192,1152]{1,0:T(8,128)(2,1)S(1)}, bf16[192,1152]{1,0:T(8,128)(2,1)S(1)}, u32[]{:S(2)}, u32[]{:S(2)}) collective-permute-start(bf16[192,1152]{1,0:T(8,128)(2,1)S(1)} %get-tuple-element.11), channel_id=1, source_target_pairs={{0,2},{1,33},{2,0},{3,35},{4,6},{5,37},{6,4},{7,39},{32,34},{33,1}... | collective-permute-start | bytes 1327112 | tf_op jit(solution)/shard_map/ppermute | solution.py:50
  62.3 3.7 %collective-permute-start.10 = (bf16[192,1152]{1,0:T(8,128)(2,1)S(1)}, bf16[192,1152]{1,0:T(8,128)(2,1)S(1)}, u32[]{:S(2)}, u32[]{:S(2)}) collective-permute-start(bf16[192,1152]{1,0:T(8,128)(2,1)S(1)} %get-tuple-element.12), channel_id=1, source_target_pairs={{0,6},{1,97},{2,4},{3,99},{4,2},{5,101},{6,0},{7,103},{32,38},{33,... | collective-permute-start | bytes 1327112 | tf_op jit(solution)/shard_map/ppermute | solution.py:50
  66.0 2.6 %collective-permute-start.11 = (bf16[192,1152]{1,0:T(8,128)(2,1)S(1)}, bf16[192,1152]{1,0:T(8,128)(2,1)S(1)}, u32[]{:S(2)}, u32[]{:S(2)}) collective-permute-start(bf16[192,1152]{1,0:T(8,128)(2,1)S(1)} %get-tuple-element.13), channel_id=1, source_target_pairs={{0,4},{1,65},{2,6},{3,67},{4,0},{5,69},{6,2},{7,71},{32,36},{33,97... | collective-permute-start | bytes 1327112 | tf_op jit(solution)/shard_map/ppermute | solution.py:50
  68.6 0.0 collective-permute-done.9
  68.6 8.9 %collective-permute-done.10 = bf16[192,1152]{1,0:T(8,128)(2,1)S(1)} collective-permute-done((bf16[192,1152]{1,0:T(8,128)(2,1)S(1)}, bf16[192,1152]{1,0:T(8,128)(2,1)S(1)}, u32[]{:S(2)}, u32[]{:S(2)}) %collective-permute-start.10) | collective-permute-done | bytes 442400 | tf_op jit(solution)/shard_map/ppermute | solution.py:50
  77.4 0.0 collective-permute-done.11
  77.5 0.1 add_convert_fusion
  77.6 2.4 %collective-permute-start.12 = (bf16[96,1152]{1,0:T(8,128)(2,1)S(1)}, bf16[96,1152]{1,0:T(8,128)(2,1)S(1)}, u32[]{:S(2)}, u32[]{:S(2)}) collective-permute-start(bf16[96,1152]{1,0:T(8,128)(2,1)S(1)} %add_convert_fusion), channel_id=1, source_target_pairs={{0,8},{1,17},{2,10},{3,19},{4,12},{5,21},{6,14},{7,23},{32,40},{33... | collective-permute-start | bytes 663560 | tf_op jit(solution)/shard_map/ppermute | solution.py:50
  80.0 7.1 %collective-permute-done.12 = bf16[96,1152]{1,0:T(8,128)(2,1)S(1)} collective-permute-done((bf16[96,1152]{1,0:T(8,128)(2,1)S(1)}, bf16[96,1152]{1,0:T(8,128)(2,1)S(1)}, u32[]{:S(2)}, u32[]{:S(2)}) %collective-permute-start.12) | collective-permute-done | bytes 221216 | tf_op jit(solution)/shard_map/ppermute | solution.py:50
  87.1 0.1 add_convert_fusion.1
  87.2 5.2 %collective-permute-start.13 = (bf16[48,1152]{1,0:T(8,128)(2,1)S(1)}, bf16[48,1152]{1,0:T(8,128)(2,1)S(1)}, u32[]{:S(2)}, u32[]{:S(2)}) collective-permute-start(bf16[48,1152]{1,0:T(8,128)(2,1)S(1)} %add_convert_fusion.1), channel_id=1, source_target_pairs={{0,128},{1,385},{2,130},{3,387},{4,132},{5,389},{6,134},{7,391},{3... | collective-permute-start | bytes 331784 | tf_op jit(solution)/shard_map/ppermute | solution.py:50
  92.5 4.3 %collective-permute-done.13 = bf16[48,1152]{1,0:T(8,128)(2,1)S(1)} collective-permute-done((bf16[48,1152]{1,0:T(8,128)(2,1)S(1)}, bf16[48,1152]{1,0:T(8,128)(2,1)S(1)}, u32[]{:S(2)}, u32[]{:S(2)}) %collective-permute-start.13) | collective-permute-done | bytes 110624 | tf_op jit(solution)/shard_map/ppermute | solution.py:50
  96.8 5.8 %collective-permute-start.14 = (bf16[24,1152]{1,0:T(8,128)(2,1)S(1)}, bf16[24,1152]{1,0:T(8,128)(2,1)S(1)}, u32[]{:S(2)}, u32[]{:S(2)}) collective-permute-start(bf16[24,1152]{1,0:T(8,128)(2,1)S(1)} %add_convert_fusion.2), channel_id=1, source_target_pairs={{0,1},{1,0},{2,3},{3,2},{4,5},{5,4},{6,7},{7,6},{8,9},{9,8},{10,11... | collective-permute-start | bytes 165896 | tf_op jit(solution)/shard_map/ppermute | solution.py:54
  102.7 0.0 copy-start
  102.7 0.0 copy-start.1
  102.7 0.8 collective-permute-done.14.refs_6_
  103.5 0.0 copy-done
  103.5 0.0 copy-done.1
  103.5 0.9 back.1
  (16 shorter events, 0.3 us)
Async XLA Ops:
  1.7 9.7 %collective-permute-start = (bf16[24,1152]{1,0:T(8,128)(2,1)S(1)}, bf16[24,1152]{1,0:T(8,128)(2,1)S(1)}, u32[]{:S(2)}, u32[]{:S(2)}) collective-permute-start(bf16[24,1152]{1,0:T(8,128)(2,1)S(1)} %get-tuple-element.9), channel_id=1, source_target_pairs={{0,1},{1,0},{2,3},{3,2},{4,5},{5,4},{6,7},{7,6},{8,9},{9,8},{10,11... | collective-permute-start | bytes 165896 | tf_op jit(solution)/shard_map/ppermute | solution.py:54
  11.3 13.2 %collective-permute-start.1 = (bf16[48,1152]{1,0:T(8,128)(2,1)S(1)}, bf16[48,1152]{1,0:T(8,128)(2,1)S(1)}, u32[]{:S(2)}, u32[]{:S(2)}) collective-permute-start(bf16[48,1152]{1,0:T(8,128)(2,1)S(1)} %get-tuple-element.22), channel_id=1, source_target_pairs={{128,0},{385,1},{130,2},{387,3},{132,4},{389,5},{134,6},{391,7},{1... | collective-permute-start | bytes 331784 | tf_op jit(solution)/shard_map/ppermute | solution.py:50
  18.4 12.8 %collective-permute-start.3 = (bf16[48,1152]{1,0:T(8,128)(2,1)S(1)}, bf16[48,1152]{1,0:T(8,128)(2,1)S(1)}, u32[]{:S(2)}, u32[]{:S(2)}) collective-permute-start(bf16[48,1152]{1,0:T(8,128)(2,1)S(1)} %get-tuple-element.22), channel_id=1, source_target_pairs={{136,0},{401,1},{138,2},{403,3},{140,4},{405,5},{142,6},{407,7},{1... | collective-permute-start | bytes 331784 | tf_op jit(solution)/shard_map/ppermute | solution.py:50
  20.4 10.9 %collective-permute-start.2 = (bf16[48,1152]{1,0:T(8,128)(2,1)S(1)}, bf16[48,1152]{1,0:T(8,128)(2,1)S(1)}, u32[]{:S(2)}, u32[]{:S(2)}) collective-permute-start(bf16[48,1152]{1,0:T(8,128)(2,1)S(1)} %get-tuple-element.22), channel_id=1, source_target_pairs={{8,0},{17,1},{10,2},{19,3},{12,4},{21,5},{14,6},{23,7},{40,32},{49... | collective-permute-start | bytes 331784 | tf_op jit(solution)/shard_map/ppermute | solution.py:50
  31.3 9.3 %collective-permute-start.4 = (bf16[192,1152]{1,0:T(8,128)(2,1)S(1)}, bf16[192,1152]{1,0:T(8,128)(2,1)S(1)}, u32[]{:S(2)}, u32[]{:S(2)}) collective-permute-start(bf16[192,1152]{1,0:T(8,128)(2,1)S(1)} %get-tuple-element.14), channel_id=1, source_target_pairs={{2,0},{33,1},{0,2},{35,3},{6,4},{37,5},{4,6},{39,7},{34,32},{1,33}... | collective-permute-start | bytes 1327112 | tf_op jit(solution)/shard_map/ppermute | solution.py:50
  33.2 15.3 %collective-permute-start.5 = (bf16[192,1152]{1,0:T(8,128)(2,1)S(1)}, bf16[192,1152]{1,0:T(8,128)(2,1)S(1)}, u32[]{:S(2)}, u32[]{:S(2)}) collective-permute-start(bf16[192,1152]{1,0:T(8,128)(2,1)S(1)} %get-tuple-element.14), channel_id=1, source_target_pairs={{6,0},{97,1},{4,2},{99,3},{2,4},{101,5},{0,6},{103,7},{38,32},{65,... | collective-permute-start | bytes 1327112 | tf_op jit(solution)/shard_map/ppermute | solution.py:50
  36.6 12.0 %collective-permute-start.6 = (bf16[192,1152]{1,0:T(8,128)(2,1)S(1)}, bf16[192,1152]{1,0:T(8,128)(2,1)S(1)}, u32[]{:S(2)}, u32[]{:S(2)}) collective-permute-start(bf16[192,1152]{1,0:T(8,128)(2,1)S(1)} %get-tuple-element.14), channel_id=1, source_target_pairs={{4,0},{65,1},{6,2},{67,3},{0,4},{69,5},{2,6},{71,7},{36,32},{97,33... | collective-permute-start | bytes 1327112 | tf_op jit(solution)/shard_map/ppermute | solution.py:50
  40.7 13.8 %collective-permute-start.7 = (bf16[384,1152]{1,0:T(8,128)(2,1)S(1)}, bf16[384,1152]{1,0:T(8,128)(2,1)S(1)}, u32[]{:S(2)}, u32[]{:S(2)}) collective-permute-start(bf16[384,1152]{1,0:T(8,128)(2,1)S(1)} %constant_dynamic-update-slice_fusion.7.me_ref), channel_id=1, source_target_pairs={{0,1},{1,0},{2,3},{3,2},{4,5},{5,4},{6,7},{7,6},{8,9},{9,8},{10,11... | collective-permute-start | bytes 2654216 | tf_op jit(solution)/shard_map/ppermute | solution.py:54
  48.6 6.4 %collective-permute-start.8 = (bf16[384,1152]{1,0:T(8,128)(2,1)S(1)}, bf16[384,1152]{1,0:T(8,128)(2,1)S(1)}, u32[]{:S(2)}, u32[]{:S(2)}) collective-permute-start(bf16[384,1152]{1,0:T(8,128)(2,1)S(1)} %constant_dynamic-update-slice_fusion.13.ml_ref), channel_id=1, source_target_pairs={{0,1},{1,0},{2,3},{3,2},{4,5},{5,4},{6,7},{7,6},{8,9},{9,8},{10,11... | collective-permute-start | bytes 2654216 | tf_op jit(solution)/shard_map/ppermute | solution.py:54
  59.1 9.4 %collective-permute-start.9 = (bf16[192,1152]{1,0:T(8,128)(2,1)S(1)}, bf16[192,1152]{1,0:T(8,128)(2,1)S(1)}, u32[]{:S(2)}, u32[]{:S(2)}) collective-permute-start(bf16[192,1152]{1,0:T(8,128)(2,1)S(1)} %get-tuple-element.11), channel_id=1, source_target_pairs={{0,2},{1,33},{2,0},{3,35},{4,6},{5,37},{6,4},{7,39},{32,34},{33,1}... | collective-permute-start | bytes 1327112 | tf_op jit(solution)/shard_map/ppermute | solution.py:50
  62.3 15.2 %collective-permute-start.10 = (bf16[192,1152]{1,0:T(8,128)(2,1)S(1)}, bf16[192,1152]{1,0:T(8,128)(2,1)S(1)}, u32[]{:S(2)}, u32[]{:S(2)}) collective-permute-start(bf16[192,1152]{1,0:T(8,128)(2,1)S(1)} %get-tuple-element.12), channel_id=1, source_target_pairs={{0,6},{1,97},{2,4},{3,99},{4,2},{5,101},{6,0},{7,103},{32,38},{33,... | collective-permute-start | bytes 1327112 | tf_op jit(solution)/shard_map/ppermute | solution.py:50
  66.0 11.5 %collective-permute-start.11 = (bf16[192,1152]{1,0:T(8,128)(2,1)S(1)}, bf16[192,1152]{1,0:T(8,128)(2,1)S(1)}, u32[]{:S(2)}, u32[]{:S(2)}) collective-permute-start(bf16[192,1152]{1,0:T(8,128)(2,1)S(1)} %get-tuple-element.13), channel_id=1, source_target_pairs={{0,4},{1,65},{2,6},{3,67},{4,0},{5,69},{6,2},{7,71},{32,36},{33,97... | collective-permute-start | bytes 1327112 | tf_op jit(solution)/shard_map/ppermute | solution.py:50
  77.6 9.6 %collective-permute-start.12 = (bf16[96,1152]{1,0:T(8,128)(2,1)S(1)}, bf16[96,1152]{1,0:T(8,128)(2,1)S(1)}, u32[]{:S(2)}, u32[]{:S(2)}) collective-permute-start(bf16[96,1152]{1,0:T(8,128)(2,1)S(1)} %add_convert_fusion), channel_id=1, source_target_pairs={{0,8},{1,17},{2,10},{3,19},{4,12},{5,21},{6,14},{7,23},{32,40},{33... | collective-permute-start | bytes 663560 | tf_op jit(solution)/shard_map/ppermute | solution.py:50
  87.2 9.5 %collective-permute-start.13 = (bf16[48,1152]{1,0:T(8,128)(2,1)S(1)}, bf16[48,1152]{1,0:T(8,128)(2,1)S(1)}, u32[]{:S(2)}, u32[]{:S(2)}) collective-permute-start(bf16[48,1152]{1,0:T(8,128)(2,1)S(1)} %add_convert_fusion.1), channel_id=1, source_target_pairs={{0,128},{1,385},{2,130},{3,387},{4,132},{5,389},{6,134},{7,391},{3... | collective-permute-start | bytes 331784 | tf_op jit(solution)/shard_map/ppermute | solution.py:50
  96.8 6.7 %collective-permute-start.14 = (bf16[24,1152]{1,0:T(8,128)(2,1)S(1)}, bf16[24,1152]{1,0:T(8,128)(2,1)S(1)}, u32[]{:S(2)}, u32[]{:S(2)}) collective-permute-start(bf16[24,1152]{1,0:T(8,128)(2,1)S(1)} %add_convert_fusion.2), channel_id=1, source_target_pairs={{0,1},{1,0},{2,3},{3,2},{4,5},{5,4},{6,7},{7,6},{8,9},{9,8},{10,11... | collective-permute-start | bytes 165896 | tf_op jit(solution)/shard_map/ppermute | solution.py:54
  102.7 0.8 copy-start
  102.7 0.8 copy-start.1

commit v6 on v5

--- a/solution.py
+++ b/solution.py
@@ -171,19 +171,19 @@
     for k, w in halves:
         for start, width in ((0, 512), (512, 512), (1024, 128)):
             cols = pl.ds(start, width)
-            g = (scal_ref[0] * jnp.dot(w, their_ref[:, cols], preferred_element_type=jnp.float32)).astype(jnp.bfloat16)
+            g = jnp.dot(w, their_ref[:, cols], preferred_element_type=jnp.float32).astype(jnp.bfloat16)
             outs[2 * k][:, cols] = g[: n // 2]
             outs[2 * k + 1][:, cols] = g[n // 2 :]
 
 
-def back_kernel(core_ref, img_ref, txt_ref, *refs):
+def back_kernel(core_ref, scal_ref, img_ref, txt_ref, *refs):
     *mine, recv_ref, img_out, txt_out = refs
 
     def work(own_src, own_out, other_src, other_out):
         own = sum(ref[...].astype(jnp.float32) for ref in mine)
         for src, g, dst in ((own_src, own, own_out), (other_src, recv_ref[...].astype(jnp.float32), other_out)):
             unit, length = unit_of(src[...])
-            g = g[:ROWS]
+            g = scal_ref[0] * g[:ROWS]
             along = jnp.sum(unit * g, axis=1, keepdims=True)
             dst[...] = (g - unit * along) / length
 
@@ -236,7 +236,7 @@
         parts = [p[:n] for p in parts] + [fetch(p, s, True) for p, s in zip(sends, sources)]
     recv = core_swap(add([p[PAD:] for p in parts]))
     wide = jax.ShapeDtypeStruct((ROWS, D), jnp.float32)
-    return call(back_kernel, "back", (wide, wide), [cores], [images, texts] + [p[:PAD] for p in parts] + [recv])
+    return call(back_kernel, "back", (wide, wide), [cores, scal], [images, texts] + [p[:PAD] for p in parts] + [recv])
 
 
 def solution(mesh):

time: 105 us -> 106 us (level)
  no operation moved by 1% of the time
where the time goes in v6:
time: 106 us; the launch traced here: 105 us
  starting transfers between devices  61.8 us (58%)
  waiting for transfers between devices  33.6 us (32%)
  Pallas kernels  5.72 us (5%)
  between operations  2.27 us (2%)
  local copies, waits for them, and re-layouts  1.18 us (1%)
    ppermute x11, starting transfers between devices, fetch(): lax.ppermute(value, AXES, [(b, a) for a, b in pairs] if back else pairs)  39.3 us
    ppermute x11, waiting for transfers between devices, fetch(): lax.ppermute(value, AXES, [(b, a) for a, b in pairs] if back else pairs)  31.4 us
    ppermute x4, starting transfers between devices, core_swap(): return lax.ppermute(value, 'core', [(0, 1), (1, 0)])  22.6 us
    pallas_call x3, Pallas kernels, call(): pl.pallas_call(kernel, out_shape=out_shape, scratch_shapes=list(scratch),...  5.72 us
    ppermute x4, waiting for transfers between devices, core_swap(): return lax.ppermute(value, 'core', [(0, 1), (1, 0)])  2.13 us
  transfers between devices with their start and end apart: 15, of which 9 were waited for; matrix products, arithmetic and copies ran while one was open for 0% of the time, Pallas kernels for 0%

profile of v6, /device:TPU:1, one launch (start us, length us, event | category | flops | bytes accessed | tf_op | source)
XLA Modules:
  0.0 105.0 jit_solution(1485454238447934293)
XLA Ops:
  0.6 0.9 pad_bitcast_fusion
  1.5 0.1 unit.1
  1.7 8.8 %collective-permute-start = (bf16[24,1152]{1,0:T(8,128)(2,1)S(1)}, bf16[24,1152]{1,0:T(8,128)(2,1)S(1)}, u32[]{:S(2)}, u32[]{:S(2)}) collective-permute-start(bf16[24,1152]{1,0:T(8,128)(2,1)S(1)} %get-tuple-element.9), channel_id=1, source_target_pairs={{0,1},{1,0},{2,3},{3,2},{4,5},{5,4},{6,7},{7,6},{8,9},{9,8},{10,11... | collective-permute-start | bytes 165896 | tf_op jit(solution)/shard_map/ppermute | solution.py:54
  10.5 0.8 collective-permute-done
  11.3 7.1 %collective-permute-start.1 = (bf16[48,1152]{1,0:T(8,128)(2,1)S(1)}, bf16[48,1152]{1,0:T(8,128)(2,1)S(1)}, u32[]{:S(2)}, u32[]{:S(2)}) collective-permute-start(bf16[48,1152]{1,0:T(8,128)(2,1)S(1)} %get-tuple-element.22), channel_id=1, source_target_pairs={{128,0},{385,1},{130,2},{387,3},{132,4},{389,5},{134,6},{391,7},{1... | collective-permute-start | bytes 331784 | tf_op jit(solution)/shard_map/ppermute | solution.py:50
  18.4 1.9 %collective-permute-start.3 = (bf16[48,1152]{1,0:T(8,128)(2,1)S(1)}, bf16[48,1152]{1,0:T(8,128)(2,1)S(1)}, u32[]{:S(2)}, u32[]{:S(2)}) collective-permute-start(bf16[48,1152]{1,0:T(8,128)(2,1)S(1)} %get-tuple-element.22), channel_id=1, source_target_pairs={{136,0},{401,1},{138,2},{403,3},{140,4},{405,5},{142,6},{407,7},{1... | collective-permute-start | bytes 331784 | tf_op jit(solution)/shard_map/ppermute | solution.py:50
  20.4 4.2 %collective-permute-start.2 = (bf16[48,1152]{1,0:T(8,128)(2,1)S(1)}, bf16[48,1152]{1,0:T(8,128)(2,1)S(1)}, u32[]{:S(2)}, u32[]{:S(2)}) collective-permute-start(bf16[48,1152]{1,0:T(8,128)(2,1)S(1)} %get-tuple-element.22), channel_id=1, source_target_pairs={{8,0},{17,1},{10,2},{19,3},{12,4},{21,5},{14,6},{23,7},{40,32},{49... | collective-permute-start | bytes 331784 | tf_op jit(solution)/shard_map/ppermute | solution.py:50
  24.5 0.0 collective-permute-done.1
  24.6 6.7 %collective-permute-done.2 = bf16[48,1152]{1,0:T(8,128)(2,1)S(1)} collective-permute-done((bf16[48,1152]{1,0:T(8,128)(2,1)S(1)}, bf16[48,1152]{1,0:T(8,128)(2,1)S(1)}, u32[]{:S(2)}, u32[]{:S(2)}) %collective-permute-start.2) | collective-permute-done | bytes 110624 | tf_op jit(solution)/shard_map/ppermute | solution.py:50
  31.3 0.0 collective-permute-done.3
  31.3 1.9 %collective-permute-start.4 = (bf16[192,1152]{1,0:T(8,128)(2,1)S(1)}, bf16[192,1152]{1,0:T(8,128)(2,1)S(1)}, u32[]{:S(2)}, u32[]{:S(2)}) collective-permute-start(bf16[192,1152]{1,0:T(8,128)(2,1)S(1)} %get-tuple-element.14), channel_id=1, source_target_pairs={{2,0},{33,1},{0,2},{35,3},{6,4},{37,5},{4,6},{39,7},{34,32},{1,33}... | collective-permute-start | bytes 1327112 | tf_op jit(solution)/shard_map/ppermute | solution.py:50
  33.2 3.4 %collective-permute-start.5 = (bf16[192,1152]{1,0:T(8,128)(2,1)S(1)}, bf16[192,1152]{1,0:T(8,128)(2,1)S(1)}, u32[]{:S(2)}, u32[]{:S(2)}) collective-permute-start(bf16[192,1152]{1,0:T(8,128)(2,1)S(1)} %get-tuple-element.14), channel_id=1, source_target_pairs={{6,0},{97,1},{4,2},{99,3},{2,4},{101,5},{0,6},{103,7},{38,32},{65,... | collective-permute-start | bytes 1327112 | tf_op jit(solution)/shard_map/ppermute | solution.py:50
  36.6 3.7 %collective-permute-start.6 = (bf16[192,1152]{1,0:T(8,128)(2,1)S(1)}, bf16[192,1152]{1,0:T(8,128)(2,1)S(1)}, u32[]{:S(2)}, u32[]{:S(2)}) collective-permute-start(bf16[192,1152]{1,0:T(8,128)(2,1)S(1)} %get-tuple-element.14), channel_id=1, source_target_pairs={{4,0},{65,1},{6,2},{67,3},{0,4},{69,5},{2,6},{71,7},{36,32},{97,33... | collective-permute-start | bytes 1327112 | tf_op jit(solution)/shard_map/ppermute | solution.py:50
  40.3 0.3 collective-permute-done.4
  40.7 3.6 %collective-permute-start.7 = (bf16[384,1152]{1,0:T(8,128)(2,1)S(1)}, bf16[384,1152]{1,0:T(8,128)(2,1)S(1)}, u32[]{:S(2)}, u32[]{:S(2)}) collective-permute-start(bf16[384,1152]{1,0:T(8,128)(2,1)S(1)} %constant_dynamic-update-slice_fusion.7.me_ref), channel_id=1, source_target_pairs={{0,1},{1,0},{2,3},{3,2},{4,5},{5,4},{6,7},{7,6},{8,9},{9,8},{10,11... | collective-permute-start | bytes 2654216 | tf_op jit(solution)/shard_map/ppermute | solution.py:54
  44.3 4.2 %collective-permute-done.5 = bf16[192,1152]{1,0:T(8,128)(2,1)S(1)} collective-permute-done((bf16[192,1152]{1,0:T(8,128)(2,1)S(1)}, bf16[192,1152]{1,0:T(8,128)(2,1)S(1)}, u32[]{:S(2)}, u32[]{:S(2)}) %collective-permute-start.5) | collective-permute-done | bytes 442400 | tf_op jit(solution)/shard_map/ppermute | solution.py:50
  48.6 0.0 collective-permute-done.6
  48.6 4.3 %collective-permute-start.8 = (bf16[384,1152]{1,0:T(8,128)(2,1)S(1)}, bf16[384,1152]{1,0:T(8,128)(2,1)S(1)}, u32[]{:S(2)}, u32[]{:S(2)}) collective-permute-start(bf16[384,1152]{1,0:T(8,128)(2,1)S(1)} %constant_dynamic-update-slice_fusion.13.ml_ref), channel_id=1, source_target_pairs={{0,1},{1,0},{2,3},{3,2},{4,5},{5,4},{6,7},{7,6},{8,9},{9,8},{10,11... | collective-permute-start | bytes 2654216 | tf_op jit(solution)/shard_map/ppermute | solution.py:54
  54.3 0.1 pad_maximum_fusion.1.scal_ref
  54.4 0.1 pad_add_fusion.place_ref
  54.5 0.0 collective-permute-done.7.re_ref
  54.5 0.5 collective-permute-done.8.rl_ref
  55.0 4.1 %pairs.1 = (bf16[192,1152]{1,0:T(8,128)(2,1)S(1)}, bf16[192,1152]{1,0:T(8,128)(2,1)S(1)}, bf16[192,1152]{1,0:T(8,128)(2,1)S(1)}, bf16[192,1152]{1,0:T(8,128)(2,1)S(1)}) custom-call(f32[2]{0:T(128)S(1)} %pad_maximum_fusion.1.scal_ref, s32[4]{0:T(128)S(1)} %pad_add_fusion.place_ref, bf16[384,1152]{1,0:T(8,128)(2,1)S(1)} %constant_dynamic-update-slice_fusion.7.me_ref, ...), custom_call_target="tpu_custom_call" | custom-call | flops 2717908992 | bytes 1048576 | tf_op jit(solution)/shard_map/pairs/pallas_call | solution.py:196
  59.1 3.1 %collective-permute-start.9 = (bf16[192,1152]{1,0:T(8,128)(2,1)S(1)}, bf16[192,1152]{1,0:T(8,128)(2,1)S(1)}, u32[]{:S(2)}, u32[]{:S(2)}) collective-permute-start(bf16[192,1152]{1,0:T(8,128)(2,1)S(1)} %get-tuple-element.11), channel_id=1, source_target_pairs={{0,2},{1,33},{2,0},{3,35},{4,6},{5,37},{6,4},{7,39},{32,34},{33,1}... | collective-permute-start | bytes 1327112 | tf_op jit(solution)/shard_map/ppermute | solution.py:50
  62.3 3.7 %collective-permute-start.10 = (bf16[192,1152]{1,0:T(8,128)(2,1)S(1)}, bf16[192,1152]{1,0:T(8,128)(2,1)S(1)}, u32[]{:S(2)}, u32[]{:S(2)}) collective-permute-start(bf16[192,1152]{1,0:T(8,128)(2,1)S(1)} %get-tuple-element.12), channel_id=1, source_target_pairs={{0,6},{1,97},{2,4},{3,99},{4,2},{5,101},{6,0},{7,103},{32,38},{33,... | collective-permute-start | bytes 1327112 | tf_op jit(solution)/shard_map/ppermute | solution.py:50
  66.0 2.6 %collective-permute-start.11 = (bf16[192,1152]{1,0:T(8,128)(2,1)S(1)}, bf16[192,1152]{1,0:T(8,128)(2,1)S(1)}, u32[]{:S(2)}, u32[]{:S(2)}) collective-permute-start(bf16[192,1152]{1,0:T(8,128)(2,1)S(1)} %get-tuple-element.13), channel_id=1, source_target_pairs={{0,4},{1,65},{2,6},{3,67},{4,0},{5,69},{6,2},{7,71},{32,36},{33,97... | collective-permute-start | bytes 1327112 | tf_op jit(solution)/shard_map/ppermute | solution.py:50
  68.6 0.0 collective-permute-done.9
  68.6 8.9 %collective-permute-done.10 = bf16[192,1152]{1,0:T(8,128)(2,1)S(1)} collective-permute-done((bf16[192,1152]{1,0:T(8,128)(2,1)S(1)}, bf16[192,1152]{1,0:T(8,128)(2,1)S(1)}, u32[]{:S(2)}, u32[]{:S(2)}) %collective-permute-start.10) | collective-permute-done | bytes 442400 | tf_op jit(solution)/shard_map/ppermute | solution.py:50
  77.5 0.0 collective-permute-done.11
  77.5 0.1 add_convert_fusion
  77.6 2.4 %collective-permute-start.12 = (bf16[96,1152]{1,0:T(8,128)(2,1)S(1)}, bf16[96,1152]{1,0:T(8,128)(2,1)S(1)}, u32[]{:S(2)}, u32[]{:S(2)}) collective-permute-start(bf16[96,1152]{1,0:T(8,128)(2,1)S(1)} %add_convert_fusion), channel_id=1, source_target_pairs={{0,8},{1,17},{2,10},{3,19},{4,12},{5,21},{6,14},{7,23},{32,40},{33... | collective-permute-start | bytes 663560 | tf_op jit(solution)/shard_map/ppermute | solution.py:50
  80.0 7.1 %collective-permute-done.12 = bf16[96,1152]{1,0:T(8,128)(2,1)S(1)} collective-permute-done((bf16[96,1152]{1,0:T(8,128)(2,1)S(1)}, bf16[96,1152]{1,0:T(8,128)(2,1)S(1)}, u32[]{:S(2)}, u32[]{:S(2)}) %collective-permute-start.12) | collective-permute-done | bytes 221216 | tf_op jit(solution)/shard_map/ppermute | solution.py:50
  87.2 0.1 add_convert_fusion.1
  87.2 5.2 %collective-permute-start.13 = (bf16[48,1152]{1,0:T(8,128)(2,1)S(1)}, bf16[48,1152]{1,0:T(8,128)(2,1)S(1)}, u32[]{:S(2)}, u32[]{:S(2)}) collective-permute-start(bf16[48,1152]{1,0:T(8,128)(2,1)S(1)} %add_convert_fusion.1), channel_id=1, source_target_pairs={{0,128},{1,385},{2,130},{3,387},{4,132},{5,389},{6,134},{7,391},{3... | collective-permute-start | bytes 331784 | tf_op jit(solution)/shard_map/ppermute | solution.py:50
  92.5 4.2 %collective-permute-done.13 = bf16[48,1152]{1,0:T(8,128)(2,1)S(1)} collective-permute-done((bf16[48,1152]{1,0:T(8,128)(2,1)S(1)}, bf16[48,1152]{1,0:T(8,128)(2,1)S(1)}, u32[]{:S(2)}, u32[]{:S(2)}) %collective-permute-start.13) | collective-permute-done | bytes 110624 | tf_op jit(solution)/shard_map/ppermute | solution.py:50
  96.8 5.8 %collective-permute-start.14 = (bf16[24,1152]{1,0:T(8,128)(2,1)S(1)}, bf16[24,1152]{1,0:T(8,128)(2,1)S(1)}, u32[]{:S(2)}, u32[]{:S(2)}) collective-permute-start(bf16[24,1152]{1,0:T(8,128)(2,1)S(1)} %add_convert_fusion.2), channel_id=1, source_target_pairs={{0,1},{1,0},{2,3},{3,2},{4,5},{5,4},{6,7},{7,6},{8,9},{9,8},{10,11... | collective-permute-start | bytes 165896 | tf_op jit(solution)/shard_map/ppermute | solution.py:54
  102.7 0.0 copy-start
  102.7 0.0 copy-start.1
  102.7 0.8 collective-permute-done.14.refs_6_
  103.5 0.0 copy-done
  103.5 0.0 copy-done.1
  103.5 1.5 %back.1 = (f32[22,1152]{1,0:T(8,128)}, f32[22,1152]{1,0:T(8,128)}) custom-call(s32[1]{0:T(128)} %bitcast.core_ref, f32[2]{0:T(128)S(1)} %pad_maximum_fusion.1.scal_ref, bf16[22,1152]{1,0:T(8,128)(2,1)S(1)} %copy-done, bf16[22,1152]{1,0:T(8,128)(2,1)S(1)} %copy-done.1, bf16[24,1152]{1,0:T(8,128)(2,1)S(1)} %slice.90.refs_0_, ...), custom_call_target="tpu_custom_call" | custom-call | bytes 1048576 | tf_op jit(solution)/shard_map/back/pallas_call | solution.py:196
  (16 shorter events, 0.3 us)
Async XLA Ops:
  1.7 9.7 %collective-permute-start = (bf16[24,1152]{1,0:T(8,128)(2,1)S(1)}, bf16[24,1152]{1,0:T(8,128)(2,1)S(1)}, u32[]{:S(2)}, u32[]{:S(2)}) collective-permute-start(bf16[24,1152]{1,0:T(8,128)(2,1)S(1)} %get-tuple-element.9), channel_id=1, source_target_pairs={{0,1},{1,0},{2,3},{3,2},{4,5},{5,4},{6,7},{7,6},{8,9},{9,8},{10,11... | collective-permute-start | bytes 165896 | tf_op jit(solution)/shard_map/ppermute | solution.py:54
  11.3 13.2 %collective-permute-start.1 = (bf16[48,1152]{1,0:T(8,128)(2,1)S(1)}, bf16[48,1152]{1,0:T(8,128)(2,1)S(1)}, u32[]{:S(2)}, u32[]{:S(2)}) collective-permute-start(bf16[48,1152]{1,0:T(8,128)(2,1)S(1)} %get-tuple-element.22), channel_id=1, source_target_pairs={{128,0},{385,1},{130,2},{387,3},{132,4},{389,5},{134,6},{391,7},{1... | collective-permute-start | bytes 331784 | tf_op jit(solution)/shard_map/ppermute | solution.py:50
  18.4 12.8 %collective-permute-start.3 = (bf16[48,1152]{1,0:T(8,128)(2,1)S(1)}, bf16[48,1152]{1,0:T(8,128)(2,1)S(1)}, u32[]{:S(2)}, u32[]{:S(2)}) collective-permute-start(bf16[48,1152]{1,0:T(8,128)(2,1)S(1)} %get-tuple-element.22), channel_id=1, source_target_pairs={{136,0},{401,1},{138,2},{403,3},{140,4},{405,5},{142,6},{407,7},{1... | collective-permute-start | bytes 331784 | tf_op jit(solution)/shard_map/ppermute | solution.py:50
  20.4 10.9 %collective-permute-start.2 = (bf16[48,1152]{1,0:T(8,128)(2,1)S(1)}, bf16[48,1152]{1,0:T(8,128)(2,1)S(1)}, u32[]{:S(2)}, u32[]{:S(2)}) collective-permute-start(bf16[48,1152]{1,0:T(8,128)(2,1)S(1)} %get-tuple-element.22), channel_id=1, source_target_pairs={{8,0},{17,1},{10,2},{19,3},{12,4},{21,5},{14,6},{23,7},{40,32},{49... | collective-permute-start | bytes 331784 | tf_op jit(solution)/shard_map/ppermute | solution.py:50
  31.3 9.3 %collective-permute-start.4 = (bf16[192,1152]{1,0:T(8,128)(2,1)S(1)}, bf16[192,1152]{1,0:T(8,128)(2,1)S(1)}, u32[]{:S(2)}, u32[]{:S(2)}) collective-permute-start(bf16[192,1152]{1,0:T(8,128)(2,1)S(1)} %get-tuple-element.14), channel_id=1, source_target_pairs={{2,0},{33,1},{0,2},{35,3},{6,4},{37,5},{4,6},{39,7},{34,32},{1,33}... | collective-permute-start | bytes 1327112 | tf_op jit(solution)/shard_map/ppermute | solution.py:50
  33.2 15.3 %collective-permute-start.5 = (bf16[192,1152]{1,0:T(8,128)(2,1)S(1)}, bf16[192,1152]{1,0:T(8,128)(2,1)S(1)}, u32[]{:S(2)}, u32[]{:S(2)}) collective-permute-start(bf16[192,1152]{1,0:T(8,128)(2,1)S(1)} %get-tuple-element.14), channel_id=1, source_target_pairs={{6,0},{97,1},{4,2},{99,3},{2,4},{101,5},{0,6},{103,7},{38,32},{65,... | collective-permute-start | bytes 1327112 | tf_op jit(solution)/shard_map/ppermute | solution.py:50
  36.6 12.0 %collective-permute-start.6 = (bf16[192,1152]{1,0:T(8,128)(2,1)S(1)}, bf16[192,1152]{1,0:T(8,128)(2,1)S(1)}, u32[]{:S(2)}, u32[]{:S(2)}) collective-permute-start(bf16[192,1152]{1,0:T(8,128)(2,1)S(1)} %get-tuple-element.14), channel_id=1, source_target_pairs={{4,0},{65,1},{6,2},{67,3},{0,4},{69,5},{2,6},{71,7},{36,32},{97,33... | collective-permute-start | bytes 1327112 | tf_op jit(solution)/shard_map/ppermute | solution.py:50
  40.7 13.8 %collective-permute-start.7 = (bf16[384,1152]{1,0:T(8,128)(2,1)S(1)}, bf16[384,1152]{1,0:T(8,128)(2,1)S(1)}, u32[]{:S(2)}, u32[]{:S(2)}) collective-permute-start(bf16[384,1152]{1,0:T(8,128)(2,1)S(1)} %constant_dynamic-update-slice_fusion.7.me_ref), channel_id=1, source_target_pairs={{0,1},{1,0},{2,3},{3,2},{4,5},{5,4},{6,7},{7,6},{8,9},{9,8},{10,11... | collective-permute-start | bytes 2654216 | tf_op jit(solution)/shard_map/ppermute | solution.py:54
  48.6 6.4 %collective-permute-start.8 = (bf16[384,1152]{1,0:T(8,128)(2,1)S(1)}, bf16[384,1152]{1,0:T(8,128)(2,1)S(1)}, u32[]{:S(2)}, u32[]{:S(2)}) collective-permute-start(bf16[384,1152]{1,0:T(8,128)(2,1)S(1)} %constant_dynamic-update-slice_fusion.13.ml_ref), channel_id=1, source_target_pairs={{0,1},{1,0},{2,3},{3,2},{4,5},{5,4},{6,7},{7,6},{8,9},{9,8},{10,11... | collective-permute-start | bytes 2654216 | tf_op jit(solution)/shard_map/ppermute | solution.py:54
  59.1 9.4 %collective-permute-start.9 = (bf16[192,1152]{1,0:T(8,128)(2,1)S(1)}, bf16[192,1152]{1,0:T(8,128)(2,1)S(1)}, u32[]{:S(2)}, u32[]{:S(2)}) collective-permute-start(bf16[192,1152]{1,0:T(8,128)(2,1)S(1)} %get-tuple-element.11), channel_id=1, source_target_pairs={{0,2},{1,33},{2,0},{3,35},{4,6},{5,37},{6,4},{7,39},{32,34},{33,1}... | collective-permute-start | bytes 1327112 | tf_op jit(solution)/shard_map/ppermute | solution.py:50
  62.3 15.2 %collective-permute-start.10 = (bf16[192,1152]{1,0:T(8,128)(2,1)S(1)}, bf16[192,1152]{1,0:T(8,128)(2,1)S(1)}, u32[]{:S(2)}, u32[]{:S(2)}) collective-permute-start(bf16[192,1152]{1,0:T(8,128)(2,1)S(1)} %get-tuple-element.12), channel_id=1, source_target_pairs={{0,6},{1,97},{2,4},{3,99},{4,2},{5,101},{6,0},{7,103},{32,38},{33,... | collective-permute-start | bytes 1327112 | tf_op jit(solution)/shard_map/ppermute | solution.py:50
  66.0 11.5 %collective-permute-start.11 = (bf16[192,1152]{1,0:T(8,128)(2,1)S(1)}, bf16[192,1152]{1,0:T(8,128)(2,1)S(1)}, u32[]{:S(2)}, u32[]{:S(2)}) collective-permute-start(bf16[192,1152]{1,0:T(8,128)(2,1)S(1)} %get-tuple-element.13), channel_id=1, source_target_pairs={{0,4},{1,65},{2,6},{3,67},{4,0},{5,69},{6,2},{7,71},{32,36},{33,97... | collective-permute-start | bytes 1327112 | tf_op jit(solution)/shard_map/ppermute | solution.py:50
  77.6 9.6 %collective-permute-start.12 = (bf16[96,1152]{1,0:T(8,128)(2,1)S(1)}, bf16[96,1152]{1,0:T(8,128)(2,1)S(1)}, u32[]{:S(2)}, u32[]{:S(2)}) collective-permute-start(bf16[96,1152]{1,0:T(8,128)(2,1)S(1)} %add_convert_fusion), channel_id=1, source_target_pairs={{0,8},{1,17},{2,10},{3,19},{4,12},{5,21},{6,14},{7,23},{32,40},{33... | collective-permute-start | bytes 663560 | tf_op jit(solution)/shard_map/ppermute | solution.py:50
  87.2 9.5 %collective-permute-start.13 = (bf16[48,1152]{1,0:T(8,128)(2,1)S(1)}, bf16[48,1152]{1,0:T(8,128)(2,1)S(1)}, u32[]{:S(2)}, u32[]{:S(2)}) collective-permute-start(bf16[48,1152]{1,0:T(8,128)(2,1)S(1)} %add_convert_fusion.1), channel_id=1, source_target_pairs={{0,128},{1,385},{2,130},{3,387},{4,132},{5,389},{6,134},{7,391},{3... | collective-permute-start | bytes 331784 | tf_op jit(solution)/shard_map/ppermute | solution.py:50
  96.8 6.7 %collective-permute-start.14 = (bf16[24,1152]{1,0:T(8,128)(2,1)S(1)}, bf16[24,1152]{1,0:T(8,128)(2,1)S(1)}, u32[]{:S(2)}, u32[]{:S(2)}) collective-permute-start(bf16[24,1152]{1,0:T(8,128)(2,1)S(1)} %add_convert_fusion.2), channel_id=1, source_target_pairs={{0,1},{1,0},{2,3},{3,2},{4,5},{5,4},{6,7},{7,6},{8,9},{9,8},{10,11... | collective-permute-start | bytes 165896 | tf_op jit(solution)/shard_map/ppermute | solution.py:54
  102.7 0.8 copy-start
  102.7 0.8 copy-start.1
